TPU v7x, 256 devices: a whole 4x4x8 slice. The times are simulated.
256 devices in a mesh: rep: 16 (over z_hi, x), table: 16 (over z_lo, y, core).
Axes of the slice: x: 4, y: 4, z: 8 (z_hi: 4, z_lo: 2; z = z_hi * 2 + z_lo), core: 2. Of those that a mesh axis runs over, the one named last changes fastest.
Arguments:
- dense_out: bfloat16 [32768, 128], P(('rep', 'table')), may hold values from -6 to 6
- pooled: bfloat16 [32768, 2048], P(('rep', 'table')), may hold values from -6 to 6
- cotangent: bfloat16 [32768, 2176], P(('rep', 'table')), may hold values from -24 to 24
- proj_v: bfloat16 [2176, 384], replicated, may hold values from -0.125 to 0.125
- proj_u: bfloat16 [384, 2176], replicated, may hold values from -0.3125 to 0.3125
- bias: float32 [2176], replicated, may hold values from -3 to 3
- lookup_slot: int32 [32768, 16, 2], P('rep', 'table'), may hold values from 0 to 2047, as said below
- uniq_rows: int32 [16, 16, 2048], P('rep', 'table'), may hold values from 0 to 8191, as said below
Outputs:
- grad_u: float32 [384, 2176], P('rep', 'table')
- grad_v: float32 [2176, 384], P('table', 'rep')
- grad_bias: float32 [2176], replicated
- row_grad: float32 [16, 8192, 128], P('table', 'rep')
Inputs may be any that keep to these rules, and one draw needn't show every extreme that they name: `lookup_slot`: within one replica group and table, every place 0 to 2047 of the distinct-row list is named by at least one lookup. `uniq_rows`: the 2048 rows listed for one replica group and table are distinct; at most 160 of them lie in one block of rows r * 512 to (r + 1) * 512 - 1, and some block holds exactly 160.
All inputs are finite; a program needn't handle non-finite values.
Results may differ from a plain program's by a relative error of at most 0.007.
Values may be sent and summed in bfloat16 or wider, within the bound.
No kernel may reach another device: no remote copies, remote signals or barrier semaphores. Data moves between devices by JAX's collectives and lax.ppermute only.
A program may use at most 64 MiB of HBM per device.

v0:
```python
import jax
import jax.numpy as jnp
from jax import lax
from jax.sharding import PartitionSpec as P

ROWS_DEV = 512


def contract_lead(left, right):
    return lax.dot_general(
        left, right, (((0,), (0,)), ((), ())), preferred_element_type=jnp.float32
    )


def contract_tail(left, right):
    return lax.dot_general(
        left, right, (((1,), (1,)), ((), ())), preferred_element_type=jnp.float32
    )


def shards(dense_out, pooled, cotangent, proj_v, proj_u, bias, lookup_slot, uniq_rows):
    emb_width = dense_out.shape[1]
    latent_width = proj_v.shape[1]
    batch_rows = dense_out.shape[0]
    n_rep = lax.axis_size("rep")
    n_table = lax.axis_size("table")
    grad_scale = float(batch_rows * n_rep * n_table) ** (-0.5)
    features = jnp.concatenate([dense_out, pooled], axis=1)
    latent = jnp.dot(features, proj_v, preferred_element_type=jnp.float32).astype(jnp.bfloat16)
    mixing = jnp.dot(latent, proj_u, preferred_element_type=jnp.float32) + bias
    grad_mix = (cotangent.astype(jnp.float32) * features.astype(jnp.float32)).astype(jnp.bfloat16)
    grad_latent = contract_tail(grad_mix, proj_u).astype(jnp.bfloat16)
    backward = contract_tail(grad_latent, proj_v[emb_width:])
    pooled_grad = (
        cotangent[:, emb_width:].astype(jnp.float32) * (mixing[:, emb_width:] + 1.0) + backward
    ).astype(jnp.bfloat16)
    outgoing = pooled_grad.reshape(batch_rows, n_table, emb_width)
    received = lax.all_to_all(outgoing, "table", split_axis=1, concat_axis=0, tiled=True)
    local_u = contract_lead(latent, grad_mix)
    local_v = contract_lead(features, grad_latent)
    local_bias = jnp.sum(grad_mix.astype(jnp.float32), axis=0)
    whole_u, whole_v, whole_bias = lax.psum((local_u, local_v, local_bias), ("rep", "table"))
    rep_part = latent_width // n_rep
    feat_part = features.shape[1] // n_table
    rep_start = lax.axis_index("rep") * rep_part
    feat_start = lax.axis_index("table") * feat_part
    part_u = lax.dynamic_slice(whole_u, (rep_start, feat_start), (rep_part, feat_part))
    part_v = lax.dynamic_slice(whole_v, (feat_start, rep_start), (feat_part, rep_part))
    recv_rows = batch_rows * n_table
    received = received.reshape(recv_rows, emb_width)
    pool_size = lookup_slot.shape[2]
    slot_ids = lookup_slot.reshape(recv_rows, pool_size)
    uniq_count = uniq_rows.shape[2]
    block_rows = min(1024, recv_rows)
    block_count = recv_rows // block_rows

    def add_block(running, block_pair):
        slot_block, grad_block = block_pair
        slot_iota = lax.broadcasted_iota(jnp.int32, (uniq_count, block_rows), 0)
        counts = jnp.zeros((uniq_count, block_rows), jnp.bfloat16)
        for column in range(pool_size):
            counts = counts + (slot_iota == slot_block[:, column][None, :]).astype(jnp.bfloat16)
        return (running + jnp.dot(counts, grad_block, preferred_element_type=jnp.float32), None)

    zero_grad = jnp.zeros((uniq_count, emb_width), jnp.float32)
    uniq_grad, _ = lax.scan(
        add_block,
        zero_grad,
        (
            slot_ids.reshape(block_count, block_rows, pool_size),
            received.reshape(block_count, block_rows, emb_width),
        ),
    )
    keeper_rows = ROWS_DEV
    flat_rows = uniq_rows.reshape(uniq_count)
    table_rows = keeper_rows * n_rep
    dense_rows = jnp.zeros((table_rows, emb_width), jnp.float32).at[flat_rows].set(uniq_grad)
    row_part = lax.psum_scatter(dense_rows, "rep", scatter_dimension=0, tiled=True)
    return (
        part_u * grad_scale,
        part_v * grad_scale,
        whole_bias * grad_scale,
        row_part.reshape(1, keeper_rows, emb_width),
    )


def solution(mesh):
    placed = (
        P(("rep", "table"), None),
        P(("rep", "table"), None),
        P(("rep", "table"), None),
        P(),
        P(),
        P(),
        P("rep", "table", None),
        P("rep", "table", None),
    )
    return jax.shard_map(
        shards,
        mesh=mesh,
        in_specs=placed,
        out_specs=(P("rep", "table"), P("table", "rep"), P(), P("table", "rep", None)),
        check_vma=False,
    )
```

profile of v0, /device:TPU:40, one launch (start us, length us, event | category | flops | bytes accessed | tf_op | source)
XLA Modules:
  0.0 312.8 jit_solution(967055902979283901)
XLA Ops:
  8.0 0.0 copy-start
  8.0 0.0 all-reduce.3.cloned.1.call-start
  8.1 0.9 constant_dynamic-update-slice_fusion.1
  8.9 1.1 constant_dynamic-update-slice_fusion
  10.1 1.9 convolution_convert_fusion.1
  12.0 0.0 copy-done
  12.0 0.0 copy-done.1
  12.0 0.6 convolution_convert_fusion
  12.6 2.3 fusion.25
  15.0 2.4 fusion.23
  17.4 0.0 all-reduce.3.cloned.1.call-update
  17.4 0.7 copy-done.5
  18.1 0.5 fusion.26
  18.6 0.9 copy-done.2
  19.6 0.7 fusion.18
  20.2 0.0 copy-start.4
  20.2 0.0 copy-start.3
  20.2 0.9 copy.17
  21.2 5.8 %all-to-all-start = ((bf16[128,16,128]{2,0,1:T(8,128)(2,1)}), bf16[128,16,128]{2,0,1:T(8,128)(2,1)S(1)}, u32[]{:S(2)}, u32[]{:S(2)}) async-start(bf16[128,16,128]{2,0,1:T(8,128)(2,1)} %bitcast.30), calls=%async_computation | async-start | bytes 1048576 | tf_op jit(solution)/shard_map/all_to_all | solution.py:38
  27.0 0.0 reduce-scatter.2.cloned.1.call-start
  27.1 8.0 %all-to-all-done = bf16[128,16,128]{2,0,1:T(8,128)(2,1)S(1)} async-done(((bf16[128,16,128]{2,0,1:T(8,128)(2,1)}), bf16[128,16,128]{2,0,1:T(8,128)(2,1)S(1)}, u32[]{:S(2)}, u32[]{:S(2)}) %all-to-all-start) | async-done | bytes 524320 | tf_op jit(solution)/shard_map/all_to_all | solution.py:38
  35.1 7.5 %while.11 = (s32[]{:T(128)}, f32[2048,128]{1,0:T(8,128)}, s32[2,1024,2]{1,2,0:T(2,128)S(1)}, bf16[2,1024,128]{2,1,0:T(8,128)(2,1)S(1)}, s32[]{:T(128)}, /*index=5*/s32[]{:T(128)}) while((s32[]{:T(128)}, f32[2048,128]{1,0:T(8,128)}, s32[2,1024,2]{1,2,0:T(2,128)S(1)}, bf16[2,1024,128]{2,1,0:T(8,128)(2,1)S(1)}, s32[]{:T(128)}, ...), condition=%wide.region_5.6_spmd.clone, body=%wide.region_4.5_spmd.clone.sunk | while | flops 554172416 | bytes 2400351 | solution.py:66
  35.1 3.1 fusion.43
  38.3 4.4 %fusion.43 = f32[2048,128]{1,0:T(8,128)} fusion(s32[1024]{0:T(1024)S(1)} %bitcast.43, s32[1024]{0:T(1024)S(1)} %bitcast.42, f32[2048,128]{1,0:T(8,128)} %get-tuple-element.90, pred[]{:T(512)S(6)} %compare.3, bf16[2,1024,128]{2,1,0:T(8,128)(2,1)S(1)} %get-tuple-element.98, s32[]{:T(128)S(6)} %copy.23), kind=kOutput, calls=%fused_computation.9.clone.1 | convolution fusion | flops 554172416 | bytes 2367493 | tf_op jit(solution)/shard_map/while/body/eval_jaxpr/dot_general | solution.py:63
  42.6 8.1 %scatter_custom_fusion = f32[8192,128]{1,0:T(8,128)} fusion(s32[2048]{0:T(1024)S(1)} %bitcast.44, f32[2048,128]{1,0:T(8,128)} %get-tuple-element.26, f32[]{:T(128)} %constant.10.clone.1), kind=kCustom, calls=%fused_computation.16 | custom fusion | bytes 4194816 | tf_op jit(solution)/shard_map/scatter | solution.py:77
  50.8 0.0 reduce-scatter.2.cloned.1.call-update
  50.8 0.2 convert_reduce_fusion
  51.0 82.2 %psum.23 = f32[2176]{0:T(1024)S(1)} all-reduce(f32[2176]{0:T(1024)S(1)} %convert_reduce_fusion), channel_id=1, replica_groups=mesh['rep'=16,'table'=16] {'rep','table'}, use_global_device_ids=true, to_apply=%region_3.0 | all-reduce | flops 2176 | bytes 17408 | tf_op jit(solution)/shard_map/psum | solution.py:42
  133.2 0.6 broadcast_multiply_fusion
  133.8 168.7 %all-reduce.3.cloned.1.call-done = (f32[384,2176]{1,0:T(8,128)}, f32[2176,384]{0,1:T(8,128)}) async-done(((f32[384,2176]{1,0:T(8,128)}, f32[2176,384]{0,1:T(8,128)}), (f32[384,2176]{1,0:T(8,128)}, f32[2176,384]{0,1:T(8,128)})) %all-reduce.3.cloned.1.call-update) | async-done | bytes 6684688 | tf_op jit(solution)/shard_map/psum | solution.py:42
  302.4 1.5 dynamic-slice_multiply_fusion.1
  303.9 1.5 dynamic-slice_multiply_fusion
  (13 shorter events, 0.1 us)
Async XLA Ops:
  8.0 4.0 %copy-start = (bf16[384,2176]{1,0:T(8,128)(2,1)S(1)}, bf16[384,2176]{1,0:T(8,128)(2,1)}, u32[]{:S(2)}) copy-start(bf16[384,2176]{1,0:T(8,128)(2,1)} %param.14) | copy-start | bytes 5013508
  8.0 294.4 %all-reduce.3.cloned.1.call-start = ((), (), s32[]{:S(2)}) async-start(), calls=%async_computation.3 | async-start | bytes 13369344 | tf_op jit(solution)/shard_map/psum | solution.py:42
  8.9 3.1 copy-start.1
  17.4 0.7 copy-start.5
  18.1 1.4 copy-start.2
  20.2 6.9 %copy-start.4 = (s32[1,1,2048]{2,1,0:T(1,128)S(1)}, s32[1,1,2048]{2,1,0:T(1,128)}, u32[]{:S(2)}) copy-start(s32[1,1,2048]{2,1,0:T(1,128)} %param.17) | copy-start | bytes 24580
  20.2 14.9 %copy-start.3 = (s32[2048,1,2]{0,2,1:T(2,128)S(1)}, s32[2048,1,2]{0,2,1:T(2,128)}, u32[]{:S(2)}) copy-start(s32[2048,1,2]{0,2,1:T(2,128)} %param.16) | copy-start | bytes 49156
  21.2 14.0 %all-to-all-start = ((bf16[128,16,128]{2,0,1:T(8,128)(2,1)}), bf16[128,16,128]{2,0,1:T(8,128)(2,1)S(1)}, u32[]{:S(2)}, u32[]{:S(2)}) async-start(bf16[128,16,128]{2,0,1:T(8,128)(2,1)} %bitcast.30), calls=%async_computation | async-start | bytes 1048576 | tf_op jit(solution)/shard_map/all_to_all | solution.py:38
  27.0 278.3 %reduce-scatter.2.cloned.1.call-start = ((), (), s32[]{:S(2)}) async-start(), calls=%async_computation.2 | async-start | bytes 4456448 | tf_op jit(solution)/shard_map/reduce_scatter | solution.py:78
Sparse Core Ops, SparseCore 0:
  17.6 284.8 all-reduce.2
Sparse Core Ops, SparseCore 1:
  50.9 100.1 reduce-scatter.1
where the time goes:
time: 316 us; the launch traced here: 313 us
  waiting for transfers between devices  177 us (56%)
  blocking collectives  82.2 us (26%)
  matrix products  15.9 us (5%)
  between operations  15.6 us (5%)
  local copies, waits for them, and re-layouts  12.8 us (4%)
  starting transfers between devices  5.91 us (2%)
  other arithmetic  3.68 us (1%)
    psum x1, waiting for transfers between devices, shards(): lax.psum((local_u, local_v, local_bias), ('rep', 'table'))  169 us
    psum x1, blocking collectives, shards(): lax.psum((local_u, local_v, local_bias), ('rep', 'table'))  82.2 us
    scatter x1, local copies, waits for them, and re-layouts, shards(): jnp.zeros((table_rows, emb_width), jnp.float32).at[flat_rows].set(uniq_grad)  8.12 us
    all_to_all x1, waiting for transfers between devices, shards(): lax.all_to_all(outgoing, 'table', split_axis=1, concat_axis=0, tiled=True)  8.03 us
    dot_general x2, matrix products, add_block(): jnp.dot(counts, grad_block, preferred_element_type=jnp.float32)  7.49 us
  transfers between devices with their start and end apart: 3, of which 2 were waited for; matrix products, arithmetic and copies ran while one was open for 7% of the time, Pallas kernels for 0%

commit v1 on v0

v1 whole, which is shorter than its diff:
```python
import jax
import jax.numpy as jnp
import numpy as np
from jax import lax
from jax.experimental import pallas as pl
from jax.experimental.pallas import tpu as pltpu
from jax.sharding import Mesh, PartitionSpec as P

BF = jnp.bfloat16
F32 = jnp.float32
TABLE = ("zl", "y", "c")
REP = ("zh", "x")
EMB = 128
LAT = 384
N_TAB = 16
N_REP = 16
D0 = 2176
FEAT = 136
LATP = 24
KEEP = 512
CAP = 160
SLOTS = N_REP * CAP
PAYLOAD = CAP + 16
UNIQ = 2048
SAMP = 2048
SCALE = float(32768) ** -0.5

VMEM = pl.BlockSpec(memory_space=pltpu.VMEM)
SMEM = pl.BlockSpec(memory_space=pltpu.SMEM)
PARAMS = pltpu.CompilerParams(vmem_limit_bytes=56 * 1024 * 1024)


def nn(a, b):
    return lax.dot_general(a, b, (((1,), (0,)), ((), ())), preferred_element_type=F32)


def nt(a, b):
    return lax.dot_general(a, b, (((1,), (1,)), ((), ())), preferred_element_type=F32)


def tn(a, b):
    return lax.dot_general(a, b, (((0,), (0,)), ((), ())), preferred_element_type=F32)


def times(a, b):
    return (a.astype(F32) * b.astype(F32)).astype(BF)


def down(dense, pooled, cot, v_ref, u_ref):
    mix_dense = times(cot[:, :EMB], dense)
    mix_pooled = times(cot[:, EMB:], pooled)
    latent = (nn(dense, v_ref[:EMB, :]) + nn(pooled, v_ref[EMB:, :])).astype(BF)
    grad_latent = (nt(mix_dense, u_ref[:, :EMB]) + nt(mix_pooled, u_ref[:, EMB:])).astype(BF)
    return latent, grad_latent, mix_dense, mix_pooled


def front_kernel(dense_ref, pooled_ref, cot_ref, v_ref, u_ref, bias_ref, out_ref, lat_ref, gl_ref):
    latent, grad_latent, _, _ = down(dense_ref[...], pooled_ref[...], cot_ref[...], v_ref, u_ref)
    lat_ref[...] = latent
    gl_ref[...] = grad_latent
    for t in range(N_TAB):
        cols = slice(EMB + t * EMB, EMB + (t + 1) * EMB)
        mixing = nn(latent, u_ref[:, cols]) + bias_ref[:, cols]
        backward = nt(grad_latent, v_ref[cols, :])
        out_ref[t] = (cot_ref[:, cols].astype(F32) * (mixing + 1.0) + backward).astype(BF)


def weight_kernel(
    place_ref, dense_ref, pooled_ref, cot_ref, lat_ref, gl_ref, dense2_ref, pooled2_ref, cot2_ref,
    v_ref, u_ref, out0, out1, out2, out3, gu, gv, bias_row,
):
    lat2, gl2, md2, mp2 = down(dense2_ref[...], pooled2_ref[...], cot2_ref[...], v_ref, u_ref)
    lat = jnp.concatenate([lat_ref[...], lat2], axis=0)
    gl = jnp.concatenate([gl_ref[...], gl2], axis=0)
    for j in range(D0 // EMB):
        cols = slice(j * EMB, (j + 1) * EMB)
        prev = slice((j - 1) * EMB, j * EMB)
        feat1 = dense_ref[...] if j == 0 else pooled_ref[:, prev]
        feat2 = dense2_ref[...] if j == 0 else pooled2_ref[:, prev]
        mix1 = times(cot_ref[:, cols], feat1)
        mix2 = md2 if j == 0 else mp2[:, prev]
        mix = jnp.concatenate([mix1, mix2], axis=0)
        feat = jnp.concatenate([feat1, feat2], axis=0)
        gu[cols, :] = tn(mix, lat)
        gv[cols, :] = tn(feat, gl)
        bias_row[:, cols] = jnp.sum(mix.astype(F32), axis=0, keepdims=True)
    high = bias_row[...].astype(BF)
    low = (bias_row[...] - high.astype(F32)).astype(BF)
    tail = jnp.zeros((1, 6 * LAT - D0), BF)
    rows = []
    for part in (high, low):
        whole = jnp.concatenate([part, tail], axis=1)
        rows += [whole[:, k * LAT : (k + 1) * LAT].astype(F32) for k in range(6)]
    rows.append(jnp.zeros((4, LAT), F32))
    bias_block = jnp.concatenate(rows, axis=0).astype(BF)
    y, c = place_ref[0], place_ref[1]
    for s, out in enumerate((out0, out1, out2, out3)):
        dest_y = lax.rem(y + s, 4)
        for part, g in enumerate((gu, gv)):
            blocks = []
            for zl in range(2):
                start = pl.multiple_of((zl * 8 + dest_y * 2 + c) * FEAT, 8)
                blocks.append(g[pl.ds(start, FEAT), :])
            out[part * 272 : (part + 1) * 272, :] = jnp.concatenate(blocks, axis=0).astype(BF)
        out[544:560, :] = bias_block


def bias_again(block):
    total = block[0:6, :] + block[6:12, :]
    high = total.astype(BF).astype(F32)
    low = (total - high).astype(BF).astype(F32)
    return jnp.concatenate([high, low, jnp.zeros((4, LAT), F32)], axis=0)


def after_y_kernel(place_ref, m0, m1, m2, m3, keep_ref, send_ref, acc):
    acc[...] = (m0[...].astype(F32) + m1[...].astype(F32)) + (m2[...].astype(F32) + m3[...].astype(F32))
    zl = place_ref[2]
    bias = bias_again(acc[544:560, :])
    for out, half in ((keep_ref, zl), (send_ref, 1 - zl)):
        blocks = [
            acc[pl.ds(pl.multiple_of(part * 272 + half * FEAT, 8), FEAT), :] for part in range(2)
        ]
        out[0:272, :] = jnp.concatenate(blocks, axis=0).astype(out.dtype)
        out[272:288, :] = bias.astype(out.dtype)


def after_zl_kernel(place_ref, keep_ref, got_ref, out0, out1, out2, out3, flip):
    total = keep_ref[...] + got_ref[...].astype(F32)
    bias = bias_again(total[272:288, :]).astype(BF)
    stacked = jnp.concatenate(
        [total[0:128], total[136:264], total[128:136], total[264:272], jnp.zeros((112, LAT), F32)],
        axis=0,
    )
    flip[...] = stacked.T
    x = place_ref[3]
    for s, out in enumerate((out0, out1, out2, out3)):
        dest_x = lax.rem(x + s, 4)
        blocks = [
            flip[pl.ds(pl.multiple_of((zh * 4 + dest_x) * LATP, 8), LATP), :] for zh in range(4)
        ]
        out[0:96, :] = jnp.concatenate(blocks, axis=0).astype(BF)
        out[96:112, :] = bias


def after_x_kernel(place_ref, m0, m1, m2, m3, out0, out1, out2, out3, acc):
    acc[...] = (m0[...].astype(F32) + m1[...].astype(F32)) + (m2[...].astype(F32) + m3[...].astype(F32))
    bias = bias_again(acc[96:112, :]).astype(BF)
    zh = place_ref[4]
    for s, out in enumerate((out0, out1, out2, out3)):
        dest = lax.rem(zh + s, 4)
        block = acc[pl.ds(pl.multiple_of(dest * LATP, 8), LATP), :]
        out[0:32, :] = jnp.concatenate([block, jnp.zeros((8, LAT), F32)], axis=0).astype(BF)
        out[32:48, :] = bias


def last_kernel(m0, m1, m2, m3, u_ref, v_ref, bias_ref):
    total = (m0[...].astype(F32) + m1[...].astype(F32)) + (m2[...].astype(F32) + m3[...].astype(F32))
    total = total * SCALE
    u_ref[:, 0:128] = total[0:LATP, 0:128]
    u_ref[:, 128:136] = total[0:LATP, 256:264]
    v_ref[:, 0:128] = total[0:LATP, 128:256]
    v_ref[:, 128:136] = total[0:LATP, 264:272]
    bias = total[32:38, :] + total[38:44, :]
    for k in range(6):
        width = min(LAT, D0 - k * LAT)
        bias_ref[:, k * LAT : k * LAT + width] = bias[k : k + 1, 0:width]


def index_kernel(uniq_ref, slot_ref, hot_ref, pos_ref):
    uniq = uniq_ref[...]
    keeper = lax.shift_right_logical(uniq, 9)
    row = jnp.bitwise_and(uniq, KEEP - 1)
    upper = (
        lax.broadcasted_iota(jnp.int32, (128, 128), 0) <= lax.broadcasted_iota(jnp.int32, (128, 128), 1)
    ).astype(F32).astype(BF)
    which = lax.broadcasted_iota(jnp.int32, (N_REP, 128), 0)
    carry = jnp.zeros((N_REP, 1), F32)
    parts = []
    for b in range(UNIQ // 128):
        member = (which == keeper[:, b * 128 : (b + 1) * 128]).astype(F32)
        running = nn(member.astype(BF), upper) + carry
        carry = running[:, 127:128]
        place = member * (running - 1.0 + which.astype(F32) * float(CAP))
        parts.append(jnp.sum(place, axis=0, keepdims=True))
    dest = jnp.concatenate(parts, axis=1).astype(jnp.int32)
    zeros6 = jnp.zeros((6, UNIQ), F32)

    def digits(values, shift):
        low = jnp.bitwise_and(values, (1 << shift) - 1).astype(F32)
        high = lax.shift_right_logical(values, shift).astype(F32)
        return jnp.concatenate([high, low, zeros6], axis=0).astype(BF)

    dest_digits = digits(dest, 4)
    row_digits = digits(row, 4)
    found = []
    for p in range(2):
        acc = jnp.zeros((8, SAMP), F32)
        for b in range(UNIQ // 256):
            names = lax.broadcasted_iota(jnp.int32, (256, SAMP), 0) + b * 256
            hot = (names == slot_ref[p : p + 1, :]).astype(F32).astype(BF)
            acc = acc + nn(dest_digits[:, b * 256 : (b + 1) * 256], hot)
        found.append((acc[0:1, :] * 16.0 + acc[1:2, :]).astype(jnp.int32))
    for k in range(N_REP):
        places = lax.broadcasted_iota(jnp.int32, (CAP, SAMP), 0) + k * CAP
        first = (places == found[0]).astype(F32)
        hot_ref[k * CAP : (k + 1) * CAP, :] = (first + (places == found[1]).astype(F32)).astype(BF)
        listed = (places == dest).astype(F32).astype(BF)
        where = nt(row_digits, listed)
        wide = jnp.concatenate([where, jnp.zeros((8, 256 - CAP), F32)], axis=1)
        block = jnp.concatenate([wide[0:1, 0:128], wide[0:1, 128:256], wide[1:2, 0:128], wide[1:2, 128:256]], axis=0)
        pos_ref[k] = jnp.concatenate([block, jnp.zeros((12, 128), F32)], axis=0).astype(BF)


def rows_kernel(hot_ref, got_ref, pos_ref, out_ref):
    out_ref[0, 0:CAP, :] = nn(hot_ref[...], got_ref[...]).astype(BF)
    out_ref[0, CAP:PAYLOAD, :] = pos_ref[0]


def keep_kernel(got_ref, out_ref):
    names = lax.broadcasted_iota(jnp.int32, (KEEP, CAP), 0).astype(F32)
    acc = jnp.zeros((KEEP, EMB), F32)
    for g in range(N_REP):
        pos = got_ref[g, CAP:PAYLOAD, :].astype(F32)
        at = pos[0:2, :] * 16.0 + pos[2:4, :]
        at = jnp.concatenate([at[0:1, :], at[1:2, 0 : CAP - 128]], axis=1)
        hot = (names == at).astype(F32).astype(BF)
        acc = acc + nn(hot, got_ref[g, 0:CAP, :])
    out_ref[...] = acc


def call(kernel, outs, ins, scratch=(), place=True):
    specs = ([SMEM] if place else []) + [VMEM] * (len(ins) - (1 if place else 0))
    return pl.pallas_call(
        kernel,
        out_shape=tuple(jax.ShapeDtypeStruct(s, d) for s, d in outs),
        in_specs=specs,
        out_specs=tuple(VMEM for _ in outs),
        scratch_shapes=list(scratch),
        compiler_params=PARAMS,
    )(*ins)


def around(messages, axis):
    return [messages[0]] + [
        lax.ppermute(messages[s], axis, [(i, (i + s) % 4) for i in range(4)]) for s in (1, 2, 3)
    ]


def shards(dense, pooled, cot, proj_v, proj_u, bias, lookup_slot, uniq_rows):
    place = jnp.stack([lax.axis_index(a) for a in ("y", "c", "zl", "x", "zh")]).astype(jnp.int32)
    swap = [(0, 1), (1, 0)]
    other = [lax.ppermute(a, "c", swap) for a in (dense, pooled, cot)]
    outgoing, latent, grad_latent = call(
        front_kernel,
        [((N_TAB, 128, EMB), BF), ((128, LAT), BF), ((128, LAT), BF)],
        [dense, pooled, cot, proj_v, proj_u, bias.reshape(1, D0)],
        place=False,
    )
    received = lax.all_to_all(outgoing, TABLE, 0, 0, tiled=True).reshape(SAMP, EMB)
    slots = lookup_slot.reshape(SAMP, 2).T
    hot, pos = call(
        index_kernel,
        [((SLOTS, SAMP), BF), ((N_REP, 16, 128), BF)],
        [uniq_rows.reshape(1, UNIQ), slots],
        place=False,
    )
    message = ((560, LAT), BF)
    along_y = call(
        weight_kernel,
        [message] * 4,
        [place, dense, pooled, cot, latent, grad_latent, *other, proj_v, proj_u],
        [pltpu.VMEM((D0, LAT), F32), pltpu.VMEM((D0, LAT), F32), pltpu.VMEM((1, D0), F32)],
    )
    along_y = around(along_y, "y")
    payload = pl.pallas_call(
        rows_kernel,
        grid=(N_REP,),
        out_shape=jax.ShapeDtypeStruct((N_REP, PAYLOAD, EMB), BF),
        in_specs=[
            pl.BlockSpec((CAP, SAMP), lambda k: (k, 0)),
            pl.BlockSpec((SAMP, EMB), lambda k: (0, 0)),
            pl.BlockSpec((1, 16, 128), lambda k: (k, 0, 0)),
        ],
        out_specs=pl.BlockSpec((1, PAYLOAD, EMB), lambda k: (k, 0, 0)),
        compiler_params=PARAMS,
    )(hot, received, pos)
    gathered = lax.all_to_all(payload, REP, 0, 0, tiled=True)
    kept, sent = call(
        after_y_kernel,
        [((288, LAT), F32), ((288, LAT), BF)],
        [place, *along_y],
        [pltpu.VMEM((560, LAT), F32)],
    )
    got = lax.ppermute(sent, "zl", swap)
    along_x = call(
        after_zl_kernel, [((112, LAT), BF)] * 4, [place, kept, got], [pltpu.VMEM((LAT, LAT), F32)]
    )
    along_x = around(along_x, "x")
    along_z = call(
        after_x_kernel, [((48, LAT), BF)] * 4, [place, *along_x], [pltpu.VMEM((112, LAT), F32)]
    )
    along_z = around(along_z, "zh")
    part_u, part_v, whole_bias = call(
        last_kernel,
        [((LATP, FEAT), F32), ((LATP, FEAT), F32), ((1, D0), F32)],
        along_z,
        place=False,
    )
    (row_part,) = call(keep_kernel, [((KEEP, EMB), F32)], [gathered], place=False)
    return part_u, part_v.T, whole_bias.reshape(D0), row_part.reshape(1, KEEP, EMB)


def solution(mesh):
    fine = Mesh(np.asarray(mesh.devices).reshape(4, 4, 2, 4, 2), ("zh", "x", "zl", "y", "c"))
    every = P(REP + TABLE, None)
    placed = (every, every, every, P(), P(), P(), P(REP, TABLE, None), P(REP, TABLE, None))
    return jax.shard_map(
        shards,
        mesh=fine,
        in_specs=placed,
        out_specs=(P(REP, TABLE), P(TABLE, REP), P(), P(TABLE, REP, None)),
        check_vma=False,
    )
```

time: 316 us -> 132 us (0.42)
  waiting for transfers between devices: 177 us -> 31.8 us
  blocking collectives: 82.2 us -> 0 us
  Pallas kernels: 0 us -> 51.9 us
  starting transfers between devices: 5.91 us -> 37.5 us
  matrix products: 15.9 us -> 0 us
  between operations: 15.6 us -> 0.71 us
  local copies, waits for them, and re-layouts: 12.8 us -> 7.29 us
    psum x1 -> x0, waiting for transfers between devices: 169 us -> none  [shards(): lax.psum((local_u, local_v, local_bias), ('rep', 'table'))]
    psum x1 -> x0, blocking collectives: 82.2 us -> none  [shards(): lax.psum((local_u, local_v, local_bias), ('rep', 'table'))]
    pallas_call x0 -> x9, Pallas kernels: none -> 51.9 us  [the longest x8 38.6 us: call(): pl.pallas_call(kernel, out_shape=tuple((jax.ShapeDtypeStruct(s, d) for s,...]
    ppermute x0 -> x13, waiting for transfers between devices: none -> 31.8 us  [the longest x9 23.9 us: around(): lax.ppermute(messages[s], axis, [(i, (i + s) % 4) for i in range(4)])]
    ppermute x0 -> x13, starting transfers between devices: none -> 21.5 us  [the longest x9 20.3 us: around(): lax.ppermute(messages[s], axis, [(i, (i + s) % 4) for i in range(4)])]
    dot_general x8 -> x0, matrix products: 15.9 us -> none  [the longest x2 7.49 us: add_block(): jnp.dot(counts, grad_block, preferred_element_type=jnp.float32)]
    all_to_all x1 -> x2, starting transfers between devices: 5.84 us -> 16 us  [the longest x1 10.1 us: shards(): gathered = lax.all_to_all(payload, REP, 0, 0, tiled=True)]
    scatter x1 -> x0, local copies, waits for them, and re-layouts: 8.12 us -> none  [shards(): jnp.zeros((table_rows, emb_width), jnp.float32).at[flat_rows].set(uniq_grad)]
  transfers between devices with their start and end apart: 3 -> 15, of which waited for: 2 -> 10; matrix products, arithmetic and copies ran while one was open for 7% -> 1% of each run, Pallas kernels for 0% -> 23%
where the time goes in v1:
time: 132 us; the launch traced here: 130 us
  Pallas kernels  51.9 us (39%)
  starting transfers between devices  37.5 us (28%)
  waiting for transfers between devices  31.8 us (24%)
  local copies, waits for them, and re-layouts  7.29 us (6%)
  other arithmetic  1.32 us (1%)
    pallas_call x8, Pallas kernels, call(): pl.pallas_call(kernel, out_shape=tuple((jax.ShapeDtypeStruct(s, d) for s,...  38.6 us
    ppermute x9, waiting for transfers between devices, around(): lax.ppermute(messages[s], axis, [(i, (i + s) % 4) for i in range(4)])  23.9 us
    ppermute x9, starting transfers between devices, around(): lax.ppermute(messages[s], axis, [(i, (i + s) % 4) for i in range(4)])  20.3 us
    pallas_call x1, Pallas kernels, shards(): pl.pallas_call(rows_kernel, grid=(N_REP,), out_shape=jax.ShapeDtypeStruct...  13.3 us
    all_to_all x1, starting transfers between devices, shards(): gathered = lax.all_to_all(payload, REP, 0, 0, tiled=True)  10.1 us
    ppermute x1, waiting for transfers between devices, shards(): got = lax.ppermute(sent, 'zl', swap)  6.52 us
    all_to_all x1, starting transfers between devices, shards(): lax.all_to_all(outgoing, TABLE, 0, 0, tiled=True).reshape(SAMP, EMB)  5.84 us
    unnamed x36, local copies, waits for them, and re-layouts  5.36 us
  transfers between devices with their start and end apart: 15, of which 10 were waited for; matrix products, arithmetic and copies ran while one was open for 1% of the time, Pallas kernels for 23%

profile of v1, /device:TPU:40, one launch (start us, length us, event | category | flops | bytes accessed | tf_op | source)
XLA Modules:
  0.0 130.4 jit_solution(3327881210001815131)
XLA Ops:
  0.6 1.3 %reshape.26.bias_ref = f32[1,2176]{1,0:T(1,128)} reshape(f32[2176]{0:T(1024)} %param.13) | data formatting | bytes 17408 | tf_op jit(solution)/shard_map/reshape | solution.py:256
  1.9 5.4 %shard_map.111 = (bf16[16,128,128]{2,1,0:T(8,128)(2,1)}, bf16[128,384]{1,0:T(8,128)(2,1)}, bf16[128,384]{1,0:T(8,128)(2,1)}) custom-call(bf16[128,128]{1,0:T(8,128)(2,1)} %dense_ref.3, bf16[128,2048]{1,0:T(8,128)(2,1)} %pooled_ref.3, bf16[128,2176]{1,0:T(8,128)(2,1)} %cot_ref.3, bf16[2176,384]{1,0:T(8,128)(2,1)} %v_ref.3, bf16[384,2176]{1,0:T(8,128)(2,1)} %u_ref.3, ...), custom_call_target="tpu_custom_call" | custom-call | tf_op jit(solution)/shard_map/pallas_call | solution.py:233
  7.3 5.8 %all-to-all-start = ((bf16[16,128,128]{2,1,0:T(8,128)(2,1)}), bf16[16,128,128]{2,1,0:T(8,128)(2,1)S(1)}, u32[]{:S(2)}, u32[]{:S(2)}) async-start(bf16[16,128,128]{2,1,0:T(8,128)(2,1)} %get-tuple-element.46), calls=%async_computation | async-start | bytes 1048576 | tf_op jit(solution)/shard_map/all_to_all | solution.py:259
  13.2 15.8 %shard_map.117 = (bf16[2560,2048]{1,0:T(8,128)(2,1)}, bf16[16,16,128]{2,1,0:T(8,128)(2,1)}) custom-call(s32[1,2048]{1,0:T(1,128)} %bitcast.15, s32[2,2048]{1,0:T(2,128)} %bitcast.14), custom_call_target="tpu_custom_call" | custom-call | tf_op jit(solution)/shard_map/pallas_call | solution.py:233
  29.8 13.3 %shard_map.118 = bf16[16,176,128]{2,1,0:T(8,128)(2,1)} custom-call(bf16[2560,2048]{1,0:T(8,128)(2,1)} %get-tuple-element.45.hot_ref, bf16[2048,128]{1,0:T(8,128)(2,1)} %bitcast.12, bf16[16,16,128]{2,1,0:T(8,128)(2,1)} %get-tuple-element.47.pos_ref), custom_call_target="tpu_custom_call" | custom-call | tf_op jit(solution)/shard_map/pallas_call | solution.py:275
  43.1 10.1 %all-to-all-start.1 = ((bf16[16,176,128]{2,1,0:T(8,128)(2,1)}), bf16[16,176,128]{2,1,0:T(8,128)(2,1)S(1)}, u32[]{:S(2)}, u32[]{:S(2)}) async-start(bf16[16,176,128]{2,1,0:T(8,128)(2,1)} %shard_map.118), calls=%async_computation.1 | async-start | bytes 1441792 | tf_op jit(solution)/shard_map/all_to_all | solution.py:287
  54.7 1.3 %collective-permute-done.dense2_ref = bf16[128,128]{1,0:T(8,128)(2,1)S(1)} collective-permute-done((bf16[128,128]{1,0:T(8,128)(2,1)S(1)}, bf16[128,128]{1,0:T(8,128)(2,1)S(1)}, u32[]{:S(2)}, u32[]{:S(2)}) %collective-permute-start) | collective-permute-done | bytes 32800 | tf_op jit(solution)/shard_map/ppermute | solution.py:252
  57.1 6.4 %shard_map.112 = (bf16[560,384]{1,0:T(8,128)(2,1)}, bf16[560,384]{1,0:T(8,128)(2,1)}, bf16[560,384]{1,0:T(8,128)(2,1)}, bf16[560,384]{1,0:T(8,128)(2,1)}) custom-call(s32[5]{0:T(128)} %stack.23.place_ref, bf16[128,128]{1,0:T(8,128)(2,1)} %dense_ref.3, bf16[128,2048]{1,0:T(8,128)(2,1)} %pooled_ref.3, bf16[128,2176]{1,0:T(8,128)(2,1)} %cot_ref.3, ...), custom_call_target="tpu_custom_call" | custom-call | tf_op jit(solution)/shard_map/pallas_call | solution.py:233
  63.5 1.5 %collective-permute-start.3 = (bf16[560,384]{1,0:T(8,128)(2,1)}, bf16[560,384]{1,0:T(8,128)(2,1)S(1)}, u32[]{:S(2)}, u32[]{:S(2)}) collective-permute-start(bf16[560,384]{1,0:T(8,128)(2,1)} %get-tuple-element.29), channel_id=1, source_target_pairs={{0,2},{2,4},{4,6},{6,0},{1,3},{3,5},{5,7},{7,1},{8,10},{10,12},{12... | collective-permute-start | bytes 1290248 | tf_op jit(solution)/shard_map/ppermute | solution.py:245
  64.9 1.2 collective-permute-start.4
  66.1 2.1 %collective-permute-start.5 = (bf16[560,384]{1,0:T(8,128)(2,1)}, bf16[560,384]{1,0:T(8,128)(2,1)S(1)}, u32[]{:S(2)}, u32[]{:S(2)}) collective-permute-start(bf16[560,384]{1,0:T(8,128)(2,1)} %get-tuple-element.31), channel_id=1, source_target_pairs={{0,6},{2,0},{4,2},{6,4},{1,7},{3,1},{5,3},{7,5},{8,14},{10,8},{12,... | collective-permute-start | bytes 1290248 | tf_op jit(solution)/shard_map/ppermute | solution.py:245
  68.2 8.3 %collective-permute-done.3.m1 = bf16[560,384]{1,0:T(8,128)(2,1)S(1)} collective-permute-done((bf16[560,384]{1,0:T(8,128)(2,1)}, bf16[560,384]{1,0:T(8,128)(2,1)S(1)}, u32[]{:S(2)}, u32[]{:S(2)}) %collective-permute-start.3) | collective-permute-done | bytes 430112 | tf_op jit(solution)/shard_map/ppermute | solution.py:245
  76.4 3.0 %collective-permute-done.4.m2 = bf16[560,384]{1,0:T(8,128)(2,1)S(1)} collective-permute-done((bf16[560,384]{1,0:T(8,128)(2,1)}, bf16[560,384]{1,0:T(8,128)(2,1)S(1)}, u32[]{:S(2)}, u32[]{:S(2)}) %collective-permute-start.4) | collective-permute-done | bytes 430112 | tf_op jit(solution)/shard_map/ppermute | solution.py:245
  79.4 7.5 %collective-permute-done.5.m3 = bf16[560,384]{1,0:T(8,128)(2,1)S(1)} collective-permute-done((bf16[560,384]{1,0:T(8,128)(2,1)}, bf16[560,384]{1,0:T(8,128)(2,1)S(1)}, u32[]{:S(2)}, u32[]{:S(2)}) %collective-permute-start.5) | collective-permute-done | bytes 430112 | tf_op jit(solution)/shard_map/ppermute | solution.py:245
  87.6 2.6 %shard_map.113 = (f32[288,384]{1,0:T(8,128)}, bf16[288,384]{1,0:T(8,128)(2,1)}) custom-call(s32[5]{0:T(128)} %stack.23.place_ref, bf16[560,384]{1,0:T(8,128)(2,1)} %get-tuple-element.28.m0, bf16[560,384]{1,0:T(8,128)(2,1)} %copy-done.6, bf16[560,384]{1,0:T(8,128)(2,1)} %copy-done.7, bf16[560,384]{1,0:T(8,128)(2,1)} %copy-done.8), custom_call_target="tpu_custom_call" | custom-call | tf_op jit(solution)/shard_map/pallas_call | solution.py:233
  90.6 6.5 %collective-permute-done.6.got_ref = bf16[288,384]{1,0:T(8,128)(2,1)S(1)} collective-permute-done((bf16[288,384]{1,0:T(8,128)(2,1)}, bf16[288,384]{1,0:T(8,128)(2,1)S(1)}, u32[]{:S(2)}, u32[]{:S(2)}) %collective-permute-start.6) | collective-permute-done | bytes 221216 | tf_op jit(solution)/shard_map/ppermute | solution.py:294
  97.8 2.1 %shard_map.114 = (bf16[112,384]{1,0:T(8,128)(2,1)}, bf16[112,384]{1,0:T(8,128)(2,1)}, bf16[112,384]{1,0:T(8,128)(2,1)}, bf16[112,384]{1,0:T(8,128)(2,1)}) custom-call(s32[5]{0:T(128)} %stack.23.place_ref, f32[288,384]{1,0:T(8,128)} %get-tuple-element.32.keep_ref, bf16[288,384]{1,0:T(8,128)(2,1)} %copy-done.9), custom_call_target="tpu_custom_call" | custom-call | tf_op jit(solution)/shard_map/pallas_call | solution.py:233
  99.9 1.9 %collective-permute-start.7 = (bf16[112,384]{1,0:T(8,128)(2,1)}, bf16[112,384]{1,0:T(8,128)(2,1)S(1)}, u32[]{:S(2)}, u32[]{:S(2)}) collective-permute-start(bf16[112,384]{1,0:T(8,128)(2,1)} %get-tuple-element.35), channel_id=1, source_target_pairs={{0,16},{16,32},{32,48},{48,0},{1,17},{17,33},{33,49},{49,1},{2,18}... | collective-permute-start | bytes 258056 | tf_op jit(solution)/shard_map/ppermute | solution.py:245
  101.9 2.7 %collective-permute-start.8 = (bf16[112,384]{1,0:T(8,128)(2,1)}, bf16[112,384]{1,0:T(8,128)(2,1)S(1)}, u32[]{:S(2)}, u32[]{:S(2)}) collective-permute-start(bf16[112,384]{1,0:T(8,128)(2,1)} %get-tuple-element.36), channel_id=1, source_target_pairs={{0,32},{16,48},{32,0},{48,16},{1,33},{17,49},{33,1},{49,17},{2,34}... | collective-permute-start | bytes 258056 | tf_op jit(solution)/shard_map/ppermute | solution.py:245
  104.5 1.4 %collective-permute-start.9 = (bf16[112,384]{1,0:T(8,128)(2,1)}, bf16[112,384]{1,0:T(8,128)(2,1)S(1)}, u32[]{:S(2)}, u32[]{:S(2)}) collective-permute-start(bf16[112,384]{1,0:T(8,128)(2,1)} %get-tuple-element.37), channel_id=1, source_target_pairs={{0,48},{16,0},{32,16},{48,32},{1,49},{17,1},{33,17},{49,33},{2,50}... | collective-permute-start | bytes 258056 | tf_op jit(solution)/shard_map/ppermute | solution.py:245
  106.5 1.6 %collective-permute-done.8.m2 = bf16[112,384]{1,0:T(8,128)(2,1)S(1)} collective-permute-done((bf16[112,384]{1,0:T(8,128)(2,1)}, bf16[112,384]{1,0:T(8,128)(2,1)S(1)}, u32[]{:S(2)}, u32[]{:S(2)}) %collective-permute-start.8) | collective-permute-done | bytes 86048 | tf_op jit(solution)/shard_map/ppermute | solution.py:245
  108.1 1.1 collective-permute-done.9.m3
  109.9 1.8 %shard_map.115 = (bf16[48,384]{1,0:T(8,128)(2,1)}, bf16[48,384]{1,0:T(8,128)(2,1)}, bf16[48,384]{1,0:T(8,128)(2,1)}, bf16[48,384]{1,0:T(8,128)(2,1)}) custom-call(s32[5]{0:T(128)} %stack.23.place_ref, bf16[112,384]{1,0:T(8,128)(2,1)} %get-tuple-element.34.m0, bf16[112,384]{1,0:T(8,128)(2,1)} %copy-done.11, bf16[112,384]{1,0:T(8,128)(2,1)} %copy-done.12, ...), custom_call_target="tpu_custom_call" | custom-call | tf_op jit(solution)/shard_map/pallas_call | solution.py:233
  111.6 2.4 %collective-permute-start.10 = (bf16[48,384]{1,0:T(8,128)(2,1)}, bf16[48,384]{1,0:T(8,128)(2,1)S(1)}, u32[]{:S(2)}, u32[]{:S(2)}) collective-permute-start(bf16[48,384]{1,0:T(8,128)(2,1)} %get-tuple-element.39), channel_id=1, source_target_pairs={{0,64},{64,128},{128,192},{192,0},{1,65},{65,129},{129,193},{193,1... | collective-permute-start | bytes 110600 | tf_op jit(solution)/shard_map/ppermute | solution.py:245
  114.0 3.6 %collective-permute-start.11 = (bf16[48,384]{1,0:T(8,128)(2,1)}, bf16[48,384]{1,0:T(8,128)(2,1)S(1)}, u32[]{:S(2)}, u32[]{:S(2)}) collective-permute-start(bf16[48,384]{1,0:T(8,128)(2,1)} %get-tuple-element.40), channel_id=1, source_target_pairs={{0,128},{64,192},{128,0},{192,64},{1,129},{65,193},{129,1},{193,65... | collective-permute-start | bytes 110600 | tf_op jit(solution)/shard_map/ppermute | solution.py:245
  117.6 3.6 %collective-permute-start.12 = (bf16[48,384]{1,0:T(8,128)(2,1)}, bf16[48,384]{1,0:T(8,128)(2,1)S(1)}, u32[]{:S(2)}, u32[]{:S(2)}) collective-permute-start(bf16[48,384]{1,0:T(8,128)(2,1)} %get-tuple-element.41), channel_id=1, source_target_pairs={{0,192},{64,0},{128,64},{192,128},{1,193},{65,1},{129,65},{193,129... | collective-permute-start | bytes 110600 | tf_op jit(solution)/shard_map/ppermute | solution.py:245
  121.1 0.9 collective-permute-done.11.m2
  122.0 1.0 collective-permute-done.12.m3
  123.7 1.5 %shard_map.116 = (f32[24,136]{1,0:T(8,128)}, f32[24,136]{1,0:T(8,128)}, f32[1,2176]{1,0:T(1,128)}) custom-call(bf16[48,384]{1,0:T(8,128)(2,1)} %get-tuple-element.38.m0, bf16[48,384]{1,0:T(8,128)(2,1)} %copy-done.14, bf16[48,384]{1,0:T(8,128)(2,1)} %copy-done.15, bf16[48,384]{1,0:T(8,128)(2,1)} %copy-done.16), custom_call_target="tpu_custom_call" | custom-call | tf_op jit(solution)/shard_map/pallas_call | solution.py:233
  125.2 1.3 %reduce = f32[2176]{0:T(1024)} reduce(f32[1,2176]{1,0:T(1,128)} %get-tuple-element.44, f32[]{:T(128)} %constant.24), dimensions={0}, to_apply=%get-tuple-element.44.reduce_sub_computation | reduce | bytes 17412 | tf_op jit(solution)/shard_map/pallas_call | solution.py:233
  126.5 0.9 copy-done
  127.4 3.0 %shard_map.119 = f32[512,128]{1,0:T(8,128)} custom-call(bf16[16,176,128]{2,1,0:T(8,128)(2,1)} %copy-done), custom_call_target="tpu_custom_call" | custom-call | tf_op jit(solution)/shard_map/pallas_call | solution.py:233
  (46 shorter events, 6.9 us)
Async XLA Ops:
  7.3 21.7 %all-to-all-start = ((bf16[16,128,128]{2,1,0:T(8,128)(2,1)}), bf16[16,128,128]{2,1,0:T(8,128)(2,1)S(1)}, u32[]{:S(2)}, u32[]{:S(2)}) async-start(bf16[16,128,128]{2,1,0:T(8,128)(2,1)} %get-tuple-element.46), calls=%async_computation | async-start | bytes 1048576 | tf_op jit(solution)/shard_map/all_to_all | solution.py:259
  29.0 0.8 copy-start.3
  29.8 23.4 %copy-start.1 = (bf16[128,2176]{1,0:T(8,128)(2,1)S(1)}, bf16[128,2176]{1,0:T(8,128)(2,1)}, u32[]{:S(2)}) copy-start(bf16[128,2176]{1,0:T(8,128)(2,1)} %cot_ref.3) | copy-start | bytes 1671172
  29.8 23.5 %copy-start.2 = (bf16[128,2048]{1,0:T(8,128)(2,1)S(1)}, bf16[128,2048]{1,0:T(8,128)(2,1)}, u32[]{:S(2)}) copy-start(bf16[128,2048]{1,0:T(8,128)(2,1)} %pooled_ref.3) | copy-start | bytes 1572868
  29.8 24.0 %copy-start.10 = (bf16[128,128]{1,0:T(8,128)(2,1)S(1)}, bf16[128,128]{1,0:T(8,128)(2,1)}, u32[]{:S(2)}) copy-start(bf16[128,128]{1,0:T(8,128)(2,1)} %dense_ref.3) | copy-start | bytes 98308
  43.1 83.5 %all-to-all-start.1 = ((bf16[16,176,128]{2,1,0:T(8,128)(2,1)}), bf16[16,176,128]{2,1,0:T(8,128)(2,1)S(1)}, u32[]{:S(2)}, u32[]{:S(2)}) async-start(bf16[16,176,128]{2,1,0:T(8,128)(2,1)} %shard_map.118), calls=%async_computation.1 | async-start | bytes 1441792 | tf_op jit(solution)/shard_map/all_to_all | solution.py:287
  53.2 2.9 %collective-permute-start.2 = (bf16[128,2176]{1,0:T(8,128)(2,1)S(1)}, bf16[128,2176]{1,0:T(8,128)(2,1)S(1)}, u32[]{:S(2)}, u32[]{:S(2)}) collective-permute-start(bf16[128,2176]{1,0:T(8,128)(2,1)S(1)} %copy-done.1), channel_id=1, source_target_pairs={{0,1},{1,0},{2,3},{3,2},{4,5},{5,4},{6,7},{7,6},{8,9},{9,8},{10,11... | collective-permute-start | bytes 1671176 | tf_op jit(solution)/shard_map/ppermute | solution.py:252
  53.3 2.7 %collective-permute-start.1 = (bf16[128,2048]{1,0:T(8,128)(2,1)S(1)}, bf16[128,2048]{1,0:T(8,128)(2,1)S(1)}, u32[]{:S(2)}, u32[]{:S(2)}) collective-permute-start(bf16[128,2048]{1,0:T(8,128)(2,1)S(1)} %copy-done.2), channel_id=1, source_target_pairs={{0,1},{1,0},{2,3},{3,2},{4,5},{5,4},{6,7},{7,6},{8,9},{9,8},{10,11... | collective-permute-start | bytes 1572872 | tf_op jit(solution)/shard_map/ppermute | solution.py:252
  53.8 2.2 %collective-permute-start = (bf16[128,128]{1,0:T(8,128)(2,1)S(1)}, bf16[128,128]{1,0:T(8,128)(2,1)S(1)}, u32[]{:S(2)}, u32[]{:S(2)}) collective-permute-start(bf16[128,128]{1,0:T(8,128)(2,1)S(1)} %copy-done.10), channel_id=1, source_target_pairs={{0,1},{1,0},{2,3},{3,2},{4,5},{5,4},{6,7},{7,6},{8,9},{9,8},{10,11... | collective-permute-start | bytes 98312 | tf_op jit(solution)/shard_map/ppermute | solution.py:252
  56.1 0.8 copy-start.5
  56.1 1.0 copy-start.4
  63.5 13.0 %collective-permute-start.3 = (bf16[560,384]{1,0:T(8,128)(2,1)}, bf16[560,384]{1,0:T(8,128)(2,1)S(1)}, u32[]{:S(2)}, u32[]{:S(2)}) collective-permute-start(bf16[560,384]{1,0:T(8,128)(2,1)} %get-tuple-element.29), channel_id=1, source_target_pairs={{0,2},{2,4},{4,6},{6,0},{1,3},{3,5},{5,7},{7,1},{8,10},{10,12},{12... | collective-permute-start | bytes 1290248 | tf_op jit(solution)/shard_map/ppermute | solution.py:245
  64.9 14.5 %collective-permute-start.4 = (bf16[560,384]{1,0:T(8,128)(2,1)}, bf16[560,384]{1,0:T(8,128)(2,1)S(1)}, u32[]{:S(2)}, u32[]{:S(2)}) collective-permute-start(bf16[560,384]{1,0:T(8,128)(2,1)} %get-tuple-element.30), channel_id=1, source_target_pairs={{0,4},{2,6},{4,0},{6,2},{1,5},{3,7},{5,1},{7,3},{8,12},{10,14},{12... | collective-permute-start | bytes 1290248 | tf_op jit(solution)/shard_map/ppermute | solution.py:245
  66.1 20.8 %collective-permute-start.5 = (bf16[560,384]{1,0:T(8,128)(2,1)}, bf16[560,384]{1,0:T(8,128)(2,1)S(1)}, u32[]{:S(2)}, u32[]{:S(2)}) collective-permute-start(bf16[560,384]{1,0:T(8,128)(2,1)} %get-tuple-element.31), channel_id=1, source_target_pairs={{0,6},{2,0},{4,2},{6,4},{1,7},{3,1},{5,3},{7,5},{8,14},{10,8},{12,... | collective-permute-start | bytes 1290248 | tf_op jit(solution)/shard_map/ppermute | solution.py:245
  76.4 10.5 %copy-start.6 = (bf16[560,384]{1,0:T(8,128)(2,1)}, bf16[560,384]{1,0:T(8,128)(2,1)S(1)}, u32[]{:S(2)}) copy-start(bf16[560,384]{1,0:T(8,128)(2,1)S(1)} %collective-permute-done.3.m1) | copy-start | bytes 1290244
  79.4 7.5 %copy-start.7 = (bf16[560,384]{1,0:T(8,128)(2,1)}, bf16[560,384]{1,0:T(8,128)(2,1)S(1)}, u32[]{:S(2)}) copy-start(bf16[560,384]{1,0:T(8,128)(2,1)S(1)} %collective-permute-done.4.m2) | copy-start | bytes 1290244
  86.9 0.8 copy-start.8
  90.3 6.9 %collective-permute-start.6 = (bf16[288,384]{1,0:T(8,128)(2,1)}, bf16[288,384]{1,0:T(8,128)(2,1)S(1)}, u32[]{:S(2)}, u32[]{:S(2)}) collective-permute-start(bf16[288,384]{1,0:T(8,128)(2,1)} %get-tuple-element.33), channel_id=1, source_target_pairs={{0,8},{8,0},{1,9},{9,1},{2,10},{10,2},{3,11},{11,3},{4,12},{12,4},... | collective-permute-start | bytes 663560 | tf_op jit(solution)/shard_map/ppermute | solution.py:294
  97.1 0.7 copy-start.9
  99.9 6.6 %collective-permute-start.7 = (bf16[112,384]{1,0:T(8,128)(2,1)}, bf16[112,384]{1,0:T(8,128)(2,1)S(1)}, u32[]{:S(2)}, u32[]{:S(2)}) collective-permute-start(bf16[112,384]{1,0:T(8,128)(2,1)} %get-tuple-element.35), channel_id=1, source_target_pairs={{0,16},{16,32},{32,48},{48,0},{1,17},{17,33},{33,49},{49,1},{2,18}... | collective-permute-start | bytes 258056 | tf_op jit(solution)/shard_map/ppermute | solution.py:245
  101.9 6.3 %collective-permute-start.8 = (bf16[112,384]{1,0:T(8,128)(2,1)}, bf16[112,384]{1,0:T(8,128)(2,1)S(1)}, u32[]{:S(2)}, u32[]{:S(2)}) collective-permute-start(bf16[112,384]{1,0:T(8,128)(2,1)} %get-tuple-element.36), channel_id=1, source_target_pairs={{0,32},{16,48},{32,0},{48,16},{1,33},{17,49},{33,1},{49,17},{2,34}... | collective-permute-start | bytes 258056 | tf_op jit(solution)/shard_map/ppermute | solution.py:245
  104.5 4.7 %collective-permute-start.9 = (bf16[112,384]{1,0:T(8,128)(2,1)}, bf16[112,384]{1,0:T(8,128)(2,1)S(1)}, u32[]{:S(2)}, u32[]{:S(2)}) collective-permute-start(bf16[112,384]{1,0:T(8,128)(2,1)} %get-tuple-element.37), channel_id=1, source_target_pairs={{0,48},{16,0},{32,16},{48,32},{1,49},{17,1},{33,17},{49,33},{2,50}... | collective-permute-start | bytes 258056 | tf_op jit(solution)/shard_map/ppermute | solution.py:245
  106.5 2.7 %copy-start.11 = (bf16[112,384]{1,0:T(8,128)(2,1)}, bf16[112,384]{1,0:T(8,128)(2,1)S(1)}, u32[]{:S(2)}) copy-start(bf16[112,384]{1,0:T(8,128)(2,1)S(1)} %collective-permute-done.7.m1) | copy-start | bytes 258052
  108.1 1.1 copy-start.12
  109.2 0.6 copy-start.13
  111.6 9.5 %collective-permute-start.10 = (bf16[48,384]{1,0:T(8,128)(2,1)}, bf16[48,384]{1,0:T(8,128)(2,1)S(1)}, u32[]{:S(2)}, u32[]{:S(2)}) collective-permute-start(bf16[48,384]{1,0:T(8,128)(2,1)} %get-tuple-element.39), channel_id=1, source_target_pairs={{0,64},{64,128},{128,192},{192,0},{1,65},{65,129},{129,193},{193,1... | collective-permute-start | bytes 110600 | tf_op jit(solution)/shard_map/ppermute | solution.py:245
  114.0 8.1 %collective-permute-start.11 = (bf16[48,384]{1,0:T(8,128)(2,1)}, bf16[48,384]{1,0:T(8,128)(2,1)S(1)}, u32[]{:S(2)}, u32[]{:S(2)}) collective-permute-start(bf16[48,384]{1,0:T(8,128)(2,1)} %get-tuple-element.40), channel_id=1, source_target_pairs={{0,128},{64,192},{128,0},{192,64},{1,129},{65,193},{129,1},{193,65... | collective-permute-start | bytes 110600 | tf_op jit(solution)/shard_map/ppermute | solution.py:245
  117.6 5.5 %collective-permute-start.12 = (bf16[48,384]{1,0:T(8,128)(2,1)}, bf16[48,384]{1,0:T(8,128)(2,1)S(1)}, u32[]{:S(2)}, u32[]{:S(2)}) collective-permute-start(bf16[48,384]{1,0:T(8,128)(2,1)} %get-tuple-element.41), channel_id=1, source_target_pairs={{0,192},{64,0},{128,64},{192,128},{1,193},{65,1},{129,65},{193,129... | collective-permute-start | bytes 110600 | tf_op jit(solution)/shard_map/ppermute | solution.py:245
  121.1 2.0 %copy-start.14 = (bf16[48,384]{1,0:T(8,128)(2,1)}, bf16[48,384]{1,0:T(8,128)(2,1)S(1)}, u32[]{:S(2)}) copy-start(bf16[48,384]{1,0:T(8,128)(2,1)S(1)} %collective-permute-done.10.m1) | copy-start | bytes 110596
  122.0 1.0 copy-start.15
  123.1 0.6 copy-start.16
  126.5 0.9 copy-start
  (1 other events, 0.6 us)

commit v2 on v1

v2 whole, which is shorter than its diff:
```python
import jax
import jax.numpy as jnp
import numpy as np
from jax import lax
from jax.experimental import pallas as pl
from jax.experimental.pallas import tpu as pltpu
from jax.sharding import Mesh, PartitionSpec as P

BF = jnp.bfloat16
F32 = jnp.float32
TABLE = ("zl", "y", "c")
REP = ("zh", "x")
EMB = 128
LAT = 384
N_TAB = 16
N_REP = 16
D0 = 2176
FEAT = 136
LATP = 24
KEEP = 512
CAP = 160
SLOTS = N_REP * CAP
PAYLOAD = CAP + 16
UNIQ = 2048
SAMP = 2048
SCALE = float(32768) ** -0.5

HBM = pl.BlockSpec(memory_space=pltpu.HBM)
ANY = pl.BlockSpec(memory_space=pl.ANY)
VMEM = pl.BlockSpec(memory_space=pltpu.VMEM)
SMEM = pl.BlockSpec(memory_space=pltpu.SMEM)


def params(mib):
    return pltpu.CompilerParams(vmem_limit_bytes=mib * 1024 * 1024)


def coords(place_ref):
    i = place_ref[0]
    return (
        lax.shift_right_logical(i, 6),
        jnp.bitwise_and(lax.shift_right_logical(i, 4), 3),
        jnp.bitwise_and(lax.shift_right_logical(i, 3), 1),
        jnp.bitwise_and(lax.shift_right_logical(i, 1), 3),
        jnp.bitwise_and(i, 1),
    )


def nn(a, b):
    return lax.dot_general(a, b, (((1,), (0,)), ((), ())), preferred_element_type=F32)


def nt(a, b):
    return lax.dot_general(a, b, (((1,), (1,)), ((), ())), preferred_element_type=F32)


def tn(a, b):
    return lax.dot_general(a, b, (((0,), (0,)), ((), ())), preferred_element_type=F32)


def times(a, b):
    return (a.astype(F32) * b.astype(F32)).astype(BF)


def front_kernel(
    dense_hbm, pooled_hbm, cot_hbm, v_hbm, u_hbm, bias_hbm, out_hbm, lat_ref, gl_ref,
    dense_ref, pooled_ref, cot_ref, v_ref, u_ref, bias_ref, out_ref, sems, out_sems,
):
    pairs = (
        (pooled_hbm, pooled_ref), (v_hbm, v_ref), (dense_hbm, dense_ref),
        (cot_hbm, cot_ref), (u_hbm, u_ref), (bias_hbm, bias_ref),
    )
    loads = [pltpu.make_async_copy(src, dst, sems.at[i]) for i, (src, dst) in enumerate(pairs)]
    for load in loads:
        load.start()
    for load in loads[:3]:
        load.wait()
    dense, pooled = dense_ref[...], pooled_ref[...]
    latent = (nn(dense, v_ref[:EMB, :]) + nn(pooled, v_ref[EMB:, :])).astype(BF)
    for load in loads[3:]:
        load.wait()
    mix_dense = times(cot_ref[:, :EMB], dense)
    mix_pooled = times(cot_ref[:, EMB:], pooled)
    grad_latent = (nt(mix_dense, u_ref[:, :EMB]) + nt(mix_pooled, u_ref[:, EMB:])).astype(BF)
    lat_ref[...] = latent
    gl_ref[...] = grad_latent
    stores = []
    for t in range(N_TAB):
        cols = slice(EMB + t * EMB, EMB + (t + 1) * EMB)
        mixing = nn(latent, u_ref[:, cols]) + bias_ref[t + 1 : t + 2, :]
        backward = nt(grad_latent, v_ref[cols, :])
        out_ref[t] = (cot_ref[:, cols].astype(F32) * (mixing + 1.0) + backward).astype(BF)
        if t % 4 == 3:
            some = slice(t - 3, t + 1)
            store = pltpu.make_async_copy(out_ref.at[some], out_hbm.at[some], out_sems.at[t // 4])
            store.start()
            stores.append(store)
    for store in stores:
        store.wait()


def order_kernel(*_):
    pass


def weight_kernel(
    place_ref, lat_ref, gl_ref, pooled2_hbm, v_hbm, dense2_hbm, cot2_hbm, u_hbm, pooled_hbm, cot_hbm, dense_hbm,
    u0, u1, u2, u3, v_keep, v_send,
    pooled2_ref, v_ref, dense2_ref, cot2_ref, u_ref, pooled_ref, cot_ref, dense_ref,
    gu, gv, bias_row, bu0, bu1, bu2, bu3, bk, bs, load_sems, sems,
):
    pairs = (
        (pooled2_hbm, pooled2_ref), (v_hbm, v_ref), (dense2_hbm, dense2_ref), (cot2_hbm, cot2_ref),
        (u_hbm, u_ref), (pooled_hbm, pooled_ref), (cot_hbm, cot_ref), (dense_hbm, dense_ref),
    )
    loads = [pltpu.make_async_copy(src, dst, load_sems.at[i]) for i, (src, dst) in enumerate(pairs)]
    for load in loads:
        load.start()
    for load in loads[:3]:
        load.wait()
    lat2 = (nn(dense2_ref[...], v_ref[:EMB, :]) + nn(pooled2_ref[...], v_ref[EMB:, :])).astype(BF)
    for load in loads[3:5]:
        load.wait()
    md2 = times(cot2_ref[:, :EMB], dense2_ref[...])
    mp2 = times(cot2_ref[:, EMB:], pooled2_ref[...])
    gl2 = (nt(md2, u_ref[:, :EMB]) + nt(mp2, u_ref[:, EMB:])).astype(BF)
    lat = jnp.concatenate([lat_ref[...], lat2], axis=0)
    gl = jnp.concatenate([gl_ref[...], gl2], axis=0)
    for load in loads[5:]:
        load.wait()
    for j in range(D0 // EMB):
        cols = slice(j * EMB, (j + 1) * EMB)
        prev = slice((j - 1) * EMB, j * EMB)
        feat1 = dense_ref[...] if j == 0 else pooled_ref[:, prev]
        feat2 = dense2_ref[...] if j == 0 else pooled2_ref[:, prev]
        mix1 = times(cot_ref[:, cols], feat1)
        mix2 = md2 if j == 0 else mp2[:, prev]
        mix = jnp.concatenate([mix1, mix2], axis=0)
        feat = jnp.concatenate([feat1, feat2], axis=0)
        gu[cols, :] = tn(mix, lat)
        gv[cols, :] = tn(feat, gl)
        bias_row[:, cols] = jnp.sum(mix.astype(F32), axis=0, keepdims=True)
    high = bias_row[...].astype(BF)
    low = (bias_row[...] - high.astype(F32)).astype(BF)
    tail = jnp.zeros((1, 6 * LAT - D0), BF)
    rows = []
    for part in (high, low):
        whole = jnp.concatenate([part, tail], axis=1)
        rows += [whole[:, k * LAT : (k + 1) * LAT].astype(F32) for k in range(6)]
    rows.append(jnp.zeros((4, LAT), F32))
    bias_block = jnp.concatenate(rows, axis=0).astype(BF)
    _, _, zl, y, c = coords(place_ref)
    copies = []

    def block(g, zl, y):
        start = pl.multiple_of((zl * 8 + y * 2 + c) * FEAT, 8)
        return g[pl.ds(start, FEAT), :]

    def leave(buffer, out):
        copy = pltpu.make_async_copy(buffer, out, sems.at[len(copies)])
        copy.start()
        copies.append(copy)

    for s, (buffer, out) in enumerate(((bu0, u0), (bu1, u1), (bu2, u2), (bu3, u3))):
        dest_y = lax.rem(y + s, 4)
        buffer[0:272, :] = jnp.concatenate([block(gu, 0, dest_y), block(gu, 1, dest_y)], axis=0).astype(BF)
        buffer[272:288, :] = bias_block
        leave(buffer, out)
    for half, buffer, out in ((zl, bk, v_keep), (1 - zl, bs, v_send)):
        for i in range(2):
            pair = jnp.concatenate([block(gv, half, 2 * i), block(gv, half, 2 * i + 1)], axis=0)
            buffer[i * 272 : (i + 1) * 272, :] = pair.astype(BF)
        leave(buffer, out)
    for copy in copies:
        copy.wait()


def bias_again(block):
    total = block[0:6, :] + block[6:12, :]
    high = total.astype(BF).astype(F32)
    low = (total - high).astype(BF).astype(F32)
    return jnp.concatenate([high, low, jnp.zeros((4, LAT), F32)], axis=0)


def first_sum_kernel(
    place_ref, m0, m1, m2, m3, v_own, v_got, _, u_keep, u_send, v0, v1, v2, v3,
    acc_u, acc_v, bs, b1, b2, b3, sems,
):
    acc_u[...] = (m0[...].astype(F32) + m1[...].astype(F32)) + (m2[...].astype(F32) + m3[...].astype(F32))
    acc_v[...] = v_own[...].astype(F32) + v_got[...].astype(F32)
    _, _, zl, y, _ = coords(place_ref)
    bias = bias_again(acc_u[272:288, :])
    gap = jnp.zeros((8, LAT), F32)
    copies = []

    def leave(buffer, out):
        copy = pltpu.make_async_copy(buffer, out, sems.at[len(copies)])
        copy.start()
        copies.append(copy)

    bs[...] = jnp.concatenate(
        [acc_u[pl.ds(pl.multiple_of((1 - zl) * FEAT, 8), FEAT), :], gap, bias], axis=0
    ).astype(BF)
    leave(bs, u_send)
    for s, buffer, out in ((1, b1, v1), (2, b2, v2), (3, b3, v3)):
        start = pl.multiple_of(lax.rem(y + s, 4) * FEAT, 8)
        buffer[...] = jnp.concatenate([acc_v[pl.ds(start, FEAT), :], gap], axis=0).astype(BF)
        leave(buffer, out)
    u_keep[...] = jnp.concatenate(
        [acc_u[pl.ds(pl.multiple_of(zl * FEAT, 8), FEAT), :], gap, bias], axis=0
    )
    v0[...] = jnp.concatenate([acc_v[pl.ds(pl.multiple_of(y * FEAT, 8), FEAT), :], gap], axis=0)
    for copy in copies:
        copy.wait()


def pick(ref, starts, rows):
    return [ref[pl.ds(pl.multiple_of(start, 8), rows), :] for start in starts]


def split(keep_ref, send_ref, buffer, sem, kept, sent):
    buffer[...] = jnp.concatenate(sent, axis=0).astype(BF)
    copy = pltpu.make_async_copy(buffer, send_ref, sem.at[0])
    copy.start()
    keep_ref[...] = jnp.concatenate(kept, axis=0)
    copy.wait()


def second_sum_kernel(
    place_ref, u_keep, u_got, v0, v1, v2, v3, keep_ref, send_ref, flip, buffer, sem
):
    u = u_keep[...] + u_got[...].astype(F32)
    v = (v0[...] + v1[...].astype(F32)) + (v2[...].astype(F32) + v3[...].astype(F32))
    bias = bias_again(u[144:160, :])
    stacked = jnp.concatenate(
        [u[0:128], v[0:128], u[128:136], v[128:136], jnp.zeros((112, LAT), F32)], axis=0
    )
    flip[...] = stacked.T
    _, x, _, _, _ = coords(place_ref)

    def rows_of(dest_x):
        return pick(flip, [(zh * 4 + dest_x) * LATP for zh in range(4)], LATP)

    kept = rows_of(x) + rows_of(3 - x) + [bias]
    sent = rows_of(jnp.bitwise_xor(x, 1)) + rows_of(jnp.bitwise_xor(x, 2)) + [bias]
    split(keep_ref, send_ref, buffer, sem, kept, sent)


def third_sum_kernel(_, keep, got, keep_ref, send_ref, acc, buffer, sem):
    acc[...] = keep[...] + got[...].astype(F32)
    bias = bias_again(acc[192:208, :])
    split(keep_ref, send_ref, buffer, sem, [acc[0:96, :], bias], [acc[96:192, :], bias])


def fourth_sum_kernel(place_ref, keep, got, keep_ref, send_ref, acc, buffer, sem):
    acc[...] = keep[...] + got[...].astype(F32)
    bias = bias_again(acc[96:112, :])
    zh, _, _, _, _ = coords(place_ref)
    kept = pick(acc, [zh * LATP, (3 - zh) * LATP], LATP)
    sent = pick(acc, [jnp.bitwise_xor(zh, 1) * LATP, jnp.bitwise_xor(zh, 2) * LATP], LATP)
    split(keep_ref, send_ref, buffer, sem, kept + [bias], sent + [bias])


def fifth_sum_kernel(_, keep, got, keep_ref, send_ref, acc, buffer, sem):
    acc[...] = keep[...] + got[...].astype(F32)
    bias = bias_again(acc[48:64, :])
    gap = jnp.zeros((8, LAT), F32)
    split(keep_ref, send_ref, buffer, sem, [acc[0:24, :], gap, bias], [acc[24:48, :], gap, bias])


def last_kernel(keep, got, u_ref, v_ref, bias_ref):
    total = keep[...] + got[...].astype(F32)
    total = total * SCALE
    u_ref[:, 0:128] = total[0:LATP, 0:128]
    u_ref[:, 128:136] = total[0:LATP, 256:264]
    v_ref[:, 0:128] = total[0:LATP, 128:256]
    v_ref[:, 128:136] = total[0:LATP, 264:272]
    bias = total[32:38, :] + total[38:44, :]
    for j in range(D0 // 128):
        k, at = j // 3, (j % 3) * 128
        bias_ref[j : j + 1, :] = bias[k : k + 1, at : at + 128]


def index_kernel(uniq_ref, slot_ref, found_ref, pos_ref):
    uniq = uniq_ref[...]
    keeper = lax.shift_right_logical(uniq, 9)
    row = jnp.bitwise_and(uniq, KEEP - 1)
    upper = (
        lax.broadcasted_iota(jnp.int32, (128, 128), 0) <= lax.broadcasted_iota(jnp.int32, (128, 128), 1)
    ).astype(F32).astype(BF)
    which = lax.broadcasted_iota(jnp.int32, (N_REP, 128), 0)
    carry = jnp.zeros((N_REP, 1), F32)
    members, ranks, keepers = [], [], []
    for b in range(UNIQ // 128):
        own = keeper[:, b * 128 : (b + 1) * 128]
        member = (which == own).astype(F32)
        running = nn(member.astype(BF), upper) + carry
        carry = running[:, 127:128]
        members.append(member)
        keepers.append(own.astype(F32))
        ranks.append(jnp.sum(member * (running - 1.0), axis=0, keepdims=True))
    member = jnp.concatenate(members, axis=1)
    rank = jnp.concatenate(ranks, axis=1)
    row_high = lax.shift_right_logical(row, 4).astype(F32)
    row_low = jnp.bitwise_and(row, 15).astype(F32)
    digits = jnp.concatenate([member * row_high, member * row_low], axis=0).astype(BF)
    ranked = lax.broadcasted_iota(jnp.int32, (CAP, UNIQ), 0).astype(F32) == rank
    where = nt(digits, ranked.astype(F32).astype(BF))
    wide = jnp.concatenate([where, jnp.zeros((2 * N_REP, 256 - CAP), F32)], axis=1)
    for k in range(N_REP):
        high, low = wide[k : k + 1, :], wide[N_REP + k : N_REP + k + 1, :]
        block = [high[:, 0:128], high[:, 128:256], low[:, 0:128], low[:, 128:256]]
        pos_ref[k] = jnp.concatenate(block + [jnp.zeros((12, 128), F32)], axis=0).astype(BF)
    table = jnp.concatenate(ranks + keepers, axis=0).astype(BF)
    found = []
    for p in range(2):
        slot = slot_ref[p : p + 1, :]
        low = jnp.bitwise_and(slot, 127)
        high = lax.shift_right_logical(slot, 7)
        hot_low = (lax.broadcasted_iota(jnp.int32, (128, SAMP), 0) == low).astype(F32).astype(BF)
        picked = nn(table, hot_low)
        hot_high = (lax.broadcasted_iota(jnp.int32, (16, SAMP), 0) == high).astype(F32)
        found.append(
            (
                jnp.sum(hot_high * picked[0:16, :], axis=0, keepdims=True),
                jnp.sum(hot_high * picked[16:32, :], axis=0, keepdims=True),
            )
        )
    rows = [row for pair in found for row in pair]
    found_ref[...] = jnp.concatenate(rows + [jnp.zeros((4, SAMP), F32)], axis=0)


def rows_kernel(found_ref, got_ref, pos_ref, out_hbm, hot, out_ref, sems):
    places = lax.broadcasted_iota(jnp.int32, (CAP, SAMP), 0).astype(F32).astype(BF)
    one, zero = jnp.ones((CAP, SAMP), BF), jnp.zeros((CAP, SAMP), BF)
    stores = []
    for j in range(4):
        for i in range(4):
            k = j * 4 + i
            hits = []
            for p in range(2):
                at, kept = found_ref[2 * p : 2 * p + 1, :], found_ref[2 * p + 1 : 2 * p + 2, :]
                own = jnp.where(kept == float(k), at, -1.0).astype(BF)
                hits.append(jnp.where(places == own, one, zero))
            hot[j % 2, i * CAP : (i + 1) * CAP, :] = hits[0] + hits[1]
        sums = nn(hot[j % 2], got_ref[...]).astype(BF)
        for i in range(4):
            k = j * 4 + i
            out_ref[k, 0:CAP, :] = sums[i * CAP : (i + 1) * CAP, :]
            out_ref[k, CAP:PAYLOAD, :] = pos_ref[k]
        some = slice(j * 4, j * 4 + 4)
        store = pltpu.make_async_copy(out_ref.at[some], out_hbm.at[some], sems.at[j])
        store.start()
        stores.append(store)
    for store in stores:
        store.wait()


def keep_kernel(got_ref, out_ref):
    names = lax.broadcasted_iota(jnp.int32, (KEEP, CAP), 0).astype(F32)
    acc = jnp.zeros((KEEP, EMB), F32)
    for g in range(N_REP):
        pos = got_ref[g, CAP:PAYLOAD, :].astype(F32)
        at = pos[0:2, :] * 16.0 + pos[2:4, :]
        at = jnp.concatenate([at[0:1, :], at[1:2, 0 : CAP - 128]], axis=1)
        hot = (names == at).astype(F32).astype(BF)
        acc = acc + nn(hot, got_ref[g, 0:CAP, :])
    out_ref[...] = acc


def call(kernel, outs, ins, scratch=(), mib=24, spare=None, us=2):
    return pl.pallas_call(
        kernel,
        out_shape=tuple(jax.ShapeDtypeStruct(s, d) for _, s, d in outs),
        in_specs=[spec for spec, _ in ins],
        out_specs=tuple(spec for spec, _, _ in outs),
        scratch_shapes=list(scratch),
        input_output_aliases={} if spare is None else {spare[0]: spare[1]},
        compiler_params=params(mib),
        cost_estimate=pl.CostEstimate(flops=us * 10**9, bytes_accessed=us * 10**6, transcendentals=0),
    )(*[a for _, a in ins])


def near(*arrays):
    return [(VMEM, a) for a in arrays]


def shifted(messages, axis):
    return [
        lax.ppermute(m, axis, [(i, (i + s) % 4) for i in range(4)]) for s, m in enumerate(messages, 1)
    ]


def shards(dense, pooled, cot, proj_v, proj_u, bias, lookup_slot, uniq_rows):
    place = (SMEM, lax.axis_index(REP + TABLE).astype(jnp.int32).reshape(1))
    swap = [(0, 1), (1, 0)]
    other = [lax.ppermute(a, "c", swap) for a in (dense, pooled, cot)]
    dma = pltpu.SemaphoreType.DMA
    weights = [(HBM, a) for a in (dense, pooled, cot, proj_v, proj_u)]
    bias_rows = (D0 // 128, 128)
    outgoing, latent, grad_latent = call(
        front_kernel,
        [(HBM, (N_TAB, 128, EMB), BF), (VMEM, (128, LAT), BF), (VMEM, (128, LAT), BF)],
        weights + [(HBM, bias.reshape(bias_rows))],
        [pltpu.VMEM(a.shape, BF) for _, a in weights]
        + [pltpu.VMEM(bias_rows, F32), pltpu.VMEM((N_TAB, 128, EMB), BF), dma((6,)), dma((4,))],
        mib=56,
        us=5,
    )
    (outgoing,) = call(
        order_kernel,
        [(HBM, outgoing.shape, BF)],
        [(HBM, outgoing)] + [(ANY, a) for a in other],
        spare=(0, 0),
    )
    received = lax.all_to_all(outgoing, TABLE, 0, 0, tiled=True).reshape(SAMP, EMB)
    u_shape, v_shape = (288, LAT), (544, LAT)
    dense2, pooled2, cot2 = other
    loaded = (pooled2, proj_v, dense2, cot2, proj_u, pooled, cot, dense)
    u0, u1, u2, u3, v_keep, v_send = call(
        weight_kernel,
        [(HBM, u_shape, BF)] * 4 + [(HBM, v_shape, BF)] * 2,
        [place] + near(latent, grad_latent) + [(HBM, a) for a in loaded],
        [pltpu.VMEM(a.shape, BF) for a in loaded]
        + [pltpu.VMEM((D0, LAT), F32), pltpu.VMEM((D0, LAT), F32), pltpu.VMEM((1, D0), F32)]
        + [pltpu.VMEM(u_shape, BF)] * 4
        + [pltpu.VMEM(v_shape, BF)] * 2
        + [dma((8,)), dma((6,))],
        mib=56,
        us=5,
    )
    u_got = shifted([u1, u2, u3], "y")
    v_got = lax.ppermute(v_send, "zl", swap)
    found, pos = call(
        index_kernel,
        [(VMEM, (8, SAMP), F32), (VMEM, (N_REP, 16, 128), BF)],
        near(uniq_rows.reshape(1, UNIQ), lookup_slot.reshape(SAMP, 2).T),
    )
    (payload,) = call(
        rows_kernel,
        [(HBM, (N_REP, PAYLOAD, EMB), BF)],
        near(found, received, pos),
        [pltpu.VMEM((2, 4 * CAP, SAMP), BF), pltpu.VMEM((N_REP, PAYLOAD, EMB), BF), dma((4,))],
        us=7,
    )
    u_shape, v_shape = (160, LAT), (144, LAT)
    u_keep, u_send, v0, v1, v2, v3 = call(
        first_sum_kernel,
        [(VMEM, u_shape, F32), (HBM, u_shape, BF), (VMEM, v_shape, F32)] + [(HBM, v_shape, BF)] * 3,
        [place] + near(u0, *u_got, v_keep, v_got) + [(ANY, payload)],
        [pltpu.VMEM((288, LAT), F32), pltpu.VMEM((544, LAT), F32), pltpu.VMEM(u_shape, BF)]
        + [pltpu.VMEM(v_shape, BF)] * 3
        + [dma((4,))],
    )
    (payload,) = call(
        order_kernel, [(HBM, payload.shape, BF)], [(HBM, payload), (ANY, u_keep)], spare=(0, 0)
    )
    gathered = lax.all_to_all(payload, REP, 0, 0, tiled=True)
    u_got = lax.ppermute(u_send, "zl", swap)
    v_got = shifted([v1, v2, v3], "y")
    flat = [(0, 1), (1, 0), (2, 3), (3, 2)]
    cross = [(0, 3), (3, 0), (1, 2), (2, 1)]

    def halve(kernel, ins, in_rows, rows, axis, pairs, us=2):
        kept, sent = call(
            kernel,
            [(VMEM, (rows, LAT), F32), (HBM, (rows, LAT), BF)],
            [place] + near(*ins),
            [pltpu.VMEM((in_rows, LAT), F32), pltpu.VMEM((rows, LAT), BF), dma((1,))],
            us=us,
        )
        return kept, lax.ppermute(sent, axis, pairs)

    both = halve(second_sum_kernel, (u_keep, u_got, v0, *v_got), LAT, 208, "x", flat, us=100)
    both = halve(third_sum_kernel, both, 208, 112, "x", cross)
    both = halve(fourth_sum_kernel, both, 112, 64, "zh", flat)
    both = halve(fifth_sum_kernel, both, 64, 48, "zh", cross)
    part_u, part_v, whole_bias = call(
        last_kernel,
        [(VMEM, (LATP, FEAT), F32), (VMEM, (LATP, FEAT), F32), (VMEM, (D0 // 128, 128), F32)],
        near(*both),
    )
    (row_part,) = call(keep_kernel, [(VMEM, (KEEP, EMB), F32)], near(gathered))
    return part_u, part_v.T, whole_bias.reshape(D0), row_part.reshape(1, KEEP, EMB)


def solution(mesh):
    fine = Mesh(np.asarray(mesh.devices).reshape(4, 4, 2, 4, 2), ("zh", "x", "zl", "y", "c"))
    every = P(REP + TABLE, None)
    placed = (every, every, every, P(), P(), P(), P(REP, TABLE, None), P(REP, TABLE, None))
    return jax.shard_map(
        shards,
        mesh=fine,
        in_specs=placed,
        out_specs=(P(REP, TABLE), P(TABLE, REP), P(), P(TABLE, REP, None)),
        check_vma=False,
    )
```

time: 132 us -> 87.8 us (0.67)
  Pallas kernels: 51.9 us -> 22.6 us
  waiting for transfers between devices: 31.8 us -> 20.6 us
  local copies, waits for them, and re-layouts: 7.29 us -> 2.23 us
  starting transfers between devices: 37.5 us -> 40.8 us
  other arithmetic: 1.32 us -> 0 us
    pallas_call x9 -> x13, Pallas kernels: 51.9 us -> 22.6 us  [call(): pl.pallas_call(kernel, out_shape=tuple((jax.ShapeDtypeStruct(s, d) for _,...]
    ppermute x10 -> x12, waiting for transfers between devices: 30.4 us -> 20.6 us  [the longest x4 13.8 us: halve(): return (kept, lax.ppermute(sent, axis, pairs))]
    ppermute x10 -> x12, starting transfers between devices: 20.6 us -> 24.1 us  [the longest x4 14.6 us: halve(): return (kept, lax.ppermute(sent, axis, pairs))]
    unnamed x36 -> x18, local copies, waits for them, and re-layouts: 5.36 us -> 2.23 us
    ppermute x3, waiting for transfers between devices: 1.33 us -> 0.01 us  [shards(): other = [lax.ppermute(a, 'c', swap) for a in (dense, pooled, cot)]]
    pallas_call x1 -> x0, other arithmetic: 1.32 us -> none  [call(): pl.pallas_call(kernel, out_shape=tuple((jax.ShapeDtypeStruct(s, d) for s,...]
  transfers between devices with their start and end apart: 15 -> 17, of which waited for: 10 -> 7; matrix products, arithmetic and copies ran while one was open for 1% -> 0% of each run, Pallas kernels for 23% -> 23%
where the time goes in v2:
time: 87.8 us; the launch traced here: 87.1 us
  starting transfers between devices  40.8 us (46%)
  Pallas kernels  22.6 us (26%)
  waiting for transfers between devices  20.6 us (23%)
  local copies, waits for them, and re-layouts  2.23 us (3%)
    pallas_call x13, Pallas kernels, call(): pl.pallas_call(kernel, out_shape=tuple((jax.ShapeDtypeStruct(s, d) for _,...  22.6 us
    ppermute x4, starting transfers between devices, halve(): return (kept, lax.ppermute(sent, axis, pairs))  14.6 us
    ppermute x4, waiting for transfers between devices, halve(): return (kept, lax.ppermute(sent, axis, pairs))  13.8 us
    all_to_all x1, starting transfers between devices, shards(): gathered = lax.all_to_all(payload, REP, 0, 0, tiled=True)  10.1 us
    ppermute x6, starting transfers between devices, shifted(): lax.ppermute(m, axis, [(i, (i + s) % 4) for i in range(4)])  8.38 us
    all_to_all x1, starting transfers between devices, shards(): lax.all_to_all(outgoing, TABLE, 0, 0, tiled=True).reshape(SAMP, EMB)  5.87 us
    ppermute x6, waiting for transfers between devices, shifted(): lax.ppermute(m, axis, [(i, (i + s) % 4) for i in range(4)])  5.56 us
    unnamed x18, local copies, waits for them, and re-layouts  2.23 us
  transfers between devices with their start and end apart: 17, of which 7 were waited for; matrix products, arithmetic and copies ran while one was open for 0% of the time, Pallas kernels for 23%

profile of v2, /device:TPU:40, one launch (start us, length us, event | category | flops | bytes accessed | tf_op | source)
XLA Modules:
  0.0 87.1 jit_solution(11248348264805757692)
XLA Ops:
  0.7 0.5 collective-permute-start
  1.3 5.7 %shard_map.111 = (bf16[16,128,128]{2,1,0:T(8,128)(2,1)}, bf16[128,384]{1,0:T(8,128)(2,1)}, bf16[128,384]{1,0:T(8,128)(2,1)}) custom-call(bf16[128,128]{1,0:T(8,128)(2,1)} %dense_hbm.3, bf16[128,2048]{1,0:T(8,128)(2,1)} %pooled_hbm.3, bf16[128,2176]{1,0:T(8,128)(2,1)} %cot_hbm.3, bf16[2176,384]{1,0:T(8,128)(2,1)} %v_hbm.3, bf16[384,2176]{1,0:T(8,128)(2,1)} %u_hbm.3, ...), custom_call_target="tpu_custom_call" | custom-call | flops 5000000000 | bytes 5000000 | tf_op jit(solution)/shard_map/pallas_call | solution.py:372
  7.1 1.4 %copy-done = bf16[16,128,128]{2,1,0:T(8,128)(2,1)S(1)} copy-done((bf16[16,128,128]{2,1,0:T(8,128)(2,1)S(1)}, bf16[16,128,128]{2,1,0:T(8,128)(2,1)}, u32[]{:S(2)}) %copy-start) | copy-done | bytes 524312
  8.6 0.8 copy-done.1
  9.4 5.9 %all-to-all-start = ((bf16[16,128,128]{2,1,0:T(8,128)(2,1)}), bf16[16,128,128]{2,1,0:T(8,128)(2,1)S(1)}, u32[]{:S(2)}, u32[]{:S(2)}) async-start(bf16[16,128,128]{2,1,0:T(8,128)(2,1)} %copy-done.1), calls=%async_computation | async-start | bytes 1048576 | tf_op jit(solution)/shard_map/all_to_all | solution.py:416
  15.3 1.6 %shard_map.113 = (f32[8,2048]{1,0:T(8,128)S(1)}, bf16[16,16,128]{2,1,0:T(8,128)(2,1)S(1)}) custom-call(s32[1,2048]{1,0:T(1,128)S(1)} %bitcast.12, s32[2,2048]{1,0:T(2,128)S(1)} %bitcast.11), custom_call_target="tpu_custom_call" | custom-call | flops 2000000000 | bytes 2000000 | tf_op jit(solution)/shard_map/pallas_call | solution.py:372
  16.8 7.1 %shard_map.112 = (bf16[288,384]{1,0:T(8,128)(2,1)}, bf16[288,384]{1,0:T(8,128)(2,1)}, bf16[288,384]{1,0:T(8,128)(2,1)}, bf16[288,384]{1,0:T(8,128)(2,1)}, bf16[5...) custom-call(s32[1]{0:T(128)} %bitcast.place_ref._, bf16[128,384]{1,0:T(8,128)(2,1)} %get-tuple-element.32.lat_ref, ...), custom_call_target="tpu_custom_call" | custom-call | flops 5000000000 | bytes 5000000 | tf_op jit(solution)/shard_map/pallas_call | solution.py:372
  23.9 1.5 %collective-permute-start.3 = (bf16[288,384]{1,0:T(8,128)(2,1)}, bf16[288,384]{1,0:T(8,128)(2,1)S(1)}, u32[]{:S(2)}, u32[]{:S(2)}) collective-permute-start(bf16[288,384]{1,0:T(8,128)(2,1)} %get-tuple-element.35), channel_id=1, source_target_pairs={{0,2},{2,4},{4,6},{6,0},{1,3},{3,5},{5,7},{7,1},{8,10},{10,12},{12... | collective-permute-start | bytes 663560 | tf_op jit(solution)/shard_map/ppermute | solution.py:390
  25.5 1.2 %collective-permute-start.4 = (bf16[288,384]{1,0:T(8,128)(2,1)}, bf16[288,384]{1,0:T(8,128)(2,1)S(1)}, u32[]{:S(2)}, u32[]{:S(2)}) collective-permute-start(bf16[288,384]{1,0:T(8,128)(2,1)} %get-tuple-element.36), channel_id=1, source_target_pairs={{0,4},{2,6},{4,0},{6,2},{1,5},{3,7},{5,1},{7,3},{8,12},{10,14},{12... | collective-permute-start | bytes 663560 | tf_op jit(solution)/shard_map/ppermute | solution.py:390
  26.6 2.1 %collective-permute-start.5 = (bf16[288,384]{1,0:T(8,128)(2,1)}, bf16[288,384]{1,0:T(8,128)(2,1)S(1)}, u32[]{:S(2)}, u32[]{:S(2)}) collective-permute-start(bf16[288,384]{1,0:T(8,128)(2,1)} %get-tuple-element.37), channel_id=1, source_target_pairs={{0,6},{2,0},{4,2},{6,4},{1,7},{3,1},{5,3},{7,5},{8,14},{10,8},{12,... | collective-permute-start | bytes 663560 | tf_op jit(solution)/shard_map/ppermute | solution.py:390
  28.7 0.6 collective-permute-start.6
  29.3 3.7 %shard_map.115._.__0_ = bf16[16,176,128]{2,1,0:T(8,128)(2,1)} custom-call(f32[8,2048]{1,0:T(8,128)S(1)} %get-tuple-element.40.found_ref, bf16[2048,128]{1,0:T(8,128)(2,1)S(1)} %bitcast.10, bf16[16,16,128]{2,1,0:T(8,128)(2,1)S(1)} %get-tuple-element.42.pos_ref), custom_call_target="tpu_custom_call" | custom-call | flops 7000000000 | bytes 7000000 | tf_op jit(solution)/shard_map/pallas_call | solution.py:372
  33.0 2.5 %collective-permute-done.4.m2 = bf16[288,384]{1,0:T(8,128)(2,1)S(1)} collective-permute-done((bf16[288,384]{1,0:T(8,128)(2,1)}, bf16[288,384]{1,0:T(8,128)(2,1)S(1)}, u32[]{:S(2)}, u32[]{:S(2)}) %collective-permute-start.4) | collective-permute-done | bytes 221216 | tf_op jit(solution)/shard_map/ppermute | solution.py:390
  35.5 3.0 %collective-permute-done.5.m3 = bf16[288,384]{1,0:T(8,128)(2,1)S(1)} collective-permute-done((bf16[288,384]{1,0:T(8,128)(2,1)}, bf16[288,384]{1,0:T(8,128)(2,1)S(1)}, u32[]{:S(2)}, u32[]{:S(2)}) %collective-permute-start.5) | collective-permute-done | bytes 221216 | tf_op jit(solution)/shard_map/ppermute | solution.py:390
  38.5 1.3 %collective-permute-done.6.v_got = bf16[544,384]{1,0:T(8,128)(2,1)S(1)} collective-permute-done((bf16[544,384]{1,0:T(8,128)(2,1)}, bf16[544,384]{1,0:T(8,128)(2,1)S(1)}, u32[]{:S(2)}, u32[]{:S(2)}) %collective-permute-start.6) | collective-permute-done | bytes 417824 | tf_op jit(solution)/shard_map/ppermute | solution.py:433
  39.8 1.0 %shard_map.116 = (f32[160,384]{1,0:T(8,128)S(1)}, bf16[160,384]{1,0:T(8,128)(2,1)S(1)}, f32[144,384]{1,0:T(8,128)S(1)}, bf16[144,384]{1,0:T(8,128)(2,1)S(1)}, bf...) custom-call(s32[1]{0:T(128)} %bitcast.place_ref._, bf16[288,384]{1,0:T(8,128)(2,1)S(1)} %copy-done.8, ...), custom_call_target="tpu_custom_call" | custom-call | flops 2000000000 | bytes 2000000 | tf_op jit(solution)/shard_map/pallas_call | solution.py:372
  40.9 3.5 %collective-permute-start.9 = (bf16[144,384]{1,0:T(8,128)(2,1)S(1)}, bf16[144,384]{1,0:T(8,128)(2,1)S(1)}, u32[]{:S(2)}, u32[]{:S(2)}) collective-permute-start(bf16[144,384]{1,0:T(8,128)(2,1)S(1)} %get-tuple-element.47), channel_id=1, source_target_pairs={{0,4},{2,6},{4,0},{6,2},{1,5},{3,7},{5,1},{7,3},{8,12},{10,14},{12... | collective-permute-start | bytes 331784 | tf_op jit(solution)/shard_map/ppermute | solution.py:390
  44.4 0.6 collective-permute-start.7
  45.0 10.1 %all-to-all-start.1 = ((bf16[16,176,128]{2,1,0:T(8,128)(2,1)}), bf16[16,176,128]{2,1,0:T(8,128)(2,1)S(1)}, u32[]{:S(2)}, u32[]{:S(2)}) async-start(bf16[16,176,128]{2,1,0:T(8,128)(2,1)} %shard_map.122), calls=%async_computation.1 | async-start | bytes 1441792 | tf_op jit(solution)/shard_map/all_to_all | solution.py:458
  55.2 0.5 shard_map.117
  55.7 2.0 %collective-permute-start.11 = (bf16[208,384]{1,0:T(8,128)(2,1)S(1)}, bf16[208,384]{1,0:T(8,128)(2,1)S(1)}, u32[]{:S(2)}, u32[]{:S(2)}) collective-permute-start(bf16[208,384]{1,0:T(8,128)(2,1)S(1)} %get-tuple-element.50), channel_id=1, source_target_pairs={{0,16},{16,0},{32,48},{48,32},{1,17},{17,1},{33,49},{49,33},{2,18}... | collective-permute-start | bytes 479240 | tf_op jit(solution)/shard_map/ppermute | solution.py:472
  57.7 6.2 %collective-permute-done.11.got = bf16[208,384]{1,0:T(8,128)(2,1)S(1)} collective-permute-done((bf16[208,384]{1,0:T(8,128)(2,1)S(1)}, bf16[208,384]{1,0:T(8,128)(2,1)S(1)}, u32[]{:S(2)}, u32[]{:S(2)}) %collective-permute-start.11) | collective-permute-done | bytes 159776 | tf_op jit(solution)/shard_map/ppermute | solution.py:472
  63.9 0.2 shard_map.118
  64.1 2.8 %collective-permute-start.12 = (bf16[112,384]{1,0:T(8,128)(2,1)S(1)}, bf16[112,384]{1,0:T(8,128)(2,1)S(1)}, u32[]{:S(2)}, u32[]{:S(2)}) collective-permute-start(bf16[112,384]{1,0:T(8,128)(2,1)S(1)} %get-tuple-element.52), channel_id=1, source_target_pairs={{0,48},{48,0},{16,32},{32,16},{1,49},{49,1},{17,33},{33,17},{2,50}... | collective-permute-start | bytes 258056 | tf_op jit(solution)/shard_map/ppermute | solution.py:472
  66.9 3.3 %collective-permute-done.12.got = bf16[112,384]{1,0:T(8,128)(2,1)S(1)} collective-permute-done((bf16[112,384]{1,0:T(8,128)(2,1)S(1)}, bf16[112,384]{1,0:T(8,128)(2,1)S(1)}, u32[]{:S(2)}, u32[]{:S(2)}) %collective-permute-start.12) | collective-permute-done | bytes 86048 | tf_op jit(solution)/shard_map/ppermute | solution.py:472
  70.2 0.1 shard_map.119
  70.3 3.8 %collective-permute-start.13 = (bf16[64,384]{1,0:T(8,128)(2,1)S(1)}, bf16[64,384]{1,0:T(8,128)(2,1)S(1)}, u32[]{:S(2)}, u32[]{:S(2)}) collective-permute-start(bf16[64,384]{1,0:T(8,128)(2,1)S(1)} %get-tuple-element.54), channel_id=1, source_target_pairs={{0,64},{64,0},{128,192},{192,128},{1,65},{65,1},{129,193},{193,129... | collective-permute-start | bytes 147464 | tf_op jit(solution)/shard_map/ppermute | solution.py:472
  74.1 2.1 %collective-permute-done.13.got = bf16[64,384]{1,0:T(8,128)(2,1)S(1)} collective-permute-done((bf16[64,384]{1,0:T(8,128)(2,1)S(1)}, bf16[64,384]{1,0:T(8,128)(2,1)S(1)}, u32[]{:S(2)}, u32[]{:S(2)}) %collective-permute-start.13) | collective-permute-done | bytes 49184 | tf_op jit(solution)/shard_map/ppermute | solution.py:472
  76.3 6.0 %collective-permute-start.14 = (bf16[48,384]{1,0:T(8,128)(2,1)S(1)}, bf16[48,384]{1,0:T(8,128)(2,1)S(1)}, u32[]{:S(2)}, u32[]{:S(2)}) collective-permute-start(bf16[48,384]{1,0:T(8,128)(2,1)S(1)} %get-tuple-element.56), channel_id=1, source_target_pairs={{0,192},{192,0},{64,128},{128,64},{1,193},{193,1},{65,129},{129,65... | collective-permute-start | bytes 110600 | tf_op jit(solution)/shard_map/ppermute | solution.py:472
  82.3 2.2 %collective-permute-done.14.got = bf16[48,384]{1,0:T(8,128)(2,1)S(1)} collective-permute-done((bf16[48,384]{1,0:T(8,128)(2,1)S(1)}, bf16[48,384]{1,0:T(8,128)(2,1)S(1)}, u32[]{:S(2)}, u32[]{:S(2)}) %collective-permute-start.14) | collective-permute-done | bytes 36896 | tf_op jit(solution)/shard_map/ppermute | solution.py:472
  84.5 0.7 shard_map.121
  85.2 1.9 %shard_map.123 = f32[512,128]{1,0:T(8,128)} custom-call(bf16[16,176,128]{2,1,0:T(8,128)(2,1)S(1)} %all-to-all-done.1.got_ref), custom_call_target="tpu_custom_call" | custom-call | flops 2000000000 | bytes 2000000 | tf_op jit(solution)/shard_map/pallas_call | solution.py:372
  (33 shorter events, 0.4 us)
Async XLA Ops:
  0.6 6.5 %collective-permute-start.2 = (bf16[128,2176]{1,0:T(8,128)(2,1)}, bf16[128,2176]{1,0:T(8,128)(2,1)S(1)}, u32[]{:S(2)}, u32[]{:S(2)}) collective-permute-start(bf16[128,2176]{1,0:T(8,128)(2,1)} %cot_hbm.3), channel_id=1, source_target_pairs={{0,1},{1,0},{2,3},{3,2},{4,5},{5,4},{6,7},{7,6},{8,9},{9,8},{10,11... | collective-permute-start | bytes 1671176 | tf_op jit(solution)/shard_map/ppermute | solution.py:397
  0.7 6.4 %collective-permute-start = (bf16[128,2048]{1,0:T(8,128)(2,1)}, bf16[128,2048]{1,0:T(8,128)(2,1)S(1)}, u32[]{:S(2)}, u32[]{:S(2)}) collective-permute-start(bf16[128,2048]{1,0:T(8,128)(2,1)} %pooled_hbm.3), channel_id=1, source_target_pairs={{0,1},{1,0},{2,3},{3,2},{4,5},{5,4},{6,7},{7,6},{8,9},{9,8},{10,11... | collective-permute-start | bytes 1572872 | tf_op jit(solution)/shard_map/ppermute | solution.py:397
  1.2 5.8 %collective-permute-start.1 = (bf16[128,128]{1,0:T(8,128)(2,1)}, bf16[128,128]{1,0:T(8,128)(2,1)S(1)}, u32[]{:S(2)}, u32[]{:S(2)}) collective-permute-start(bf16[128,128]{1,0:T(8,128)(2,1)} %dense_hbm.3), channel_id=1, source_target_pairs={{0,1},{1,0},{2,3},{3,2},{4,5},{5,4},{6,7},{7,6},{8,9},{9,8},{10,11... | collective-permute-start | bytes 98312 | tf_op jit(solution)/shard_map/ppermute | solution.py:397
  7.1 1.5 %copy-start.4 = (bf16[128,128]{1,0:T(8,128)(2,1)}, bf16[128,128]{1,0:T(8,128)(2,1)S(1)}, u32[]{:S(2)}) copy-start(bf16[128,128]{1,0:T(8,128)(2,1)S(1)} %collective-permute-done.1.dense2_hbm.__1_) | copy-start | bytes 98308
  7.1 1.5 %copy-start.3 = (bf16[128,2048]{1,0:T(8,128)(2,1)}, bf16[128,2048]{1,0:T(8,128)(2,1)S(1)}, u32[]{:S(2)}) copy-start(bf16[128,2048]{1,0:T(8,128)(2,1)S(1)} %collective-permute-done.pooled2_hbm.__2_) | copy-start | bytes 1572868
  7.1 1.4 %copy-start.2 = (bf16[128,2176]{1,0:T(8,128)(2,1)}, bf16[128,2176]{1,0:T(8,128)(2,1)S(1)}, u32[]{:S(2)}) copy-start(bf16[128,2176]{1,0:T(8,128)(2,1)S(1)} %collective-permute-done.2.cot2_hbm.__3_) | copy-start | bytes 1671172
  7.1 1.4 %copy-start = (bf16[16,128,128]{2,1,0:T(8,128)(2,1)S(1)}, bf16[16,128,128]{2,1,0:T(8,128)(2,1)}, u32[]{:S(2)}) copy-start(bf16[16,128,128]{2,1,0:T(8,128)(2,1)} %get-tuple-element.41.__0_) | copy-start | bytes 1572868
  8.5 6.7 %copy-start.5 = (s32[2048,1,2]{0,2,1:T(2,128)S(1)}, s32[2048,1,2]{0,2,1:T(2,128)}, u32[]{:S(2)}) copy-start(s32[2048,1,2]{0,2,1:T(2,128)} %param.14) | copy-start | bytes 49156
  8.5 6.7 %copy-start.6 = (s32[1,1,2048]{2,1,0:T(1,128)S(1)}, s32[1,1,2048]{2,1,0:T(1,128)}, u32[]{:S(2)}) copy-start(s32[1,1,2048]{2,1,0:T(1,128)} %param.15) | copy-start | bytes 24580
  8.6 0.8 copy-start.1
  9.4 19.9 %all-to-all-start = ((bf16[16,128,128]{2,1,0:T(8,128)(2,1)}), bf16[16,128,128]{2,1,0:T(8,128)(2,1)S(1)}, u32[]{:S(2)}, u32[]{:S(2)}) async-start(bf16[16,128,128]{2,1,0:T(8,128)(2,1)} %copy-done.1), calls=%async_computation | async-start | bytes 1048576 | tf_op jit(solution)/shard_map/all_to_all | solution.py:416
  23.9 9.0 %collective-permute-start.3 = (bf16[288,384]{1,0:T(8,128)(2,1)}, bf16[288,384]{1,0:T(8,128)(2,1)S(1)}, u32[]{:S(2)}, u32[]{:S(2)}) collective-permute-start(bf16[288,384]{1,0:T(8,128)(2,1)} %get-tuple-element.35), channel_id=1, source_target_pairs={{0,2},{2,4},{4,6},{6,0},{1,3},{3,5},{5,7},{7,1},{8,10},{10,12},{12... | collective-permute-start | bytes 663560 | tf_op jit(solution)/shard_map/ppermute | solution.py:390
  25.5 10.0 %collective-permute-start.4 = (bf16[288,384]{1,0:T(8,128)(2,1)}, bf16[288,384]{1,0:T(8,128)(2,1)S(1)}, u32[]{:S(2)}, u32[]{:S(2)}) collective-permute-start(bf16[288,384]{1,0:T(8,128)(2,1)} %get-tuple-element.36), channel_id=1, source_target_pairs={{0,4},{2,6},{4,0},{6,2},{1,5},{3,7},{5,1},{7,3},{8,12},{10,14},{12... | collective-permute-start | bytes 663560 | tf_op jit(solution)/shard_map/ppermute | solution.py:390
  26.6 11.9 %collective-permute-start.5 = (bf16[288,384]{1,0:T(8,128)(2,1)}, bf16[288,384]{1,0:T(8,128)(2,1)S(1)}, u32[]{:S(2)}, u32[]{:S(2)}) collective-permute-start(bf16[288,384]{1,0:T(8,128)(2,1)} %get-tuple-element.37), channel_id=1, source_target_pairs={{0,6},{2,0},{4,2},{6,4},{1,7},{3,1},{5,3},{7,5},{8,14},{10,8},{12,... | collective-permute-start | bytes 663560 | tf_op jit(solution)/shard_map/ppermute | solution.py:390
  28.7 11.1 %collective-permute-start.6 = (bf16[544,384]{1,0:T(8,128)(2,1)}, bf16[544,384]{1,0:T(8,128)(2,1)S(1)}, u32[]{:S(2)}, u32[]{:S(2)}) collective-permute-start(bf16[544,384]{1,0:T(8,128)(2,1)} %get-tuple-element.39), channel_id=1, source_target_pairs={{0,8},{8,0},{1,9},{9,1},{2,10},{10,2},{3,11},{11,3},{4,12},{12,4},... | collective-permute-start | bytes 1253384 | tf_op jit(solution)/shard_map/ppermute | solution.py:433
  29.3 10.5 %copy-start.7 = (bf16[544,384]{1,0:T(8,128)(2,1)S(1)}, bf16[544,384]{1,0:T(8,128)(2,1)}, u32[]{:S(2)}) copy-start(bf16[544,384]{1,0:T(8,128)(2,1)} %get-tuple-element.38.v_own) | copy-start | bytes 1253380
  29.3 10.5 %copy-start.8 = (bf16[288,384]{1,0:T(8,128)(2,1)S(1)}, bf16[288,384]{1,0:T(8,128)(2,1)}, u32[]{:S(2)}) copy-start(bf16[288,384]{1,0:T(8,128)(2,1)} %get-tuple-element.34.m0) | copy-start | bytes 663556
  40.8 14.3 %collective-permute-start.8 = (bf16[144,384]{1,0:T(8,128)(2,1)S(1)}, bf16[144,384]{1,0:T(8,128)(2,1)S(1)}, u32[]{:S(2)}, u32[]{:S(2)}) collective-permute-start(bf16[144,384]{1,0:T(8,128)(2,1)S(1)} %get-tuple-element.46), channel_id=1, source_target_pairs={{0,2},{2,4},{4,6},{6,0},{1,3},{3,5},{5,7},{7,1},{8,10},{10,12},{12... | collective-permute-start | bytes 331784 | tf_op jit(solution)/shard_map/ppermute | solution.py:390
  40.9 14.2 %collective-permute-start.9 = (bf16[144,384]{1,0:T(8,128)(2,1)S(1)}, bf16[144,384]{1,0:T(8,128)(2,1)S(1)}, u32[]{:S(2)}, u32[]{:S(2)}) collective-permute-start(bf16[144,384]{1,0:T(8,128)(2,1)S(1)} %get-tuple-element.47), channel_id=1, source_target_pairs={{0,4},{2,6},{4,0},{6,2},{1,5},{3,7},{5,1},{7,3},{8,12},{10,14},{12... | collective-permute-start | bytes 331784 | tf_op jit(solution)/shard_map/ppermute | solution.py:390
  44.4 10.7 %collective-permute-start.10 = (bf16[144,384]{1,0:T(8,128)(2,1)S(1)}, bf16[144,384]{1,0:T(8,128)(2,1)S(1)}, u32[]{:S(2)}, u32[]{:S(2)}) collective-permute-start(bf16[144,384]{1,0:T(8,128)(2,1)S(1)} %get-tuple-element.48), channel_id=1, source_target_pairs={{0,6},{2,0},{4,2},{6,4},{1,7},{3,1},{5,3},{7,5},{8,14},{10,8},{12,... | collective-permute-start | bytes 331784 | tf_op jit(solution)/shard_map/ppermute | solution.py:390
  44.4 10.7 %collective-permute-start.7 = (bf16[160,384]{1,0:T(8,128)(2,1)S(1)}, bf16[160,384]{1,0:T(8,128)(2,1)S(1)}, u32[]{:S(2)}, u32[]{:S(2)}) collective-permute-start(bf16[160,384]{1,0:T(8,128)(2,1)S(1)} %get-tuple-element.44), channel_id=1, source_target_pairs={{0,8},{8,0},{1,9},{9,1},{2,10},{10,2},{3,11},{11,3},{4,12},{12,4},... | collective-permute-start | bytes 368648 | tf_op jit(solution)/shard_map/ppermute | solution.py:459
  45.0 40.2 %all-to-all-start.1 = ((bf16[16,176,128]{2,1,0:T(8,128)(2,1)}), bf16[16,176,128]{2,1,0:T(8,128)(2,1)S(1)}, u32[]{:S(2)}, u32[]{:S(2)}) async-start(bf16[16,176,128]{2,1,0:T(8,128)(2,1)} %shard_map.122), calls=%async_computation.1 | async-start | bytes 1441792 | tf_op jit(solution)/shard_map/all_to_all | solution.py:458
  55.7 8.2 %collective-permute-start.11 = (bf16[208,384]{1,0:T(8,128)(2,1)S(1)}, bf16[208,384]{1,0:T(8,128)(2,1)S(1)}, u32[]{:S(2)}, u32[]{:S(2)}) collective-permute-start(bf16[208,384]{1,0:T(8,128)(2,1)S(1)} %get-tuple-element.50), channel_id=1, source_target_pairs={{0,16},{16,0},{32,48},{48,32},{1,17},{17,1},{33,49},{49,33},{2,18}... | collective-permute-start | bytes 479240 | tf_op jit(solution)/shard_map/ppermute | solution.py:472
  64.1 6.1 %collective-permute-start.12 = (bf16[112,384]{1,0:T(8,128)(2,1)S(1)}, bf16[112,384]{1,0:T(8,128)(2,1)S(1)}, u32[]{:S(2)}, u32[]{:S(2)}) collective-permute-start(bf16[112,384]{1,0:T(8,128)(2,1)S(1)} %get-tuple-element.52), channel_id=1, source_target_pairs={{0,48},{48,0},{16,32},{32,16},{1,49},{49,1},{17,33},{33,17},{2,50}... | collective-permute-start | bytes 258056 | tf_op jit(solution)/shard_map/ppermute | solution.py:472
  70.3 5.9 %collective-permute-start.13 = (bf16[64,384]{1,0:T(8,128)(2,1)S(1)}, bf16[64,384]{1,0:T(8,128)(2,1)S(1)}, u32[]{:S(2)}, u32[]{:S(2)}) collective-permute-start(bf16[64,384]{1,0:T(8,128)(2,1)S(1)} %get-tuple-element.54), channel_id=1, source_target_pairs={{0,64},{64,0},{128,192},{192,128},{1,65},{65,1},{129,193},{193,129... | collective-permute-start | bytes 147464 | tf_op jit(solution)/shard_map/ppermute | solution.py:472
  76.3 8.2 %collective-permute-start.14 = (bf16[48,384]{1,0:T(8,128)(2,1)S(1)}, bf16[48,384]{1,0:T(8,128)(2,1)S(1)}, u32[]{:S(2)}, u32[]{:S(2)}) collective-permute-start(bf16[48,384]{1,0:T(8,128)(2,1)S(1)} %get-tuple-element.56), channel_id=1, source_target_pairs={{0,192},{192,0},{64,128},{128,64},{1,193},{193,1},{65,129},{129,65... | collective-permute-start | bytes 110600 | tf_op jit(solution)/shard_map/ppermute | solution.py:472

commit v3 on v2

--- a/solution.py
+++ b/solution.py
@@ -62,30 +62,33 @@
     return (a.astype(F32) * b.astype(F32)).astype(BF)
 
 
-def front_kernel(
-    dense_hbm, pooled_hbm, cot_hbm, v_hbm, u_hbm, bias_hbm, out_hbm, lat_ref, gl_ref,
-    dense_ref, pooled_ref, cot_ref, v_ref, u_ref, bias_ref, out_ref, sems, out_sems,
+def pooled_kernel(
+    lat_ref, gl_ref, cot_hbm, v_hbm, u_hbm, bias_hbm, out_hbm,
+    cot_ref, v_ref, u_ref, bias_ref, out_ref, sems, v_sems, u_sems, out_sems,
 ):
-    pairs = (
-        (pooled_hbm, pooled_ref), (v_hbm, v_ref), (dense_hbm, dense_ref),
-        (cot_hbm, cot_ref), (u_hbm, u_ref), (bias_hbm, bias_ref),
-    )
-    loads = [pltpu.make_async_copy(src, dst, sems.at[i]) for i, (src, dst) in enumerate(pairs)]
+    loads = [
+        pltpu.make_async_copy(cot_hbm, cot_ref, sems.at[0]),
+        pltpu.make_async_copy(bias_hbm, bias_ref, sems.at[1]),
+    ]
+    parts = []
+    for j in range(4):
+        cols = slice(EMB + j * 512, EMB + (j + 1) * 512)
+        parts.append(
+            (
+                pltpu.make_async_copy(u_hbm.at[:, cols], u_ref.at[:, cols], u_sems.at[j]),
+                pltpu.make_async_copy(v_hbm.at[cols, :], v_ref.at[cols, :], v_sems.at[j]),
+            )
+        )
+    for copy in (*parts[0], *loads, *parts[1], *parts[2], *parts[3]):
+        copy.start()
+    latent, grad_latent = lat_ref[...], gl_ref[...]
     for load in loads:
-        load.start()
-    for load in loads[:3]:
         load.wait()
-    dense, pooled = dense_ref[...], pooled_ref[...]
-    latent = (nn(dense, v_ref[:EMB, :]) + nn(pooled, v_ref[EMB:, :])).astype(BF)
-    for load in loads[3:]:
-        load.wait()
-    mix_dense = times(cot_ref[:, :EMB], dense)
-    mix_pooled = times(cot_ref[:, EMB:], pooled)
-    grad_latent = (nt(mix_dense, u_ref[:, :EMB]) + nt(mix_pooled, u_ref[:, EMB:])).astype(BF)
-    lat_ref[...] = latent
-    gl_ref[...] = grad_latent
     stores = []
     for t in range(N_TAB):
+        if t % 4 == 0:
+            for part in parts[t // 4]:
+                part.wait()
         cols = slice(EMB + t * EMB, EMB + (t + 1) * EMB)
         mixing = nn(latent, u_ref[:, cols]) + bias_ref[t + 1 : t + 2, :]
         backward = nt(grad_latent, v_ref[cols, :])
@@ -99,44 +102,36 @@
         store.wait()
 
 
-def order_kernel(*_):
-    pass
-
-
 def weight_kernel(
-    place_ref, lat_ref, gl_ref, pooled2_hbm, v_hbm, dense2_hbm, cot2_hbm, u_hbm, pooled_hbm, cot_hbm, dense_hbm,
-    u0, u1, u2, u3, v_keep, v_send,
-    pooled2_ref, v_ref, dense2_ref, cot2_ref, u_ref, pooled_ref, cot_ref, dense_ref,
+    place_ref, pooled_hbm, pooled2_hbm, dense_hbm, dense2_hbm, v_hbm, cot_hbm, cot2_hbm, u_hbm, _,
+    u0, u1, u2, u3, v_keep, v_send, lat_ref, gl_ref,
+    pooled_ref, dense_ref, cot_ref, mix_ref, v_ref, u_ref,
     gu, gv, bias_row, bu0, bu1, bu2, bu3, bk, bs, load_sems, sems,
 ):
+    own, other = slice(0, 128), slice(128, 256)
     pairs = (
-        (pooled2_hbm, pooled2_ref), (v_hbm, v_ref), (dense2_hbm, dense2_ref), (cot2_hbm, cot2_ref),
-        (u_hbm, u_ref), (pooled_hbm, pooled_ref), (cot_hbm, cot_ref), (dense_hbm, dense_ref),
+        (pooled_hbm, pooled_ref.at[own, :]), (pooled2_hbm, pooled_ref.at[other, :]),
+        (dense_hbm, dense_ref.at[own, :]), (dense2_hbm, dense_ref.at[other, :]),
+        (v_hbm, v_ref), (cot_hbm, cot_ref.at[own, :]), (cot2_hbm, cot_ref.at[other, :]), (u_hbm, u_ref),
     )
     loads = [pltpu.make_async_copy(src, dst, load_sems.at[i]) for i, (src, dst) in enumerate(pairs)]
     for load in loads:
         load.start()
-    for load in loads[:3]:
+    for load in loads[:5]:
         load.wait()
-    lat2 = (nn(dense2_ref[...], v_ref[:EMB, :]) + nn(pooled2_ref[...], v_ref[EMB:, :])).astype(BF)
-    for load in loads[3:5]:
+    lat = (nn(dense_ref[...], v_ref[:EMB, :]) + nn(pooled_ref[...], v_ref[EMB:, :])).astype(BF)
+    for load in loads[5:7]:
         load.wait()
-    md2 = times(cot2_ref[:, :EMB], dense2_ref[...])
-    mp2 = times(cot2_ref[:, EMB:], pooled2_ref[...])
-    gl2 = (nt(md2, u_ref[:, :EMB]) + nt(mp2, u_ref[:, EMB:])).astype(BF)
-    lat = jnp.concatenate([lat_ref[...], lat2], axis=0)
-    gl = jnp.concatenate([gl_ref[...], gl2], axis=0)
-    for load in loads[5:]:
-        load.wait()
+    mix_ref[:, :EMB] = times(cot_ref[:, :EMB], dense_ref[...])
+    mix_ref[:, EMB:] = times(cot_ref[:, EMB:], pooled_ref[...])
+    loads[7].wait()
+    gl = nt(mix_ref[...], u_ref[...]).astype(BF)
+    lat_ref[...] = lat[0:128, :]
+    gl_ref[...] = gl[0:128, :]
     for j in range(D0 // EMB):
         cols = slice(j * EMB, (j + 1) * EMB)
-        prev = slice((j - 1) * EMB, j * EMB)
-        feat1 = dense_ref[...] if j == 0 else pooled_ref[:, prev]
-        feat2 = dense2_ref[...] if j == 0 else pooled2_ref[:, prev]
-        mix1 = times(cot_ref[:, cols], feat1)
-        mix2 = md2 if j == 0 else mp2[:, prev]
-        mix = jnp.concatenate([mix1, mix2], axis=0)
-        feat = jnp.concatenate([feat1, feat2], axis=0)
+        mix = mix_ref[:, cols]
+        feat = dense_ref[...] if j == 0 else pooled_ref[:, (j - 1) * EMB : j * EMB]
         gu[cols, :] = tn(mix, lat)
         gv[cols, :] = tn(feat, gl)
         bias_row[:, cols] = jnp.sum(mix.astype(F32), axis=0, keepdims=True)
@@ -183,7 +178,7 @@
 
 
 def first_sum_kernel(
-    place_ref, m0, m1, m2, m3, v_own, v_got, _, u_keep, u_send, v0, v1, v2, v3,
+    place_ref, m0, m1, m2, m3, v_own, v_got, u_keep, u_send, v0, v1, v2, v3,
     acc_u, acc_v, bs, b1, b2, b3, sems,
 ):
     acc_u[...] = (m0[...].astype(F32) + m1[...].astype(F32)) + (m2[...].astype(F32) + m3[...].astype(F32))
@@ -227,7 +222,7 @@
 
 
 def second_sum_kernel(
-    place_ref, u_keep, u_got, v0, v1, v2, v3, keep_ref, send_ref, flip, buffer, sem
+    place_ref, u_keep, u_got, v0, v1, v2, v3, _, keep_ref, send_ref, flip, buffer, sem
 ):
     u = u_keep[...] + u_got[...].astype(F32)
     v = (v0[...] + v1[...].astype(F32)) + (v2[...].astype(F32) + v3[...].astype(F32))
@@ -236,29 +231,29 @@
         [u[0:128], v[0:128], u[128:136], v[128:136], jnp.zeros((112, LAT), F32)], axis=0
     )
     flip[...] = stacked.T
-    _, x, _, _, _ = coords(place_ref)
-
-    def rows_of(dest_x):
-        return pick(flip, [(zh * 4 + dest_x) * LATP for zh in range(4)], LATP)
-
-    kept = rows_of(x) + rows_of(3 - x) + [bias]
-    sent = rows_of(jnp.bitwise_xor(x, 1)) + rows_of(jnp.bitwise_xor(x, 2)) + [bias]
+    zh, x, _, _, _ = coords(place_ref)
+
+    def rows_of(dest):
+        order = (x, 3 - x, jnp.bitwise_xor(x, 1), jnp.bitwise_xor(x, 2))
+        return pick(flip, [(dest * 4 + dest_x) * LATP for dest_x in order], LATP)
+
+    kept = rows_of(zh) + rows_of(3 - zh) + [bias]
+    sent = rows_of(jnp.bitwise_xor(zh, 1)) + rows_of(jnp.bitwise_xor(zh, 2)) + [bias]
     split(keep_ref, send_ref, buffer, sem, kept, sent)
 
 
 def third_sum_kernel(_, keep, got, keep_ref, send_ref, acc, buffer, sem):
     acc[...] = keep[...] + got[...].astype(F32)
     bias = bias_again(acc[192:208, :])
-    split(keep_ref, send_ref, buffer, sem, [acc[0:96, :], bias], [acc[96:192, :], bias])
-
-
-def fourth_sum_kernel(place_ref, keep, got, keep_ref, send_ref, acc, buffer, sem):
+    kept = [acc[0:48, :], acc[96:144, :], bias]
+    split(keep_ref, send_ref, buffer, sem, kept, [acc[48:96, :], acc[144:192, :], bias])
+
+
+def fourth_sum_kernel(_, keep, got, keep_ref, send_ref, acc, buffer, sem):
     acc[...] = keep[...] + got[...].astype(F32)
     bias = bias_again(acc[96:112, :])
-    zh, _, _, _, _ = coords(place_ref)
-    kept = pick(acc, [zh * LATP, (3 - zh) * LATP], LATP)
-    sent = pick(acc, [jnp.bitwise_xor(zh, 1) * LATP, jnp.bitwise_xor(zh, 2) * LATP], LATP)
-    split(keep_ref, send_ref, buffer, sem, kept + [bias], sent + [bias])
+    kept = [acc[0:24, :], acc[48:72, :], bias]
+    split(keep_ref, send_ref, buffer, sem, kept, [acc[24:48, :], acc[72:96, :], bias])
 
 
 def fifth_sum_kernel(_, keep, got, keep_ref, send_ref, acc, buffer, sem):
@@ -330,7 +325,7 @@
     found_ref[...] = jnp.concatenate(rows + [jnp.zeros((4, SAMP), F32)], axis=0)
 
 
-def rows_kernel(found_ref, got_ref, pos_ref, out_hbm, hot, out_ref, sems):
+def rows_kernel(found_ref, got_ref, pos_ref, _, out_hbm, hot, out_ref, sems):
     places = lax.broadcasted_iota(jnp.int32, (CAP, SAMP), 0).astype(F32).astype(BF)
     one, zero = jnp.ones((CAP, SAMP), BF), jnp.zeros((CAP, SAMP), BF)
     stores = []
@@ -396,84 +391,79 @@
     swap = [(0, 1), (1, 0)]
     other = [lax.ppermute(a, "c", swap) for a in (dense, pooled, cot)]
     dma = pltpu.SemaphoreType.DMA
-    weights = [(HBM, a) for a in (dense, pooled, cot, proj_v, proj_u)]
-    bias_rows = (D0 // 128, 128)
-    outgoing, latent, grad_latent = call(
-        front_kernel,
-        [(HBM, (N_TAB, 128, EMB), BF), (VMEM, (128, LAT), BF), (VMEM, (128, LAT), BF)],
-        weights + [(HBM, bias.reshape(bias_rows))],
-        [pltpu.VMEM(a.shape, BF) for _, a in weights]
-        + [pltpu.VMEM(bias_rows, F32), pltpu.VMEM((N_TAB, 128, EMB), BF), dma((6,)), dma((4,))],
+    dense2, pooled2, cot2 = other
+    found, pos = call(
+        index_kernel,
+        [(VMEM, (8, SAMP), F32), (VMEM, (N_REP, 16, 128), BF)],
+        near(uniq_rows.reshape(1, UNIQ), lookup_slot.reshape(SAMP, 2).T),
         mib=56,
-        us=5,
-    )
-    (outgoing,) = call(
-        order_kernel,
-        [(HBM, outgoing.shape, BF)],
-        [(HBM, outgoing)] + [(ANY, a) for a in other],
-        spare=(0, 0),
-    )
-    received = lax.all_to_all(outgoing, TABLE, 0, 0, tiled=True).reshape(SAMP, EMB)
-    u_shape, v_shape = (288, LAT), (544, LAT)
-    dense2, pooled2, cot2 = other
-    loaded = (pooled2, proj_v, dense2, cot2, proj_u, pooled, cot, dense)
-    u0, u1, u2, u3, v_keep, v_send = call(
+    )
+    u_shape, v_shape, lat_shape = (288, LAT), (544, LAT), (128, LAT)
+    u0, u1, u2, u3, v_keep, v_send, latent, grad_latent = call(
         weight_kernel,
-        [(HBM, u_shape, BF)] * 4 + [(HBM, v_shape, BF)] * 2,
-        [place] + near(latent, grad_latent) + [(HBM, a) for a in loaded],
-        [pltpu.VMEM(a.shape, BF) for a in loaded]
+        [(HBM, u_shape, BF)] * 4 + [(HBM, v_shape, BF)] * 2 + [(VMEM, lat_shape, BF)] * 2,
+        [place] + [(HBM, a) for a in (pooled, pooled2, dense, dense2, proj_v, cot, cot2, proj_u)]
+        + [(ANY, found)],
+        [pltpu.VMEM((256, w), BF) for w in (D0 - EMB, EMB, D0, D0)]
+        + [pltpu.VMEM((D0, LAT), BF), pltpu.VMEM((LAT, D0), BF)]
         + [pltpu.VMEM((D0, LAT), F32), pltpu.VMEM((D0, LAT), F32), pltpu.VMEM((1, D0), F32)]
         + [pltpu.VMEM(u_shape, BF)] * 4
         + [pltpu.VMEM(v_shape, BF)] * 2
         + [dma((8,)), dma((6,))],
         mib=56,
-        us=5,
-    )
+        us=6,
+    )
+    bias_rows, out_shape = (D0 // 128, 128), (N_TAB, 128, EMB)
+    (outgoing,) = call(
+        pooled_kernel,
+        [(HBM, out_shape, BF)],
+        near(latent, grad_latent)
+        + [(HBM, a) for a in (cot, proj_v, proj_u, bias.reshape(bias_rows))],
+        [pltpu.VMEM((128, D0), BF), pltpu.VMEM((D0, LAT), BF), pltpu.VMEM((LAT, D0), BF)]
+        + [pltpu.VMEM(bias_rows, F32), pltpu.VMEM(out_shape, BF)]
+        + [dma((2,)), dma((4,)), dma((4,)), dma((4,))],
+        mib=56,
+        us=4,
+    )
+    received = lax.all_to_all(outgoing, TABLE, 0, 0, tiled=True).reshape(SAMP, EMB)
     u_got = shifted([u1, u2, u3], "y")
     v_got = lax.ppermute(v_send, "zl", swap)
-    found, pos = call(
-        index_kernel,
-        [(VMEM, (8, SAMP), F32), (VMEM, (N_REP, 16, 128), BF)],
-        near(uniq_rows.reshape(1, UNIQ), lookup_slot.reshape(SAMP, 2).T),
-    )
-    (payload,) = call(
-        rows_kernel,
-        [(HBM, (N_REP, PAYLOAD, EMB), BF)],
-        near(found, received, pos),
-        [pltpu.VMEM((2, 4 * CAP, SAMP), BF), pltpu.VMEM((N_REP, PAYLOAD, EMB), BF), dma((4,))],
-        us=7,
-    )
     u_shape, v_shape = (160, LAT), (144, LAT)
     u_keep, u_send, v0, v1, v2, v3 = call(
         first_sum_kernel,
         [(VMEM, u_shape, F32), (HBM, u_shape, BF), (VMEM, v_shape, F32)] + [(HBM, v_shape, BF)] * 3,
-        [place] + near(u0, *u_got, v_keep, v_got) + [(ANY, payload)],
+        [place] + near(u0, *u_got, v_keep, v_got),
         [pltpu.VMEM((288, LAT), F32), pltpu.VMEM((544, LAT), F32), pltpu.VMEM(u_shape, BF)]
         + [pltpu.VMEM(v_shape, BF)] * 3
         + [dma((4,))],
+        us=100,
     )
     (payload,) = call(
-        order_kernel, [(HBM, payload.shape, BF)], [(HBM, payload), (ANY, u_keep)], spare=(0, 0)
-    )
-    gathered = lax.all_to_all(payload, REP, 0, 0, tiled=True)
+        rows_kernel,
+        [(HBM, (N_REP, PAYLOAD, EMB), BF)],
+        near(found, received, pos) + [(ANY, u_keep)],
+        [pltpu.VMEM((2, 4 * CAP, SAMP), BF), pltpu.VMEM((N_REP, PAYLOAD, EMB), BF), dma((4,))],
+        us=7,
+    )
     u_got = lax.ppermute(u_send, "zl", swap)
     v_got = shifted([v1, v2, v3], "y")
     flat = [(0, 1), (1, 0), (2, 3), (3, 2)]
     cross = [(0, 3), (3, 0), (1, 2), (2, 1)]
 
-    def halve(kernel, ins, in_rows, rows, axis, pairs, us=2):
+    def halve(kernel, ins, in_rows, rows, axis, pairs, us=2, after=()):
         kept, sent = call(
             kernel,
             [(VMEM, (rows, LAT), F32), (HBM, (rows, LAT), BF)],
-            [place] + near(*ins),
+            [place] + near(*ins) + [(ANY, a) for a in after],
             [pltpu.VMEM((in_rows, LAT), F32), pltpu.VMEM((rows, LAT), BF), dma((1,))],
             us=us,
         )
         return kept, lax.ppermute(sent, axis, pairs)
 
-    both = halve(second_sum_kernel, (u_keep, u_got, v0, *v_got), LAT, 208, "x", flat, us=100)
-    both = halve(third_sum_kernel, both, 208, 112, "x", cross)
-    both = halve(fourth_sum_kernel, both, 112, 64, "zh", flat)
+    both = halve(second_sum_kernel, (u_keep, u_got, v0, *v_got), LAT, 208, "zh", flat, after=(payload,))
+    gathered = lax.all_to_all(payload, REP, 0, 0, tiled=True)
+    both = halve(third_sum_kernel, both, 208, 112, "x", flat, us=100)
+    both = halve(fourth_sum_kernel, both, 112, 64, "x", cross)
     both = halve(fifth_sum_kernel, both, 64, 48, "zh", cross)
     part_u, part_v, whole_bias = call(
         last_kernel,

time: 87.8 us -> 80.8 us (0.920)
  the two profiles are of different devices: /device:TPU:40 before, /device:TPU:64 now
where the time goes in v3:
time: 80.8 us; the launch traced here: 80.4 us
  starting transfers between devices  40.1 us (50%)
  Pallas kernels  23.3 us (29%)
  waiting for transfers between devices  15.2 us (19%)
  local copies, waits for them, and re-layouts  0.99 us (1%)
  between operations  0.83 us (1%)
    pallas_call x11, Pallas kernels, call(): pl.pallas_call(kernel, out_shape=tuple((jax.ShapeDtypeStruct(s, d) for _,...  23.3 us
    ppermute x4, waiting for transfers between devices, halve(): return (kept, lax.ppermute(sent, axis, pairs))  12.1 us
    ppermute x6, starting transfers between devices, shifted(): lax.ppermute(m, axis, [(i, (i + s) % 4) for i in range(4)])  11.4 us
    all_to_all x1, starting transfers between devices, shards(): gathered = lax.all_to_all(payload, REP, 0, 0, tiled=True)  11.2 us
    ppermute x4, starting transfers between devices, halve(): return (kept, lax.ppermute(sent, axis, pairs))  9.69 us
    all_to_all x1, starting transfers between devices, shards(): lax.all_to_all(outgoing, TABLE, 0, 0, tiled=True).reshape(SAMP, EMB)  3.58 us
    all_to_all x1, waiting for transfers between devices, shards(): lax.all_to_all(outgoing, TABLE, 0, 0, tiled=True).reshape(SAMP, EMB)  2.66 us
    ppermute x1, starting transfers between devices, shards(): v_got = lax.ppermute(v_send, 'zl', swap)  2 us
  transfers between devices with their start and end apart: 17, of which 5 were waited for; matrix products, arithmetic and copies ran while one was open for 0% of the time, Pallas kernels for 17%

profile of v3, /device:TPU:64, one launch (start us, length us, event | category | flops | bytes accessed | tf_op | source)
XLA Modules:
  0.0 80.4 jit_solution(8678587608678775300)
XLA Ops:
  0.7 0.5 collective-permute-start
  1.3 2.9 %shard_map.111 = (f32[8,2048]{1,0:T(8,128)}, bf16[16,16,128]{2,1,0:T(8,128)(2,1)}) custom-call(s32[1,2048]{1,0:T(1,128)} %bitcast.13, s32[2,2048]{1,0:T(2,128)} %bitcast.11), custom_call_target="tpu_custom_call" | custom-call | flops 2000000000 | bytes 2000000 | tf_op jit(solution)/shard_map/pallas_call | solution.py:367
  4.3 0.6 copy-done.6
  4.9 0.2 copy-done.5
  5.1 0.2 copy-done.4
  5.3 7.2 %shard_map.112 = (bf16[288,384]{1,0:T(8,128)(2,1)}, bf16[288,384]{1,0:T(8,128)(2,1)}, bf16[288,384]{1,0:T(8,128)(2,1)}, bf16[288,384]{1,0:T(8,128)(2,1)}, bf16[5...) custom-call(s32[1]{0:T(128)} %bitcast.place_ref._, ...), custom_call_target="tpu_custom_call" | custom-call | flops 6000000000 | bytes 6000000 | tf_op jit(solution)/shard_map/pallas_call | solution.py:367
  12.5 2.0 %collective-permute-start.6 = (bf16[544,384]{1,0:T(8,128)(2,1)}, bf16[544,384]{1,0:T(8,128)(2,1)S(1)}, u32[]{:S(2)}, u32[]{:S(2)}) collective-permute-start(bf16[544,384]{1,0:T(8,128)(2,1)} %get-tuple-element.37), channel_id=1, source_target_pairs={{0,8},{8,0},{1,9},{9,1},{2,10},{10,2},{3,11},{11,3},{4,12},{12,4},... | collective-permute-start | bytes 1253384 | tf_op jit(solution)/shard_map/ppermute | solution.py:430
  14.5 1.6 %collective-permute-start.3 = (bf16[288,384]{1,0:T(8,128)(2,1)}, bf16[288,384]{1,0:T(8,128)(2,1)S(1)}, u32[]{:S(2)}, u32[]{:S(2)}) collective-permute-start(bf16[288,384]{1,0:T(8,128)(2,1)} %get-tuple-element.33), channel_id=1, source_target_pairs={{0,2},{2,4},{4,6},{6,0},{1,3},{3,5},{5,7},{7,1},{8,10},{10,12},{12... | collective-permute-start | bytes 663560 | tf_op jit(solution)/shard_map/ppermute | solution.py:385
  16.0 2.9 %collective-permute-start.4 = (bf16[288,384]{1,0:T(8,128)(2,1)}, bf16[288,384]{1,0:T(8,128)(2,1)S(1)}, u32[]{:S(2)}, u32[]{:S(2)}) collective-permute-start(bf16[288,384]{1,0:T(8,128)(2,1)} %get-tuple-element.34), channel_id=1, source_target_pairs={{0,4},{2,6},{4,0},{6,2},{1,5},{3,7},{5,1},{7,3},{8,12},{10,14},{12... | collective-permute-start | bytes 663560 | tf_op jit(solution)/shard_map/ppermute | solution.py:385
  18.9 1.4 %collective-permute-start.5 = (bf16[288,384]{1,0:T(8,128)(2,1)}, bf16[288,384]{1,0:T(8,128)(2,1)S(1)}, u32[]{:S(2)}, u32[]{:S(2)}) collective-permute-start(bf16[288,384]{1,0:T(8,128)(2,1)} %get-tuple-element.35), channel_id=1, source_target_pairs={{0,6},{2,0},{4,2},{6,4},{1,7},{3,1},{5,3},{7,5},{8,14},{10,8},{12,... | collective-permute-start | bytes 663560 | tf_op jit(solution)/shard_map/ppermute | solution.py:385
  20.3 5.0 %shard_map.114 = bf16[16,128,128]{2,1,0:T(8,128)(2,1)} custom-call(bf16[128,384]{1,0:T(8,128)(2,1)} %get-tuple-element.44.lat_ref, bf16[128,384]{1,0:T(8,128)(2,1)} %get-tuple-element.45.gl_ref, bf16[128,2176]{1,0:T(8,128)(2,1)} %cot_hbm.3, bf16[2176,384]{1,0:T(8,128)(2,1)} %v_hbm.3, bf16[384,2176]{1,0:T(8,128)(2,1)} %u_hbm.3, f32[17,128]{1,0:T(8,128)} %bitcast.12), custom_call_target="tpu_custom_call" | custom-call | flops 4000000000 | bytes 4000000 | tf_op jit(solution)/shard_map/pallas_call | solution.py:367
  25.3 3.6 %all-to-all-start = ((bf16[16,128,128]{2,1,0:T(8,128)(2,1)}), bf16[16,128,128]{2,1,0:T(8,128)(2,1)S(1)}, u32[]{:S(2)}, u32[]{:S(2)}) async-start(bf16[16,128,128]{2,1,0:T(8,128)(2,1)} %shard_map.114), calls=%async_computation | async-start | bytes 1048576 | tf_op jit(solution)/shard_map/all_to_all | solution.py:428
  28.9 0.4 collective-permute-done.4.m2
  29.4 1.0 %shard_map.113 = (f32[160,384]{1,0:T(8,128)S(1)}, bf16[160,384]{1,0:T(8,128)(2,1)S(1)}, f32[144,384]{1,0:T(8,128)S(1)}, bf16[144,384]{1,0:T(8,128)(2,1)S(1)}, bf...) custom-call(s32[1]{0:T(128)} %bitcast.place_ref._, bf16[288,384]{1,0:T(8,128)(2,1)S(1)} %copy-done.3, ...), custom_call_target="tpu_custom_call" | custom-call | flops 99999997952 | bytes 100000000 | tf_op jit(solution)/shard_map/pallas_call | solution.py:367
  30.4 1.5 %collective-permute-start.8 = (bf16[144,384]{1,0:T(8,128)(2,1)S(1)}, bf16[144,384]{1,0:T(8,128)(2,1)S(1)}, u32[]{:S(2)}, u32[]{:S(2)}) collective-permute-start(bf16[144,384]{1,0:T(8,128)(2,1)S(1)} %get-tuple-element.41), channel_id=1, source_target_pairs={{0,2},{2,4},{4,6},{6,0},{1,3},{3,5},{5,7},{7,1},{8,10},{10,12},{12... | collective-permute-start | bytes 331784 | tf_op jit(solution)/shard_map/ppermute | solution.py:385
  31.9 2.7 %collective-permute-start.9 = (bf16[144,384]{1,0:T(8,128)(2,1)S(1)}, bf16[144,384]{1,0:T(8,128)(2,1)S(1)}, u32[]{:S(2)}, u32[]{:S(2)}) collective-permute-start(bf16[144,384]{1,0:T(8,128)(2,1)S(1)} %get-tuple-element.42), channel_id=1, source_target_pairs={{0,4},{2,6},{4,0},{6,2},{1,5},{3,7},{5,1},{7,3},{8,12},{10,14},{12... | collective-permute-start | bytes 331784 | tf_op jit(solution)/shard_map/ppermute | solution.py:385
  34.6 1.4 %collective-permute-start.10 = (bf16[144,384]{1,0:T(8,128)(2,1)S(1)}, bf16[144,384]{1,0:T(8,128)(2,1)S(1)}, u32[]{:S(2)}, u32[]{:S(2)}) collective-permute-start(bf16[144,384]{1,0:T(8,128)(2,1)S(1)} %get-tuple-element.43), channel_id=1, source_target_pairs={{0,6},{2,0},{4,2},{6,4},{1,7},{3,1},{5,3},{7,5},{8,14},{10,8},{12,... | collective-permute-start | bytes 331784 | tf_op jit(solution)/shard_map/ppermute | solution.py:385
  36.0 1.5 %collective-permute-start.7 = (bf16[160,384]{1,0:T(8,128)(2,1)S(1)}, bf16[160,384]{1,0:T(8,128)(2,1)S(1)}, u32[]{:S(2)}, u32[]{:S(2)}) collective-permute-start(bf16[160,384]{1,0:T(8,128)(2,1)S(1)} %get-tuple-element.39), channel_id=1, source_target_pairs={{0,8},{8,0},{1,9},{9,1},{2,10},{10,2},{3,11},{11,3},{4,12},{12,4},... | collective-permute-start | bytes 368648 | tf_op jit(solution)/shard_map/ppermute | solution.py:448
  37.5 2.7 %all-to-all-done = bf16[16,128,128]{2,1,0:T(8,128)(2,1)S(1)} async-done(((bf16[16,128,128]{2,1,0:T(8,128)(2,1)}), bf16[16,128,128]{2,1,0:T(8,128)(2,1)S(1)}, u32[]{:S(2)}, u32[]{:S(2)}) %all-to-all-start) | async-done | bytes 524320 | tf_op jit(solution)/shard_map/all_to_all | solution.py:428
  40.2 3.7 %shard_map.115._ = bf16[16,176,128]{2,1,0:T(8,128)(2,1)} custom-call(f32[8,2048]{1,0:T(8,128)S(1)} %copy-done.1, bf16[2048,128]{1,0:T(8,128)(2,1)S(1)} %bitcast.10, bf16[16,16,128]{2,1,0:T(8,128)(2,1)S(1)} %copy-done.2, f32[160,384]{1,0:T(8,128)S(1)} %get-tuple-element.38._.u_keep), custom_call_target="tpu_custom_call" | custom-call | flops 7000000000 | bytes 7000000 | tf_op jit(solution)/shard_map/pallas_call | solution.py:367
  43.9 0.5 shard_map.116
  44.6 11.2 %all-to-all-start.1 = ((bf16[16,176,128]{2,1,0:T(8,128)(2,1)}), bf16[16,176,128]{2,1,0:T(8,128)(2,1)S(1)}, u32[]{:S(2)}, u32[]{:S(2)}) async-start(bf16[16,176,128]{2,1,0:T(8,128)(2,1)} %shard_map.115._), calls=%async_computation.1 | async-start | bytes 1441792 | tf_op jit(solution)/shard_map/all_to_all | solution.py:464
  55.7 0.2 shard_map.117
  55.9 1.6 %collective-permute-start.12 = (bf16[112,384]{1,0:T(8,128)(2,1)S(1)}, bf16[112,384]{1,0:T(8,128)(2,1)S(1)}, u32[]{:S(2)}, u32[]{:S(2)}) collective-permute-start(bf16[112,384]{1,0:T(8,128)(2,1)S(1)} %get-tuple-element.50), channel_id=1, source_target_pairs={{0,16},{16,0},{32,48},{48,32},{1,17},{17,1},{33,49},{49,33},{2,18}... | collective-permute-start | bytes 258056 | tf_op jit(solution)/shard_map/ppermute | solution.py:461
  57.4 6.3 %collective-permute-done.12.got = bf16[112,384]{1,0:T(8,128)(2,1)S(1)} collective-permute-done((bf16[112,384]{1,0:T(8,128)(2,1)S(1)}, bf16[112,384]{1,0:T(8,128)(2,1)S(1)}, u32[]{:S(2)}, u32[]{:S(2)}) %collective-permute-start.12) | collective-permute-done | bytes 86048 | tf_op jit(solution)/shard_map/ppermute | solution.py:461
  63.8 0.1 shard_map.118
  63.9 2.0 %collective-permute-start.13 = (bf16[64,384]{1,0:T(8,128)(2,1)S(1)}, bf16[64,384]{1,0:T(8,128)(2,1)S(1)}, u32[]{:S(2)}, u32[]{:S(2)}) collective-permute-start(bf16[64,384]{1,0:T(8,128)(2,1)S(1)} %get-tuple-element.52), channel_id=1, source_target_pairs={{0,48},{48,0},{16,32},{32,16},{1,49},{49,1},{17,33},{33,17},{2,50}... | collective-permute-start | bytes 147464 | tf_op jit(solution)/shard_map/ppermute | solution.py:461
  65.9 3.8 %collective-permute-done.13.got = bf16[64,384]{1,0:T(8,128)(2,1)S(1)} collective-permute-done((bf16[64,384]{1,0:T(8,128)(2,1)S(1)}, bf16[64,384]{1,0:T(8,128)(2,1)S(1)}, u32[]{:S(2)}, u32[]{:S(2)}) %collective-permute-start.13) | collective-permute-done | bytes 49184 | tf_op jit(solution)/shard_map/ppermute | solution.py:461
  69.8 6.0 %collective-permute-start.14 = (bf16[48,384]{1,0:T(8,128)(2,1)S(1)}, bf16[48,384]{1,0:T(8,128)(2,1)S(1)}, u32[]{:S(2)}, u32[]{:S(2)}) collective-permute-start(bf16[48,384]{1,0:T(8,128)(2,1)S(1)} %get-tuple-element.54), channel_id=1, source_target_pairs={{0,192},{192,0},{64,128},{128,64},{1,193},{193,1},{65,129},{129,65... | collective-permute-start | bytes 110600 | tf_op jit(solution)/shard_map/ppermute | solution.py:461
  75.9 1.9 %collective-permute-done.14.got = bf16[48,384]{1,0:T(8,128)(2,1)S(1)} collective-permute-done((bf16[48,384]{1,0:T(8,128)(2,1)S(1)}, bf16[48,384]{1,0:T(8,128)(2,1)S(1)}, u32[]{:S(2)}, u32[]{:S(2)}) %collective-permute-start.14) | collective-permute-done | bytes 36896 | tf_op jit(solution)/shard_map/ppermute | solution.py:461
  77.8 0.7 shard_map.120
  78.5 1.9 %shard_map.121 = f32[512,128]{1,0:T(8,128)} custom-call(bf16[16,176,128]{2,1,0:T(8,128)(2,1)S(1)} %all-to-all-done.1.got_ref), custom_call_target="tpu_custom_call" | custom-call | flops 2000000000 | bytes 2000000 | tf_op jit(solution)/shard_map/pallas_call | solution.py:367
  (27 shorter events, 0.4 us)
Async XLA Ops:
  0.6 3.7 %collective-permute-start.2 = (bf16[128,2176]{1,0:T(8,128)(2,1)}, bf16[128,2176]{1,0:T(8,128)(2,1)S(1)}, u32[]{:S(2)}, u32[]{:S(2)}) collective-permute-start(bf16[128,2176]{1,0:T(8,128)(2,1)} %cot_hbm.3), channel_id=1, source_target_pairs={{0,1},{1,0},{2,3},{3,2},{4,5},{5,4},{6,7},{7,6},{8,9},{9,8},{10,11... | collective-permute-start | bytes 1671176 | tf_op jit(solution)/shard_map/ppermute | solution.py:392
  0.7 3.5 %collective-permute-start = (bf16[128,2048]{1,0:T(8,128)(2,1)}, bf16[128,2048]{1,0:T(8,128)(2,1)S(1)}, u32[]{:S(2)}, u32[]{:S(2)}) collective-permute-start(bf16[128,2048]{1,0:T(8,128)(2,1)} %pooled_hbm.1), channel_id=1, source_target_pairs={{0,1},{1,0},{2,3},{3,2},{4,5},{5,4},{6,7},{7,6},{8,9},{9,8},{10,11... | collective-permute-start | bytes 1572872 | tf_op jit(solution)/shard_map/ppermute | solution.py:392
  1.2 3.0 %collective-permute-start.1 = (bf16[128,128]{1,0:T(8,128)(2,1)}, bf16[128,128]{1,0:T(8,128)(2,1)S(1)}, u32[]{:S(2)}, u32[]{:S(2)}) collective-permute-start(bf16[128,128]{1,0:T(8,128)(2,1)} %dense_hbm.1), channel_id=1, source_target_pairs={{0,1},{1,0},{2,3},{3,2},{4,5},{5,4},{6,7},{7,6},{8,9},{9,8},{10,11... | collective-permute-start | bytes 98312 | tf_op jit(solution)/shard_map/ppermute | solution.py:392
  4.3 0.6 copy-start.6
  4.3 0.8 %copy-start.5 = (bf16[128,2048]{1,0:T(8,128)(2,1)}, bf16[128,2048]{1,0:T(8,128)(2,1)S(1)}, u32[]{:S(2)}) copy-start(bf16[128,2048]{1,0:T(8,128)(2,1)S(1)} %collective-permute-done.pooled2_hbm) | copy-start | bytes 1572868
  4.3 1.0 %copy-start.4 = (bf16[128,2176]{1,0:T(8,128)(2,1)}, bf16[128,2176]{1,0:T(8,128)(2,1)S(1)}, u32[]{:S(2)}) copy-start(bf16[128,2176]{1,0:T(8,128)(2,1)S(1)} %collective-permute-done.2.cot2_hbm) | copy-start | bytes 1671172
  12.5 16.9 %collective-permute-start.6 = (bf16[544,384]{1,0:T(8,128)(2,1)}, bf16[544,384]{1,0:T(8,128)(2,1)S(1)}, u32[]{:S(2)}, u32[]{:S(2)}) collective-permute-start(bf16[544,384]{1,0:T(8,128)(2,1)} %get-tuple-element.37), channel_id=1, source_target_pairs={{0,8},{8,0},{1,9},{9,1},{2,10},{10,2},{3,11},{11,3},{4,12},{12,4},... | collective-permute-start | bytes 1253384 | tf_op jit(solution)/shard_map/ppermute | solution.py:430
  14.5 14.4 %collective-permute-start.3 = (bf16[288,384]{1,0:T(8,128)(2,1)}, bf16[288,384]{1,0:T(8,128)(2,1)S(1)}, u32[]{:S(2)}, u32[]{:S(2)}) collective-permute-start(bf16[288,384]{1,0:T(8,128)(2,1)} %get-tuple-element.33), channel_id=1, source_target_pairs={{0,2},{2,4},{4,6},{6,0},{1,3},{3,5},{5,7},{7,1},{8,10},{10,12},{12... | collective-permute-start | bytes 663560 | tf_op jit(solution)/shard_map/ppermute | solution.py:385
  16.0 13.3 %collective-permute-start.4 = (bf16[288,384]{1,0:T(8,128)(2,1)}, bf16[288,384]{1,0:T(8,128)(2,1)S(1)}, u32[]{:S(2)}, u32[]{:S(2)}) collective-permute-start(bf16[288,384]{1,0:T(8,128)(2,1)} %get-tuple-element.34), channel_id=1, source_target_pairs={{0,4},{2,6},{4,0},{6,2},{1,5},{3,7},{5,1},{7,3},{8,12},{10,14},{12... | collective-permute-start | bytes 663560 | tf_op jit(solution)/shard_map/ppermute | solution.py:385
  18.9 10.4 %collective-permute-start.5 = (bf16[288,384]{1,0:T(8,128)(2,1)}, bf16[288,384]{1,0:T(8,128)(2,1)S(1)}, u32[]{:S(2)}, u32[]{:S(2)}) collective-permute-start(bf16[288,384]{1,0:T(8,128)(2,1)} %get-tuple-element.35), channel_id=1, source_target_pairs={{0,6},{2,0},{4,2},{6,4},{1,7},{3,1},{5,3},{7,5},{8,14},{10,8},{12,... | collective-permute-start | bytes 663560 | tf_op jit(solution)/shard_map/ppermute | solution.py:385
  20.3 9.1 %copy-start = (bf16[544,384]{1,0:T(8,128)(2,1)S(1)}, bf16[544,384]{1,0:T(8,128)(2,1)}, u32[]{:S(2)}) copy-start(bf16[544,384]{1,0:T(8,128)(2,1)} %get-tuple-element.36.v_own) | copy-start | bytes 1253380
  20.3 9.1 %copy-start.3 = (bf16[288,384]{1,0:T(8,128)(2,1)S(1)}, bf16[288,384]{1,0:T(8,128)(2,1)}, u32[]{:S(2)}) copy-start(bf16[288,384]{1,0:T(8,128)(2,1)} %get-tuple-element.32.m0) | copy-start | bytes 663556
  25.3 14.9 %all-to-all-start = ((bf16[16,128,128]{2,1,0:T(8,128)(2,1)}), bf16[16,128,128]{2,1,0:T(8,128)(2,1)S(1)}, u32[]{:S(2)}, u32[]{:S(2)}) async-start(bf16[16,128,128]{2,1,0:T(8,128)(2,1)} %shard_map.114), calls=%async_computation | async-start | bytes 1048576 | tf_op jit(solution)/shard_map/all_to_all | solution.py:428
  29.4 10.8 %copy-start.1 = (f32[8,2048]{1,0:T(8,128)S(1)}, f32[8,2048]{1,0:T(8,128)}, u32[]{:S(2)}) copy-start(f32[8,2048]{1,0:T(8,128)} %get-tuple-element.31._.found_ref) | copy-start | bytes 196612
  29.4 10.8 %copy-start.2 = (bf16[16,16,128]{2,1,0:T(8,128)(2,1)S(1)}, bf16[16,16,128]{2,1,0:T(8,128)(2,1)}, u32[]{:S(2)}) copy-start(bf16[16,16,128]{2,1,0:T(8,128)(2,1)} %get-tuple-element.46.pos_ref) | copy-start | bytes 196612
  30.4 13.5 %collective-permute-start.8 = (bf16[144,384]{1,0:T(8,128)(2,1)S(1)}, bf16[144,384]{1,0:T(8,128)(2,1)S(1)}, u32[]{:S(2)}, u32[]{:S(2)}) collective-permute-start(bf16[144,384]{1,0:T(8,128)(2,1)S(1)} %get-tuple-element.41), channel_id=1, source_target_pairs={{0,2},{2,4},{4,6},{6,0},{1,3},{3,5},{5,7},{7,1},{8,10},{10,12},{12... | collective-permute-start | bytes 331784 | tf_op jit(solution)/shard_map/ppermute | solution.py:385
  31.9 12.0 %collective-permute-start.9 = (bf16[144,384]{1,0:T(8,128)(2,1)S(1)}, bf16[144,384]{1,0:T(8,128)(2,1)S(1)}, u32[]{:S(2)}, u32[]{:S(2)}) collective-permute-start(bf16[144,384]{1,0:T(8,128)(2,1)S(1)} %get-tuple-element.42), channel_id=1, source_target_pairs={{0,4},{2,6},{4,0},{6,2},{1,5},{3,7},{5,1},{7,3},{8,12},{10,14},{12... | collective-permute-start | bytes 331784 | tf_op jit(solution)/shard_map/ppermute | solution.py:385
  34.6 9.3 %collective-permute-start.10 = (bf16[144,384]{1,0:T(8,128)(2,1)S(1)}, bf16[144,384]{1,0:T(8,128)(2,1)S(1)}, u32[]{:S(2)}, u32[]{:S(2)}) collective-permute-start(bf16[144,384]{1,0:T(8,128)(2,1)S(1)} %get-tuple-element.43), channel_id=1, source_target_pairs={{0,6},{2,0},{4,2},{6,4},{1,7},{3,1},{5,3},{7,5},{8,14},{10,8},{12,... | collective-permute-start | bytes 331784 | tf_op jit(solution)/shard_map/ppermute | solution.py:385
  36.0 7.9 %collective-permute-start.7 = (bf16[160,384]{1,0:T(8,128)(2,1)S(1)}, bf16[160,384]{1,0:T(8,128)(2,1)S(1)}, u32[]{:S(2)}, u32[]{:S(2)}) collective-permute-start(bf16[160,384]{1,0:T(8,128)(2,1)S(1)} %get-tuple-element.39), channel_id=1, source_target_pairs={{0,8},{8,0},{1,9},{9,1},{2,10},{10,2},{3,11},{11,3},{4,12},{12,4},... | collective-permute-start | bytes 368648 | tf_op jit(solution)/shard_map/ppermute | solution.py:448
  44.5 11.3 %collective-permute-start.11 = (bf16[208,384]{1,0:T(8,128)(2,1)S(1)}, bf16[208,384]{1,0:T(8,128)(2,1)S(1)}, u32[]{:S(2)}, u32[]{:S(2)}) collective-permute-start(bf16[208,384]{1,0:T(8,128)(2,1)S(1)} %get-tuple-element.48), channel_id=1, source_target_pairs={{0,64},{64,0},{128,192},{192,128},{1,65},{65,1},{129,193},{193,129... | collective-permute-start | bytes 479240 | tf_op jit(solution)/shard_map/ppermute | solution.py:461
  44.6 33.9 %all-to-all-start.1 = ((bf16[16,176,128]{2,1,0:T(8,128)(2,1)}), bf16[16,176,128]{2,1,0:T(8,128)(2,1)S(1)}, u32[]{:S(2)}, u32[]{:S(2)}) async-start(bf16[16,176,128]{2,1,0:T(8,128)(2,1)} %shard_map.115._), calls=%async_computation.1 | async-start | bytes 1441792 | tf_op jit(solution)/shard_map/all_to_all | solution.py:464
  55.9 7.9 %collective-permute-start.12 = (bf16[112,384]{1,0:T(8,128)(2,1)S(1)}, bf16[112,384]{1,0:T(8,128)(2,1)S(1)}, u32[]{:S(2)}, u32[]{:S(2)}) collective-permute-start(bf16[112,384]{1,0:T(8,128)(2,1)S(1)} %get-tuple-element.50), channel_id=1, source_target_pairs={{0,16},{16,0},{32,48},{48,32},{1,17},{17,1},{33,49},{49,33},{2,18}... | collective-permute-start | bytes 258056 | tf_op jit(solution)/shard_map/ppermute | solution.py:461
  63.9 5.9 %collective-permute-start.13 = (bf16[64,384]{1,0:T(8,128)(2,1)S(1)}, bf16[64,384]{1,0:T(8,128)(2,1)S(1)}, u32[]{:S(2)}, u32[]{:S(2)}) collective-permute-start(bf16[64,384]{1,0:T(8,128)(2,1)S(1)} %get-tuple-element.52), channel_id=1, source_target_pairs={{0,48},{48,0},{16,32},{32,16},{1,49},{49,1},{17,33},{33,17},{2,50}... | collective-permute-start | bytes 147464 | tf_op jit(solution)/shard_map/ppermute | solution.py:461
  69.8 7.9 %collective-permute-start.14 = (bf16[48,384]{1,0:T(8,128)(2,1)S(1)}, bf16[48,384]{1,0:T(8,128)(2,1)S(1)}, u32[]{:S(2)}, u32[]{:S(2)}) collective-permute-start(bf16[48,384]{1,0:T(8,128)(2,1)S(1)} %get-tuple-element.54), channel_id=1, source_target_pairs={{0,192},{192,0},{64,128},{128,64},{1,193},{193,1},{65,129},{129,65... | collective-permute-start | bytes 110600 | tf_op jit(solution)/shard_map/ppermute | solution.py:461

commit v4 on v3

--- a/solution.py
+++ b/solution.py
@@ -62,57 +62,18 @@
     return (a.astype(F32) * b.astype(F32)).astype(BF)
 
 
-def pooled_kernel(
-    lat_ref, gl_ref, cot_hbm, v_hbm, u_hbm, bias_hbm, out_hbm,
-    cot_ref, v_ref, u_ref, bias_ref, out_ref, sems, v_sems, u_sems, out_sems,
-):
-    loads = [
-        pltpu.make_async_copy(cot_hbm, cot_ref, sems.at[0]),
-        pltpu.make_async_copy(bias_hbm, bias_ref, sems.at[1]),
-    ]
-    parts = []
-    for j in range(4):
-        cols = slice(EMB + j * 512, EMB + (j + 1) * 512)
-        parts.append(
-            (
-                pltpu.make_async_copy(u_hbm.at[:, cols], u_ref.at[:, cols], u_sems.at[j]),
-                pltpu.make_async_copy(v_hbm.at[cols, :], v_ref.at[cols, :], v_sems.at[j]),
-            )
-        )
-    for copy in (*parts[0], *loads, *parts[1], *parts[2], *parts[3]):
-        copy.start()
-    latent, grad_latent = lat_ref[...], gl_ref[...]
-    for load in loads:
-        load.wait()
-    stores = []
-    for t in range(N_TAB):
-        if t % 4 == 0:
-            for part in parts[t // 4]:
-                part.wait()
-        cols = slice(EMB + t * EMB, EMB + (t + 1) * EMB)
-        mixing = nn(latent, u_ref[:, cols]) + bias_ref[t + 1 : t + 2, :]
-        backward = nt(grad_latent, v_ref[cols, :])
-        out_ref[t] = (cot_ref[:, cols].astype(F32) * (mixing + 1.0) + backward).astype(BF)
-        if t % 4 == 3:
-            some = slice(t - 3, t + 1)
-            store = pltpu.make_async_copy(out_ref.at[some], out_hbm.at[some], out_sems.at[t // 4])
-            store.start()
-            stores.append(store)
-    for store in stores:
-        store.wait()
-
-
 def weight_kernel(
-    place_ref, pooled_hbm, pooled2_hbm, dense_hbm, dense2_hbm, v_hbm, cot_hbm, cot2_hbm, u_hbm, _,
-    u0, u1, u2, u3, v_keep, v_send, lat_ref, gl_ref,
+    place_ref, pooled_hbm, pooled2_hbm, dense_hbm, dense2_hbm, v_hbm, cot_hbm, cot2_hbm, u_hbm, bias_hbm, _,
+    u0, u1, u2, u3, v_keep, v_send, out_hbm,
     pooled_ref, dense_ref, cot_ref, mix_ref, v_ref, u_ref,
-    gu, gv, bias_row, bu0, bu1, bu2, bu3, bk, bs, load_sems, sems,
+    gu, gv, bias_row, bu0, bu1, bu2, bu3, bk, bs, bias_ref, out_ref, load_sems, sems, out_sems,
 ):
     own, other = slice(0, 128), slice(128, 256)
     pairs = (
         (pooled_hbm, pooled_ref.at[own, :]), (pooled2_hbm, pooled_ref.at[other, :]),
         (dense_hbm, dense_ref.at[own, :]), (dense2_hbm, dense_ref.at[other, :]),
         (v_hbm, v_ref), (cot_hbm, cot_ref.at[own, :]), (cot2_hbm, cot_ref.at[other, :]), (u_hbm, u_ref),
+        (bias_hbm, bias_ref),
     )
     loads = [pltpu.make_async_copy(src, dst, load_sems.at[i]) for i, (src, dst) in enumerate(pairs)]
     for load in loads:
@@ -124,10 +85,9 @@
         load.wait()
     mix_ref[:, :EMB] = times(cot_ref[:, :EMB], dense_ref[...])
     mix_ref[:, EMB:] = times(cot_ref[:, EMB:], pooled_ref[...])
-    loads[7].wait()
+    for load in loads[7:]:
+        load.wait()
     gl = nt(mix_ref[...], u_ref[...]).astype(BF)
-    lat_ref[...] = lat[0:128, :]
-    gl_ref[...] = gl[0:128, :]
     for j in range(D0 // EMB):
         cols = slice(j * EMB, (j + 1) * EMB)
         mix = mix_ref[:, cols]
@@ -166,6 +126,17 @@
             pair = jnp.concatenate([block(gv, half, 2 * i), block(gv, half, 2 * i + 1)], axis=0)
             buffer[i * 272 : (i + 1) * 272, :] = pair.astype(BF)
         leave(buffer, out)
+    latent, grad_latent = lat[0:128, :], gl[0:128, :]
+    for t in range(N_TAB):
+        cols = slice(EMB + t * EMB, EMB + (t + 1) * EMB)
+        mixing = nn(latent, u_ref[:, cols]) + bias_ref[t + 1 : t + 2, :]
+        backward = nt(grad_latent, v_ref[cols, :])
+        out_ref[t] = (cot_ref[0:128, cols].astype(F32) * (mixing + 1.0) + backward).astype(BF)
+        if t % 4 == 3:
+            some = slice(t - 3, t + 1)
+            copy = pltpu.make_async_copy(out_ref.at[some], out_hbm.at[some], out_sems.at[t // 4])
+            copy.start()
+            copies.append(copy)
     for copy in copies:
         copy.wait()
 
@@ -177,34 +148,26 @@
     return jnp.concatenate([high, low, jnp.zeros((4, LAT), F32)], axis=0)
 
 
-def first_sum_kernel(
-    place_ref, m0, m1, m2, m3, v_own, v_got, u_keep, u_send, v0, v1, v2, v3,
-    acc_u, acc_v, bs, b1, b2, b3, sems,
-):
-    acc_u[...] = (m0[...].astype(F32) + m1[...].astype(F32)) + (m2[...].astype(F32) + m3[...].astype(F32))
-    acc_v[...] = v_own[...].astype(F32) + v_got[...].astype(F32)
-    _, _, zl, y, _ = coords(place_ref)
-    bias = bias_again(acc_u[272:288, :])
-    gap = jnp.zeros((8, LAT), F32)
+def first_u_kernel(place_ref, m0, m1, m2, m3, _, keep_ref, send_ref, acc, buffer, sem):
+    acc[...] = (m0[...].astype(F32) + m1[...].astype(F32)) + (m2[...].astype(F32) + m3[...].astype(F32))
+    _, _, zl, _, _ = coords(place_ref)
+    rest = [jnp.zeros((8, LAT), F32), bias_again(acc[272:288, :])]
+    kept = pick(acc, [zl * FEAT], FEAT) + rest
+    split(keep_ref, send_ref, buffer, sem, kept, pick(acc, [(1 - zl) * FEAT], FEAT) + rest)
+
+
+def first_v_kernel(place_ref, own, got, v0, v1, v2, v3, acc, b1, b2, b3, sems):
+    acc[...] = own[...].astype(F32) + got[...].astype(F32)
+    _, _, _, y, _ = coords(place_ref)
+    gap = [jnp.zeros((8, LAT), F32)]
     copies = []
-
-    def leave(buffer, out):
-        copy = pltpu.make_async_copy(buffer, out, sems.at[len(copies)])
+    for s, buffer, out in ((1, b1, v1), (2, b2, v2), (3, b3, v3)):
+        block = pick(acc, [lax.rem(y + s, 4) * FEAT], FEAT)
+        buffer[...] = jnp.concatenate(block + gap, axis=0).astype(BF)
+        copy = pltpu.make_async_copy(buffer, out, sems.at[s])
         copy.start()
         copies.append(copy)
-
-    bs[...] = jnp.concatenate(
-        [acc_u[pl.ds(pl.multiple_of((1 - zl) * FEAT, 8), FEAT), :], gap, bias], axis=0
-    ).astype(BF)
-    leave(bs, u_send)
-    for s, buffer, out in ((1, b1, v1), (2, b2, v2), (3, b3, v3)):
-        start = pl.multiple_of(lax.rem(y + s, 4) * FEAT, 8)
-        buffer[...] = jnp.concatenate([acc_v[pl.ds(start, FEAT), :], gap], axis=0).astype(BF)
-        leave(buffer, out)
-    u_keep[...] = jnp.concatenate(
-        [acc_u[pl.ds(pl.multiple_of(zl * FEAT, 8), FEAT), :], gap, bias], axis=0
-    )
-    v0[...] = jnp.concatenate([acc_v[pl.ds(pl.multiple_of(y * FEAT, 8), FEAT), :], gap], axis=0)
+    v0[...] = jnp.concatenate(pick(acc, [y * FEAT], FEAT) + gap, axis=0)
     for copy in copies:
         copy.wait()
 
@@ -398,44 +361,40 @@
         near(uniq_rows.reshape(1, UNIQ), lookup_slot.reshape(SAMP, 2).T),
         mib=56,
     )
-    u_shape, v_shape, lat_shape = (288, LAT), (544, LAT), (128, LAT)
-    u0, u1, u2, u3, v_keep, v_send, latent, grad_latent = call(
+    u_shape, v_shape = (288, LAT), (544, LAT)
+    bias_rows, out_shape = (D0 // 128, 128), (N_TAB, 128, EMB)
+    loaded = (pooled, pooled2, dense, dense2, proj_v, cot, cot2, proj_u, bias.reshape(bias_rows))
+    u0, u1, u2, u3, v_keep, v_send, outgoing = call(
         weight_kernel,
-        [(HBM, u_shape, BF)] * 4 + [(HBM, v_shape, BF)] * 2 + [(VMEM, lat_shape, BF)] * 2,
-        [place] + [(HBM, a) for a in (pooled, pooled2, dense, dense2, proj_v, cot, cot2, proj_u)]
-        + [(ANY, found)],
+        [(HBM, u_shape, BF)] * 4 + [(HBM, v_shape, BF)] * 2 + [(HBM, out_shape, BF)],
+        [place] + [(HBM, a) for a in loaded] + [(ANY, found)],
         [pltpu.VMEM((256, w), BF) for w in (D0 - EMB, EMB, D0, D0)]
         + [pltpu.VMEM((D0, LAT), BF), pltpu.VMEM((LAT, D0), BF)]
         + [pltpu.VMEM((D0, LAT), F32), pltpu.VMEM((D0, LAT), F32), pltpu.VMEM((1, D0), F32)]
         + [pltpu.VMEM(u_shape, BF)] * 4
         + [pltpu.VMEM(v_shape, BF)] * 2
-        + [dma((8,)), dma((6,))],
+        + [pltpu.VMEM(bias_rows, F32), pltpu.VMEM(out_shape, BF)]
+        + [dma((9,)), dma((6,)), dma((4,))],
         mib=56,
-        us=6,
-    )
-    bias_rows, out_shape = (D0 // 128, 128), (N_TAB, 128, EMB)
-    (outgoing,) = call(
-        pooled_kernel,
-        [(HBM, out_shape, BF)],
-        near(latent, grad_latent)
-        + [(HBM, a) for a in (cot, proj_v, proj_u, bias.reshape(bias_rows))],
-        [pltpu.VMEM((128, D0), BF), pltpu.VMEM((D0, LAT), BF), pltpu.VMEM((LAT, D0), BF)]
-        + [pltpu.VMEM(bias_rows, F32), pltpu.VMEM(out_shape, BF)]
-        + [dma((2,)), dma((4,)), dma((4,)), dma((4,))],
-        mib=56,
-        us=4,
+        us=8,
     )
     received = lax.all_to_all(outgoing, TABLE, 0, 0, tiled=True).reshape(SAMP, EMB)
     u_got = shifted([u1, u2, u3], "y")
     v_got = lax.ppermute(v_send, "zl", swap)
     u_shape, v_shape = (160, LAT), (144, LAT)
-    u_keep, u_send, v0, v1, v2, v3 = call(
-        first_sum_kernel,
-        [(VMEM, u_shape, F32), (HBM, u_shape, BF), (VMEM, v_shape, F32)] + [(HBM, v_shape, BF)] * 3,
-        [place] + near(u0, *u_got, v_keep, v_got),
-        [pltpu.VMEM((288, LAT), F32), pltpu.VMEM((544, LAT), F32), pltpu.VMEM(u_shape, BF)]
-        + [pltpu.VMEM(v_shape, BF)] * 3
-        + [dma((4,))],
+    v0, v1, v2, v3 = call(
+        first_v_kernel,
+        [(VMEM, v_shape, F32)] + [(HBM, v_shape, BF)] * 3,
+        [place] + near(v_keep, v_got),
+        [pltpu.VMEM((544, LAT), F32)] + [pltpu.VMEM(v_shape, BF)] * 3 + [dma((4,))],
+        us=2,
+    )
+    v_got = shifted([v1, v2, v3], "y")
+    u_keep, u_send = call(
+        first_u_kernel,
+        [(VMEM, u_shape, F32), (HBM, u_shape, BF)],
+        [place] + near(u0, *u_got) + [(ANY, v0)],
+        [pltpu.VMEM((288, LAT), F32), pltpu.VMEM(u_shape, BF), dma((1,))],
         us=100,
     )
     (payload,) = call(
@@ -446,7 +405,6 @@
         us=7,
     )
     u_got = lax.ppermute(u_send, "zl", swap)
-    v_got = shifted([v1, v2, v3], "y")
     flat = [(0, 1), (1, 0), (2, 3), (3, 2)]
     cross = [(0, 3), (3, 0), (1, 2), (2, 1)]
 

time: 80.8 us -> 77.1 us (0.954)
  the two profiles are of different devices: /device:TPU:64 before, /device:TPU:40 now
where the time goes in v4:
time: 77.1 us; the launch traced here: 76.7 us
  starting transfers between devices  39.6 us (51%)
  Pallas kernels  18.3 us (24%)
  waiting for transfers between devices  16 us (21%)
  local copies, waits for them, and re-layouts  1.99 us (3%)
  between operations  0.8 us (1%)
    pallas_call x11, Pallas kernels, call(): pl.pallas_call(kernel, out_shape=tuple((jax.ShapeDtypeStruct(s, d) for _,...  18.3 us
    ppermute x4, waiting for transfers between devices, halve(): return (kept, lax.ppermute(sent, axis, pairs))  13 us
    ppermute x4, starting transfers between devices, halve(): return (kept, lax.ppermute(sent, axis, pairs))  12 us
    ppermute x6, starting transfers between devices, shifted(): lax.ppermute(m, axis, [(i, (i + s) % 4) for i in range(4)])  9.92 us
    all_to_all x1, starting transfers between devices, shards(): gathered = lax.all_to_all(payload, REP, 0, 0, tiled=True)  8.88 us
    all_to_all x1, starting transfers between devices, shards(): lax.all_to_all(outgoing, TABLE, 0, 0, tiled=True).reshape(SAMP, EMB)  6.12 us
    unnamed x14, local copies, waits for them, and re-layouts  1.99 us
    ppermute x1, starting transfers between devices, shards(): u_got = lax.ppermute(u_send, 'zl', swap)  1.81 us
  transfers between devices with their start and end apart: 17, of which 7 were waited for; matrix products, arithmetic and copies ran while one was open for 0% of the time, Pallas kernels for 11%

profile of v4, /device:TPU:40, one launch (start us, length us, event | category | flops | bytes accessed | tf_op | source)
XLA Modules:
  0.0 76.7 jit_solution(5118772557402629558)
XLA Ops:
  0.7 0.5 collective-permute-start
  1.3 2.9 %shard_map.111 = (f32[8,2048]{1,0:T(8,128)}, bf16[16,16,128]{2,1,0:T(8,128)(2,1)}) custom-call(s32[1,2048]{1,0:T(1,128)} %bitcast.13, s32[2,2048]{1,0:T(2,128)} %bitcast.11), custom_call_target="tpu_custom_call" | custom-call | flops 2000000000 | bytes 2000000 | tf_op jit(solution)/shard_map/pallas_call | solution.py:330
  4.3 0.6 copy-done.6
  4.9 0.2 copy-done.5
  5.3 7.1 %shard_map.112 = (bf16[288,384]{1,0:T(8,128)(2,1)}, bf16[288,384]{1,0:T(8,128)(2,1)}, bf16[288,384]{1,0:T(8,128)(2,1)}, bf16[288,384]{1,0:T(8,128)(2,1)}, bf16[5...) custom-call(s32[1]{0:T(128)} %bitcast.place_ref._, bf16[128,2048]{1,0:T(8,128)(2,1)} %pooled_hbm.1, ...), custom_call_target="tpu_custom_call" | custom-call | flops 8000000000 | bytes 8000000 | tf_op jit(solution)/shard_map/pallas_call | solution.py:330
  12.6 1.6 %collective-permute-start.3 = (bf16[288,384]{1,0:T(8,128)(2,1)}, bf16[288,384]{1,0:T(8,128)(2,1)S(1)}, u32[]{:S(2)}, u32[]{:S(2)}) collective-permute-start(bf16[288,384]{1,0:T(8,128)(2,1)} %get-tuple-element.32), channel_id=1, source_target_pairs={{0,2},{2,4},{4,6},{6,0},{1,3},{3,5},{5,7},{7,1},{8,10},{10,12},{12... | collective-permute-start | bytes 663560 | tf_op jit(solution)/shard_map/ppermute | solution.py:348
  14.2 2.7 %collective-permute-start.4 = (bf16[288,384]{1,0:T(8,128)(2,1)}, bf16[288,384]{1,0:T(8,128)(2,1)S(1)}, u32[]{:S(2)}, u32[]{:S(2)}) collective-permute-start(bf16[288,384]{1,0:T(8,128)(2,1)} %get-tuple-element.33), channel_id=1, source_target_pairs={{0,4},{2,6},{4,0},{6,2},{1,5},{3,7},{5,1},{7,3},{8,12},{10,14},{12... | collective-permute-start | bytes 663560 | tf_op jit(solution)/shard_map/ppermute | solution.py:348
  16.9 0.7 collective-permute-start.5
  17.5 6.1 %all-to-all-start = ((bf16[16,128,128]{2,1,0:T(8,128)(2,1)}), bf16[16,128,128]{2,1,0:T(8,128)(2,1)S(1)}, u32[]{:S(2)}, u32[]{:S(2)}) async-start(bf16[16,128,128]{2,1,0:T(8,128)(2,1)} %get-tuple-element.43), calls=%async_computation | async-start | bytes 1048576 | tf_op jit(solution)/shard_map/all_to_all | solution.py:381
  23.7 1.0 %collective-permute-done.6.got = bf16[544,384]{1,0:T(8,128)(2,1)S(1)} collective-permute-done((bf16[544,384]{1,0:T(8,128)(2,1)}, bf16[544,384]{1,0:T(8,128)(2,1)S(1)}, u32[]{:S(2)}, u32[]{:S(2)}) %collective-permute-start.6) | collective-permute-done | bytes 417824 | tf_op jit(solution)/shard_map/ppermute | solution.py:383
  24.7 1.0 %copy-done = bf16[544,384]{1,0:T(8,128)(2,1)S(1)} copy-done((bf16[544,384]{1,0:T(8,128)(2,1)S(1)}, bf16[544,384]{1,0:T(8,128)(2,1)}, u32[]{:S(2)}) %copy-start) | copy-done | bytes 417816
  25.7 0.7 shard_map.113
  26.4 1.6 %collective-permute-start.8 = (bf16[144,384]{1,0:T(8,128)(2,1)S(1)}, bf16[144,384]{1,0:T(8,128)(2,1)S(1)}, u32[]{:S(2)}, u32[]{:S(2)}) collective-permute-start(bf16[144,384]{1,0:T(8,128)(2,1)S(1)} %get-tuple-element.40), channel_id=1, source_target_pairs={{0,2},{2,4},{4,6},{6,0},{1,3},{3,5},{5,7},{7,1},{8,10},{10,12},{12... | collective-permute-start | bytes 331784 | tf_op jit(solution)/shard_map/ppermute | solution.py:348
  28.0 1.0 %collective-permute-start.9 = (bf16[144,384]{1,0:T(8,128)(2,1)S(1)}, bf16[144,384]{1,0:T(8,128)(2,1)S(1)}, u32[]{:S(2)}, u32[]{:S(2)}) collective-permute-start(bf16[144,384]{1,0:T(8,128)(2,1)S(1)} %get-tuple-element.41), channel_id=1, source_target_pairs={{0,4},{2,6},{4,0},{6,2},{1,5},{3,7},{5,1},{7,3},{8,12},{10,14},{12... | collective-permute-start | bytes 331784 | tf_op jit(solution)/shard_map/ppermute | solution.py:348
  29.1 2.3 %collective-permute-start.10 = (bf16[144,384]{1,0:T(8,128)(2,1)S(1)}, bf16[144,384]{1,0:T(8,128)(2,1)S(1)}, u32[]{:S(2)}, u32[]{:S(2)}) collective-permute-start(bf16[144,384]{1,0:T(8,128)(2,1)S(1)} %get-tuple-element.42), channel_id=1, source_target_pairs={{0,6},{2,0},{4,2},{6,4},{1,7},{3,1},{5,3},{7,5},{8,14},{10,8},{12,... | collective-permute-start | bytes 331784 | tf_op jit(solution)/shard_map/ppermute | solution.py:348
  31.4 0.4 shard_map.114
  31.8 1.8 %collective-permute-start.7 = (bf16[160,384]{1,0:T(8,128)(2,1)S(1)}, bf16[160,384]{1,0:T(8,128)(2,1)S(1)}, u32[]{:S(2)}, u32[]{:S(2)}) collective-permute-start(bf16[160,384]{1,0:T(8,128)(2,1)S(1)} %get-tuple-element.39), channel_id=1, source_target_pairs={{0,8},{8,0},{1,9},{9,1},{2,10},{10,2},{3,11},{11,3},{4,12},{12,4},... | collective-permute-start | bytes 368648 | tf_op jit(solution)/shard_map/ppermute | solution.py:407
  33.6 0.7 all-to-all-done
  34.3 3.7 %shard_map.115._ = bf16[16,176,128]{2,1,0:T(8,128)(2,1)} custom-call(f32[8,2048]{1,0:T(8,128)S(1)} %copy-done.1, bf16[2048,128]{1,0:T(8,128)(2,1)S(1)} %bitcast.10, bf16[16,16,128]{2,1,0:T(8,128)(2,1)S(1)} %copy-done.2, f32[160,384]{1,0:T(8,128)S(1)} %get-tuple-element.38._.u_keep), custom_call_target="tpu_custom_call" | custom-call | flops 7000000000 | bytes 7000000 | tf_op jit(solution)/shard_map/pallas_call | solution.py:330
  38.0 0.5 collective-permute-done.10.v3
  38.5 0.5 shard_map.116
  39.0 2.7 %collective-permute-start.11 = (bf16[208,384]{1,0:T(8,128)(2,1)S(1)}, bf16[208,384]{1,0:T(8,128)(2,1)S(1)}, u32[]{:S(2)}, u32[]{:S(2)}) collective-permute-start(bf16[208,384]{1,0:T(8,128)(2,1)S(1)} %get-tuple-element.46), channel_id=1, source_target_pairs={{0,64},{64,0},{128,192},{192,128},{1,65},{65,1},{129,193},{193,129... | collective-permute-start | bytes 479240 | tf_op jit(solution)/shard_map/ppermute | solution.py:419
  41.7 8.9 %all-to-all-start.1 = ((bf16[16,176,128]{2,1,0:T(8,128)(2,1)}), bf16[16,176,128]{2,1,0:T(8,128)(2,1)S(1)}, u32[]{:S(2)}, u32[]{:S(2)}) async-start(bf16[16,176,128]{2,1,0:T(8,128)(2,1)} %shard_map.115._), calls=%async_computation.1 | async-start | bytes 1441792 | tf_op jit(solution)/shard_map/all_to_all | solution.py:422
  50.8 2.0 %collective-permute-start.12 = (bf16[112,384]{1,0:T(8,128)(2,1)S(1)}, bf16[112,384]{1,0:T(8,128)(2,1)S(1)}, u32[]{:S(2)}, u32[]{:S(2)}) collective-permute-start(bf16[112,384]{1,0:T(8,128)(2,1)S(1)} %get-tuple-element.48), channel_id=1, source_target_pairs={{0,16},{16,0},{32,48},{48,32},{1,17},{17,1},{33,49},{49,33},{2,18}... | collective-permute-start | bytes 258056 | tf_op jit(solution)/shard_map/ppermute | solution.py:419
  52.8 5.1 %collective-permute-done.12.got = bf16[112,384]{1,0:T(8,128)(2,1)S(1)} collective-permute-done((bf16[112,384]{1,0:T(8,128)(2,1)S(1)}, bf16[112,384]{1,0:T(8,128)(2,1)S(1)}, u32[]{:S(2)}, u32[]{:S(2)}) %collective-permute-start.12) | collective-permute-done | bytes 86048 | tf_op jit(solution)/shard_map/ppermute | solution.py:419
  58.0 2.2 %collective-permute-start.13 = (bf16[64,384]{1,0:T(8,128)(2,1)S(1)}, bf16[64,384]{1,0:T(8,128)(2,1)S(1)}, u32[]{:S(2)}, u32[]{:S(2)}) collective-permute-start(bf16[64,384]{1,0:T(8,128)(2,1)S(1)} %get-tuple-element.50), channel_id=1, source_target_pairs={{0,48},{48,0},{16,32},{32,16},{1,49},{49,1},{17,33},{33,17},{2,50}... | collective-permute-start | bytes 147464 | tf_op jit(solution)/shard_map/ppermute | solution.py:419
  60.2 3.4 %collective-permute-done.13.got = bf16[64,384]{1,0:T(8,128)(2,1)S(1)} collective-permute-done((bf16[64,384]{1,0:T(8,128)(2,1)S(1)}, bf16[64,384]{1,0:T(8,128)(2,1)S(1)}, u32[]{:S(2)}, u32[]{:S(2)}) %collective-permute-start.13) | collective-permute-done | bytes 49184 | tf_op jit(solution)/shard_map/ppermute | solution.py:419
  63.7 5.1 %collective-permute-start.14 = (bf16[48,384]{1,0:T(8,128)(2,1)S(1)}, bf16[48,384]{1,0:T(8,128)(2,1)S(1)}, u32[]{:S(2)}, u32[]{:S(2)}) collective-permute-start(bf16[48,384]{1,0:T(8,128)(2,1)S(1)} %get-tuple-element.52), channel_id=1, source_target_pairs={{0,192},{192,0},{64,128},{128,64},{1,193},{193,1},{65,129},{129,65... | collective-permute-start | bytes 110600 | tf_op jit(solution)/shard_map/ppermute | solution.py:419
  68.8 4.4 %collective-permute-done.14.got = bf16[48,384]{1,0:T(8,128)(2,1)S(1)} collective-permute-done((bf16[48,384]{1,0:T(8,128)(2,1)S(1)}, bf16[48,384]{1,0:T(8,128)(2,1)S(1)}, u32[]{:S(2)}, u32[]{:S(2)}) %collective-permute-start.14) | collective-permute-done | bytes 36896 | tf_op jit(solution)/shard_map/ppermute | solution.py:419
  73.2 0.7 shard_map.120
  73.9 0.9 %all-to-all-done.1.got_ref = bf16[16,176,128]{2,1,0:T(8,128)(2,1)S(1)} async-done(((bf16[16,176,128]{2,1,0:T(8,128)(2,1)}), bf16[16,176,128]{2,1,0:T(8,128)(2,1)S(1)}, u32[]{:S(2)}, u32[]{:S(2)}) %all-to-all-start.1) | async-done | bytes 720928 | tf_op jit(solution)/shard_map/all_to_all | solution.py:422
  74.8 1.9 %shard_map.121 = f32[512,128]{1,0:T(8,128)} custom-call(bf16[16,176,128]{2,1,0:T(8,128)(2,1)S(1)} %all-to-all-done.1.got_ref), custom_call_target="tpu_custom_call" | custom-call | flops 2000000000 | bytes 2000000 | tf_op jit(solution)/shard_map/pallas_call | solution.py:330
  (27 shorter events, 1.0 us)
Async XLA Ops:
  0.6 3.7 %collective-permute-start.2 = (bf16[128,2176]{1,0:T(8,128)(2,1)}, bf16[128,2176]{1,0:T(8,128)(2,1)S(1)}, u32[]{:S(2)}, u32[]{:S(2)}) collective-permute-start(bf16[128,2176]{1,0:T(8,128)(2,1)} %cot_hbm.1), channel_id=1, source_target_pairs={{0,1},{1,0},{2,3},{3,2},{4,5},{5,4},{6,7},{7,6},{8,9},{9,8},{10,11... | collective-permute-start | bytes 1671176 | tf_op jit(solution)/shard_map/ppermute | solution.py:355
  0.7 3.5 %collective-permute-start = (bf16[128,2048]{1,0:T(8,128)(2,1)}, bf16[128,2048]{1,0:T(8,128)(2,1)S(1)}, u32[]{:S(2)}, u32[]{:S(2)}) collective-permute-start(bf16[128,2048]{1,0:T(8,128)(2,1)} %pooled_hbm.1), channel_id=1, source_target_pairs={{0,1},{1,0},{2,3},{3,2},{4,5},{5,4},{6,7},{7,6},{8,9},{9,8},{10,11... | collective-permute-start | bytes 1572872 | tf_op jit(solution)/shard_map/ppermute | solution.py:355
  1.2 3.0 %collective-permute-start.1 = (bf16[128,128]{1,0:T(8,128)(2,1)}, bf16[128,128]{1,0:T(8,128)(2,1)S(1)}, u32[]{:S(2)}, u32[]{:S(2)}) collective-permute-start(bf16[128,128]{1,0:T(8,128)(2,1)} %dense_hbm.1), channel_id=1, source_target_pairs={{0,1},{1,0},{2,3},{3,2},{4,5},{5,4},{6,7},{7,6},{8,9},{9,8},{10,11... | collective-permute-start | bytes 98312 | tf_op jit(solution)/shard_map/ppermute | solution.py:355
  4.3 0.6 copy-start.6
  4.3 0.8 %copy-start.5 = (bf16[128,2048]{1,0:T(8,128)(2,1)}, bf16[128,2048]{1,0:T(8,128)(2,1)S(1)}, u32[]{:S(2)}) copy-start(bf16[128,2048]{1,0:T(8,128)(2,1)S(1)} %collective-permute-done.pooled2_hbm) | copy-start | bytes 1572868
  4.3 1.0 %copy-start.4 = (bf16[128,2176]{1,0:T(8,128)(2,1)}, bf16[128,2176]{1,0:T(8,128)(2,1)S(1)}, u32[]{:S(2)}) copy-start(bf16[128,2176]{1,0:T(8,128)(2,1)S(1)} %collective-permute-done.2.cot2_hbm) | copy-start | bytes 1671172
  12.4 12.3 %collective-permute-start.6 = (bf16[544,384]{1,0:T(8,128)(2,1)}, bf16[544,384]{1,0:T(8,128)(2,1)S(1)}, u32[]{:S(2)}, u32[]{:S(2)}) collective-permute-start(bf16[544,384]{1,0:T(8,128)(2,1)} %get-tuple-element.36), channel_id=1, source_target_pairs={{0,8},{8,0},{1,9},{9,1},{2,10},{10,2},{3,11},{11,3},{4,12},{12,4},... | collective-permute-start | bytes 1253384 | tf_op jit(solution)/shard_map/ppermute | solution.py:383
  12.6 16.5 %collective-permute-start.3 = (bf16[288,384]{1,0:T(8,128)(2,1)}, bf16[288,384]{1,0:T(8,128)(2,1)S(1)}, u32[]{:S(2)}, u32[]{:S(2)}) collective-permute-start(bf16[288,384]{1,0:T(8,128)(2,1)} %get-tuple-element.32), channel_id=1, source_target_pairs={{0,2},{2,4},{4,6},{6,0},{1,3},{3,5},{5,7},{7,1},{8,10},{10,12},{12... | collective-permute-start | bytes 663560 | tf_op jit(solution)/shard_map/ppermute | solution.py:348
  14.2 17.2 %collective-permute-start.4 = (bf16[288,384]{1,0:T(8,128)(2,1)}, bf16[288,384]{1,0:T(8,128)(2,1)S(1)}, u32[]{:S(2)}, u32[]{:S(2)}) collective-permute-start(bf16[288,384]{1,0:T(8,128)(2,1)} %get-tuple-element.33), channel_id=1, source_target_pairs={{0,4},{2,6},{4,0},{6,2},{1,5},{3,7},{5,1},{7,3},{8,12},{10,14},{12... | collective-permute-start | bytes 663560 | tf_op jit(solution)/shard_map/ppermute | solution.py:348
  16.9 14.5 %collective-permute-start.5 = (bf16[288,384]{1,0:T(8,128)(2,1)}, bf16[288,384]{1,0:T(8,128)(2,1)S(1)}, u32[]{:S(2)}, u32[]{:S(2)}) collective-permute-start(bf16[288,384]{1,0:T(8,128)(2,1)} %get-tuple-element.34), channel_id=1, source_target_pairs={{0,6},{2,0},{4,2},{6,4},{1,7},{3,1},{5,3},{7,5},{8,14},{10,8},{12,... | collective-permute-start | bytes 663560 | tf_op jit(solution)/shard_map/ppermute | solution.py:348
  17.5 16.8 %all-to-all-start = ((bf16[16,128,128]{2,1,0:T(8,128)(2,1)}), bf16[16,128,128]{2,1,0:T(8,128)(2,1)S(1)}, u32[]{:S(2)}, u32[]{:S(2)}) async-start(bf16[16,128,128]{2,1,0:T(8,128)(2,1)} %get-tuple-element.43), calls=%async_computation | async-start | bytes 1048576 | tf_op jit(solution)/shard_map/all_to_all | solution.py:381
  24.7 1.0 %copy-start = (bf16[544,384]{1,0:T(8,128)(2,1)S(1)}, bf16[544,384]{1,0:T(8,128)(2,1)}, u32[]{:S(2)}) copy-start(bf16[544,384]{1,0:T(8,128)(2,1)} %get-tuple-element.35.own) | copy-start | bytes 1253380
  25.7 5.7 %copy-start.3 = (bf16[288,384]{1,0:T(8,128)(2,1)S(1)}, bf16[288,384]{1,0:T(8,128)(2,1)}, u32[]{:S(2)}) copy-start(bf16[288,384]{1,0:T(8,128)(2,1)} %get-tuple-element.31.m0) | copy-start | bytes 663556
  26.4 11.6 %collective-permute-start.8 = (bf16[144,384]{1,0:T(8,128)(2,1)S(1)}, bf16[144,384]{1,0:T(8,128)(2,1)S(1)}, u32[]{:S(2)}, u32[]{:S(2)}) collective-permute-start(bf16[144,384]{1,0:T(8,128)(2,1)S(1)} %get-tuple-element.40), channel_id=1, source_target_pairs={{0,2},{2,4},{4,6},{6,0},{1,3},{3,5},{5,7},{7,1},{8,10},{10,12},{12... | collective-permute-start | bytes 331784 | tf_op jit(solution)/shard_map/ppermute | solution.py:348
  28.0 10.0 %collective-permute-start.9 = (bf16[144,384]{1,0:T(8,128)(2,1)S(1)}, bf16[144,384]{1,0:T(8,128)(2,1)S(1)}, u32[]{:S(2)}, u32[]{:S(2)}) collective-permute-start(bf16[144,384]{1,0:T(8,128)(2,1)S(1)} %get-tuple-element.41), channel_id=1, source_target_pairs={{0,4},{2,6},{4,0},{6,2},{1,5},{3,7},{5,1},{7,3},{8,12},{10,14},{12... | collective-permute-start | bytes 331784 | tf_op jit(solution)/shard_map/ppermute | solution.py:348
  29.1 9.4 %collective-permute-start.10 = (bf16[144,384]{1,0:T(8,128)(2,1)S(1)}, bf16[144,384]{1,0:T(8,128)(2,1)S(1)}, u32[]{:S(2)}, u32[]{:S(2)}) collective-permute-start(bf16[144,384]{1,0:T(8,128)(2,1)S(1)} %get-tuple-element.42), channel_id=1, source_target_pairs={{0,6},{2,0},{4,2},{6,4},{1,7},{3,1},{5,3},{7,5},{8,14},{10,8},{12,... | collective-permute-start | bytes 331784 | tf_op jit(solution)/shard_map/ppermute | solution.py:348
  31.4 2.9 %copy-start.1 = (f32[8,2048]{1,0:T(8,128)S(1)}, f32[8,2048]{1,0:T(8,128)}, u32[]{:S(2)}) copy-start(f32[8,2048]{1,0:T(8,128)} %get-tuple-element.30._.found_ref) | copy-start | bytes 196612
  31.4 2.9 %copy-start.2 = (bf16[16,16,128]{2,1,0:T(8,128)(2,1)S(1)}, bf16[16,16,128]{2,1,0:T(8,128)(2,1)}, u32[]{:S(2)}) copy-start(bf16[16,16,128]{2,1,0:T(8,128)(2,1)} %get-tuple-element.44.pos_ref) | copy-start | bytes 196612
  31.8 6.7 %collective-permute-start.7 = (bf16[160,384]{1,0:T(8,128)(2,1)S(1)}, bf16[160,384]{1,0:T(8,128)(2,1)S(1)}, u32[]{:S(2)}, u32[]{:S(2)}) collective-permute-start(bf16[160,384]{1,0:T(8,128)(2,1)S(1)} %get-tuple-element.39), channel_id=1, source_target_pairs={{0,8},{8,0},{1,9},{9,1},{2,10},{10,2},{3,11},{11,3},{4,12},{12,4},... | collective-permute-start | bytes 368648 | tf_op jit(solution)/shard_map/ppermute | solution.py:407
  39.0 11.6 %collective-permute-start.11 = (bf16[208,384]{1,0:T(8,128)(2,1)S(1)}, bf16[208,384]{1,0:T(8,128)(2,1)S(1)}, u32[]{:S(2)}, u32[]{:S(2)}) collective-permute-start(bf16[208,384]{1,0:T(8,128)(2,1)S(1)} %get-tuple-element.46), channel_id=1, source_target_pairs={{0,64},{64,0},{128,192},{192,128},{1,65},{65,1},{129,193},{193,129... | collective-permute-start | bytes 479240 | tf_op jit(solution)/shard_map/ppermute | solution.py:419
  41.7 33.1 %all-to-all-start.1 = ((bf16[16,176,128]{2,1,0:T(8,128)(2,1)}), bf16[16,176,128]{2,1,0:T(8,128)(2,1)S(1)}, u32[]{:S(2)}, u32[]{:S(2)}) async-start(bf16[16,176,128]{2,1,0:T(8,128)(2,1)} %shard_map.115._), calls=%async_computation.1 | async-start | bytes 1441792 | tf_op jit(solution)/shard_map/all_to_all | solution.py:422
  50.8 7.1 %collective-permute-start.12 = (bf16[112,384]{1,0:T(8,128)(2,1)S(1)}, bf16[112,384]{1,0:T(8,128)(2,1)S(1)}, u32[]{:S(2)}, u32[]{:S(2)}) collective-permute-start(bf16[112,384]{1,0:T(8,128)(2,1)S(1)} %get-tuple-element.48), channel_id=1, source_target_pairs={{0,16},{16,0},{32,48},{48,32},{1,17},{17,1},{33,49},{49,33},{2,18}... | collective-permute-start | bytes 258056 | tf_op jit(solution)/shard_map/ppermute | solution.py:419
  58.0 5.6 %collective-permute-start.13 = (bf16[64,384]{1,0:T(8,128)(2,1)S(1)}, bf16[64,384]{1,0:T(8,128)(2,1)S(1)}, u32[]{:S(2)}, u32[]{:S(2)}) collective-permute-start(bf16[64,384]{1,0:T(8,128)(2,1)S(1)} %get-tuple-element.50), channel_id=1, source_target_pairs={{0,48},{48,0},{16,32},{32,16},{1,49},{49,1},{17,33},{33,17},{2,50}... | collective-permute-start | bytes 147464 | tf_op jit(solution)/shard_map/ppermute | solution.py:419
  63.7 9.6 %collective-permute-start.14 = (bf16[48,384]{1,0:T(8,128)(2,1)S(1)}, bf16[48,384]{1,0:T(8,128)(2,1)S(1)}, u32[]{:S(2)}, u32[]{:S(2)}) collective-permute-start(bf16[48,384]{1,0:T(8,128)(2,1)S(1)} %get-tuple-element.52), channel_id=1, source_target_pairs={{0,192},{192,0},{64,128},{128,64},{1,193},{193,1},{65,129},{129,65... | collective-permute-start | bytes 110600 | tf_op jit(solution)/shard_map/ppermute | solution.py:419

commit v5 on v4

--- a/solution.py
+++ b/solution.py
@@ -63,7 +63,7 @@
 
 
 def weight_kernel(
-    place_ref, pooled_hbm, pooled2_hbm, dense_hbm, dense2_hbm, v_hbm, cot_hbm, cot2_hbm, u_hbm, bias_hbm, _,
+    place_ref, pooled_hbm, pooled2_hbm, dense_hbm, dense2_hbm, v_hbm, cot_hbm, cot2_hbm, u_hbm, bias_hbm,
     u0, u1, u2, u3, v_keep, v_send, out_hbm,
     pooled_ref, dense_ref, cot_ref, mix_ref, v_ref, u_ref,
     gu, gv, bias_row, bu0, bu1, bu2, bu3, bk, bs, bias_ref, out_ref, load_sems, sems, out_sems,
@@ -239,7 +239,7 @@
         bias_ref[j : j + 1, :] = bias[k : k + 1, at : at + 128]
 
 
-def index_kernel(uniq_ref, slot_ref, found_ref, pos_ref):
+def index_kernel(uniq_ref, slot_ref, _, found_ref, pos_ref):
     uniq = uniq_ref[...]
     keeper = lax.shift_right_logical(uniq, 9)
     row = jnp.bitwise_and(uniq, KEEP - 1)
@@ -259,8 +259,8 @@
         ranks.append(jnp.sum(member * (running - 1.0), axis=0, keepdims=True))
     member = jnp.concatenate(members, axis=1)
     rank = jnp.concatenate(ranks, axis=1)
-    row_high = lax.shift_right_logical(row, 4).astype(F32)
-    row_low = jnp.bitwise_and(row, 15).astype(F32)
+    row_high = lax.shift_right_logical(row, 8).astype(F32)
+    row_low = jnp.bitwise_and(row, 255).astype(F32)
     digits = jnp.concatenate([member * row_high, member * row_low], axis=0).astype(BF)
     ranked = lax.broadcasted_iota(jnp.int32, (CAP, UNIQ), 0).astype(F32) == rank
     where = nt(digits, ranked.astype(F32).astype(BF))
@@ -315,15 +315,18 @@
 
 
 def keep_kernel(got_ref, out_ref):
-    names = lax.broadcasted_iota(jnp.int32, (KEEP, CAP), 0).astype(F32)
-    acc = jnp.zeros((KEEP, EMB), F32)
+    names = lax.broadcasted_iota(jnp.int32, (256, CAP), 0).astype(F32).astype(BF)
+    one, zero = jnp.ones((256, CAP), BF), jnp.zeros((256, CAP), BF)
+    accs = [jnp.zeros((256, EMB), F32) for _ in range(2)]
     for g in range(N_REP):
         pos = got_ref[g, CAP:PAYLOAD, :].astype(F32)
-        at = pos[0:2, :] * 16.0 + pos[2:4, :]
-        at = jnp.concatenate([at[0:1, :], at[1:2, 0 : CAP - 128]], axis=1)
-        hot = (names == at).astype(F32).astype(BF)
-        acc = acc + nn(hot, got_ref[g, 0:CAP, :])
-    out_ref[...] = acc
+        at = [jnp.concatenate([pos[i : i + 1, :], pos[i + 1 : i + 2, 0 : CAP - 128]], axis=1) for i in (0, 2)]
+        for half in range(2):
+            own = jnp.where(at[0] == float(half), at[1], -1.0).astype(BF)
+            hot = jnp.where(names == own, one, zero)
+            accs[half] = accs[half] + nn(hot, got_ref[g, 0:CAP, :])
+    for half in range(2):
+        out_ref[half * 256 : (half + 1) * 256, :] = accs[half]
 
 
 def call(kernel, outs, ins, scratch=(), mib=24, spare=None, us=2):
@@ -344,9 +347,10 @@
 
 
 def shifted(messages, axis):
-    return [
-        lax.ppermute(m, axis, [(i, (i + s) % 4) for i in range(4)]) for s, m in enumerate(messages, 1)
-    ]
+    got = {
+        s: lax.ppermute(messages[s - 1], axis, [(i, (i + s) % 4) for i in range(4)]) for s in (2, 1, 3)
+    }
+    return [got[s] for s in (1, 2, 3)]
 
 
 def shards(dense, pooled, cot, proj_v, proj_u, bias, lookup_slot, uniq_rows):
@@ -355,19 +359,13 @@
     other = [lax.ppermute(a, "c", swap) for a in (dense, pooled, cot)]
     dma = pltpu.SemaphoreType.DMA
     dense2, pooled2, cot2 = other
-    found, pos = call(
-        index_kernel,
-        [(VMEM, (8, SAMP), F32), (VMEM, (N_REP, 16, 128), BF)],
-        near(uniq_rows.reshape(1, UNIQ), lookup_slot.reshape(SAMP, 2).T),
-        mib=56,
-    )
     u_shape, v_shape = (288, LAT), (544, LAT)
     bias_rows, out_shape = (D0 // 128, 128), (N_TAB, 128, EMB)
     loaded = (pooled, pooled2, dense, dense2, proj_v, cot, cot2, proj_u, bias.reshape(bias_rows))
     u0, u1, u2, u3, v_keep, v_send, outgoing = call(
         weight_kernel,
         [(HBM, u_shape, BF)] * 4 + [(HBM, v_shape, BF)] * 2 + [(HBM, out_shape, BF)],
-        [place] + [(HBM, a) for a in loaded] + [(ANY, found)],
+        [place] + [(HBM, a) for a in loaded],
         [pltpu.VMEM((256, w), BF) for w in (D0 - EMB, EMB, D0, D0)]
         + [pltpu.VMEM((D0, LAT), BF), pltpu.VMEM((LAT, D0), BF)]
         + [pltpu.VMEM((D0, LAT), F32), pltpu.VMEM((D0, LAT), F32), pltpu.VMEM((1, D0), F32)]
@@ -397,6 +395,12 @@
         [pltpu.VMEM((288, LAT), F32), pltpu.VMEM(u_shape, BF), dma((1,))],
         us=100,
     )
+    found, pos = call(
+        index_kernel,
+        [(VMEM, (8, SAMP), F32), (VMEM, (N_REP, 16, 128), BF)],
+        near(uniq_rows.reshape(1, UNIQ), lookup_slot.reshape(SAMP, 2).T) + [(ANY, u_keep)],
+        mib=24,
+    )
     (payload,) = call(
         rows_kernel,
         [(HBM, (N_REP, PAYLOAD, EMB), BF)],

time: 77.1 us -> 76.1 us (0.987)
  Pallas kernels: 18.3 us -> 16.9 us
  starting transfers between devices: 39.6 us -> 38.5 us
  waiting for transfers between devices: 16 us -> 16.8 us
    ppermute x3, waiting for transfers between devices: 0.01 us -> 2.36 us  [shards(): other = [lax.ppermute(a, 'c', swap) for a in (dense, pooled, cot)]]
    pallas_call x11, Pallas kernels: 18.3 us -> 16.9 us  [call(): pl.pallas_call(kernel, out_shape=tuple((jax.ShapeDtypeStruct(s, d) for _,...]
    ppermute x4, starting transfers between devices: 12 us -> 11 us  [halve(): return (kept, lax.ppermute(sent, axis, pairs))]
  transfers between devices with their start and end apart: 17 -> 17, of which waited for: 7 -> 7; matrix products, arithmetic and copies ran while one was open for 0% -> 0% of each run, Pallas kernels for 11% -> 10%
where the time goes in v5:
time: 76.1 us; the launch traced here: 75 us
  starting transfers between devices  38.5 us (51%)
  Pallas kernels  16.9 us (22%)
  waiting for transfers between devices  16.8 us (22%)
  local copies, waits for them, and re-layouts  2 us (3%)
  between operations  0.8 us (1%)
    pallas_call x11, Pallas kernels, call(): pl.pallas_call(kernel, out_shape=tuple((jax.ShapeDtypeStruct(s, d) for _,...  16.9 us
    ppermute x4, waiting for transfers between devices, halve(): return (kept, lax.ppermute(sent, axis, pairs))  13.1 us
    ppermute x4, starting transfers between devices, halve(): return (kept, lax.ppermute(sent, axis, pairs))  11 us
    ppermute x6, starting transfers between devices, shifted(): lax.ppermute(messages[s - 1], axis, [(i, (i + s) % 4) for i in range(4)])  9.93 us
    all_to_all x1, starting transfers between devices, shards(): gathered = lax.all_to_all(payload, REP, 0, 0, tiled=True)  8.32 us
    all_to_all x1, starting transfers between devices, shards(): lax.all_to_all(outgoing, TABLE, 0, 0, tiled=True).reshape(SAMP, EMB)  6.13 us
    ppermute x3, waiting for transfers between devices, shards(): other = [lax.ppermute(a, 'c', swap) for a in (dense, pooled, cot)]  2.36 us
    ppermute x1, starting transfers between devices, shards(): u_got = lax.ppermute(u_send, 'zl', swap)  2.26 us
  transfers between devices with their start and end apart: 17, of which 7 were waited for; matrix products, arithmetic and copies ran while one was open for 0% of the time, Pallas kernels for 10%

profile of v5, /device:TPU:40, one launch (start us, length us, event | category | flops | bytes accessed | tf_op | source)
XLA Modules:
  0.0 75.0 jit_solution(9586227995857507058)
XLA Ops:
  0.7 0.5 collective-permute-start
  1.3 2.4 %collective-permute-done.1.dense2_hbm = bf16[128,128]{1,0:T(8,128)(2,1)S(1)} collective-permute-done((bf16[128,128]{1,0:T(8,128)(2,1)}, bf16[128,128]{1,0:T(8,128)(2,1)S(1)}, u32[]{:S(2)}, u32[]{:S(2)}) %collective-permute-start.1) | collective-permute-done | bytes 32800 | tf_op jit(solution)/shard_map/ppermute | solution.py:359
  3.7 0.6 copy-done.6
  4.3 0.2 copy-done.5
  4.7 7.1 %shard_map.111 = (bf16[288,384]{1,0:T(8,128)(2,1)}, bf16[288,384]{1,0:T(8,128)(2,1)}, bf16[288,384]{1,0:T(8,128)(2,1)}, bf16[288,384]{1,0:T(8,128)(2,1)}, bf16[5...) custom-call(s32[1]{0:T(128)} %bitcast.place_ref._, bf16[128,2048]{1,0:T(8,128)(2,1)} %pooled_hbm.1, ...), custom_call_target="tpu_custom_call" | custom-call | flops 8000000000 | bytes 8000000 | tf_op jit(solution)/shard_map/pallas_call | solution.py:333
  11.8 0.2 collective-permute-start.6
  12.0 1.6 %collective-permute-start.3 = (bf16[288,384]{1,0:T(8,128)(2,1)}, bf16[288,384]{1,0:T(8,128)(2,1)S(1)}, u32[]{:S(2)}, u32[]{:S(2)}) collective-permute-start(bf16[288,384]{1,0:T(8,128)(2,1)} %get-tuple-element.31), channel_id=1, source_target_pairs={{0,2},{2,4},{4,6},{6,0},{1,3},{3,5},{5,7},{7,1},{8,10},{10,12},{12... | collective-permute-start | bytes 663560 | tf_op jit(solution)/shard_map/ppermute | solution.py:351
  13.6 2.7 %collective-permute-start.4 = (bf16[288,384]{1,0:T(8,128)(2,1)}, bf16[288,384]{1,0:T(8,128)(2,1)S(1)}, u32[]{:S(2)}, u32[]{:S(2)}) collective-permute-start(bf16[288,384]{1,0:T(8,128)(2,1)} %get-tuple-element.32), channel_id=1, source_target_pairs={{0,4},{2,6},{4,0},{6,2},{1,5},{3,7},{5,1},{7,3},{8,12},{10,14},{12... | collective-permute-start | bytes 663560 | tf_op jit(solution)/shard_map/ppermute | solution.py:351
  16.3 0.7 collective-permute-start.5
  17.0 6.1 %all-to-all-start = ((bf16[16,128,128]{2,1,0:T(8,128)(2,1)}), bf16[16,128,128]{2,1,0:T(8,128)(2,1)S(1)}, u32[]{:S(2)}, u32[]{:S(2)}) async-start(bf16[16,128,128]{2,1,0:T(8,128)(2,1)} %get-tuple-element.43), calls=%async_computation | async-start | bytes 1048576 | tf_op jit(solution)/shard_map/all_to_all | solution.py:379
  23.1 0.8 %collective-permute-done.6.got = bf16[544,384]{1,0:T(8,128)(2,1)S(1)} collective-permute-done((bf16[544,384]{1,0:T(8,128)(2,1)}, bf16[544,384]{1,0:T(8,128)(2,1)S(1)}, u32[]{:S(2)}, u32[]{:S(2)}) %collective-permute-start.6) | collective-permute-done | bytes 417824 | tf_op jit(solution)/shard_map/ppermute | solution.py:381
  23.8 1.0 %copy-done.2 = bf16[544,384]{1,0:T(8,128)(2,1)S(1)} copy-done((bf16[544,384]{1,0:T(8,128)(2,1)S(1)}, bf16[544,384]{1,0:T(8,128)(2,1)}, u32[]{:S(2)}) %copy-start.2) | copy-done | bytes 417816
  24.9 0.7 shard_map.112
  25.5 1.7 %collective-permute-start.8 = (bf16[144,384]{1,0:T(8,128)(2,1)S(1)}, bf16[144,384]{1,0:T(8,128)(2,1)S(1)}, u32[]{:S(2)}, u32[]{:S(2)}) collective-permute-start(bf16[144,384]{1,0:T(8,128)(2,1)S(1)} %get-tuple-element.39), channel_id=1, source_target_pairs={{0,2},{2,4},{4,6},{6,0},{1,3},{3,5},{5,7},{7,1},{8,10},{10,12},{12... | collective-permute-start | bytes 331784 | tf_op jit(solution)/shard_map/ppermute | solution.py:351
  27.2 1.0 %collective-permute-start.9 = (bf16[144,384]{1,0:T(8,128)(2,1)S(1)}, bf16[144,384]{1,0:T(8,128)(2,1)S(1)}, u32[]{:S(2)}, u32[]{:S(2)}) collective-permute-start(bf16[144,384]{1,0:T(8,128)(2,1)S(1)} %get-tuple-element.40), channel_id=1, source_target_pairs={{0,4},{2,6},{4,0},{6,2},{1,5},{3,7},{5,1},{7,3},{8,12},{10,14},{12... | collective-permute-start | bytes 331784 | tf_op jit(solution)/shard_map/ppermute | solution.py:351
  28.2 2.3 %collective-permute-start.10 = (bf16[144,384]{1,0:T(8,128)(2,1)S(1)}, bf16[144,384]{1,0:T(8,128)(2,1)S(1)}, u32[]{:S(2)}, u32[]{:S(2)}) collective-permute-start(bf16[144,384]{1,0:T(8,128)(2,1)S(1)} %get-tuple-element.41), channel_id=1, source_target_pairs={{0,6},{2,0},{4,2},{6,4},{1,7},{3,1},{5,3},{7,5},{8,14},{10,8},{12,... | collective-permute-start | bytes 331784 | tf_op jit(solution)/shard_map/ppermute | solution.py:351
  30.6 0.4 shard_map.113
  31.0 2.3 %collective-permute-start.7 = (bf16[160,384]{1,0:T(8,128)(2,1)S(1)}, bf16[160,384]{1,0:T(8,128)(2,1)S(1)}, u32[]{:S(2)}, u32[]{:S(2)}) collective-permute-start(bf16[160,384]{1,0:T(8,128)(2,1)S(1)} %get-tuple-element.38), channel_id=1, source_target_pairs={{0,8},{8,0},{1,9},{9,1},{2,10},{10,2},{3,11},{11,3},{4,12},{12,4},... | collective-permute-start | bytes 368648 | tf_op jit(solution)/shard_map/ppermute | solution.py:411
  33.3 1.6 %shard_map.114 = (f32[8,2048]{1,0:T(8,128)S(1)}, bf16[16,16,128]{2,1,0:T(8,128)(2,1)S(1)}) custom-call(s32[1,2048]{1,0:T(1,128)S(1)} %bitcast.12, s32[2,2048]{1,0:T(2,128)S(1)} %bitcast.11, f32[160,384]{1,0:T(8,128)S(1)} %get-tuple-element.37._.u_keep), custom_call_target="tpu_custom_call" | custom-call | flops 2000000000 | bytes 2000000 | tf_op jit(solution)/shard_map/pallas_call | solution.py:333
  34.8 3.7 %shard_map.115._ = bf16[16,176,128]{2,1,0:T(8,128)(2,1)} custom-call(f32[8,2048]{1,0:T(8,128)S(1)} %get-tuple-element.42.found_ref, bf16[2048,128]{1,0:T(8,128)(2,1)S(1)} %bitcast.10, bf16[16,16,128]{2,1,0:T(8,128)(2,1)S(1)} %get-tuple-element.44.pos_ref, f32[160,384]{1,0:T(8,128)S(1)} %get-tuple-element.37._.u_keep), custom_call_target="tpu_custom_call" | custom-call | flops 7000000000 | bytes 7000000 | tf_op jit(solution)/shard_map/pallas_call | solution.py:333
  38.6 0.5 shard_map.116
  39.1 3.4 %collective-permute-start.11 = (bf16[208,384]{1,0:T(8,128)(2,1)S(1)}, bf16[208,384]{1,0:T(8,128)(2,1)S(1)}, u32[]{:S(2)}, u32[]{:S(2)}) collective-permute-start(bf16[208,384]{1,0:T(8,128)(2,1)S(1)} %get-tuple-element.46), channel_id=1, source_target_pairs={{0,64},{64,0},{128,192},{192,128},{1,65},{65,1},{129,193},{193,129... | collective-permute-start | bytes 479240 | tf_op jit(solution)/shard_map/ppermute | solution.py:423
  42.5 8.3 %all-to-all-start.1 = ((bf16[16,176,128]{2,1,0:T(8,128)(2,1)}), bf16[16,176,128]{2,1,0:T(8,128)(2,1)S(1)}, u32[]{:S(2)}, u32[]{:S(2)}) async-start(bf16[16,176,128]{2,1,0:T(8,128)(2,1)} %shard_map.115._), calls=%async_computation.1 | async-start | bytes 1441792 | tf_op jit(solution)/shard_map/all_to_all | solution.py:426
  51.0 2.0 %collective-permute-start.12 = (bf16[112,384]{1,0:T(8,128)(2,1)S(1)}, bf16[112,384]{1,0:T(8,128)(2,1)S(1)}, u32[]{:S(2)}, u32[]{:S(2)}) collective-permute-start(bf16[112,384]{1,0:T(8,128)(2,1)S(1)} %get-tuple-element.48), channel_id=1, source_target_pairs={{0,16},{16,0},{32,48},{48,32},{1,17},{17,1},{33,49},{49,33},{2,18}... | collective-permute-start | bytes 258056 | tf_op jit(solution)/shard_map/ppermute | solution.py:423
  53.0 4.1 %collective-permute-done.12.got = bf16[112,384]{1,0:T(8,128)(2,1)S(1)} collective-permute-done((bf16[112,384]{1,0:T(8,128)(2,1)S(1)}, bf16[112,384]{1,0:T(8,128)(2,1)S(1)}, u32[]{:S(2)}, u32[]{:S(2)}) %collective-permute-start.12) | collective-permute-done | bytes 86048 | tf_op jit(solution)/shard_map/ppermute | solution.py:423
  57.3 2.1 %collective-permute-start.13 = (bf16[64,384]{1,0:T(8,128)(2,1)S(1)}, bf16[64,384]{1,0:T(8,128)(2,1)S(1)}, u32[]{:S(2)}, u32[]{:S(2)}) collective-permute-start(bf16[64,384]{1,0:T(8,128)(2,1)S(1)} %get-tuple-element.50), channel_id=1, source_target_pairs={{0,48},{48,0},{16,32},{32,16},{1,49},{49,1},{17,33},{33,17},{2,50}... | collective-permute-start | bytes 147464 | tf_op jit(solution)/shard_map/ppermute | solution.py:423
  59.4 4.8 %collective-permute-done.13.got = bf16[64,384]{1,0:T(8,128)(2,1)S(1)} collective-permute-done((bf16[64,384]{1,0:T(8,128)(2,1)S(1)}, bf16[64,384]{1,0:T(8,128)(2,1)S(1)}, u32[]{:S(2)}, u32[]{:S(2)}) %collective-permute-start.13) | collective-permute-done | bytes 49184 | tf_op jit(solution)/shard_map/ppermute | solution.py:423
  64.2 3.5 %collective-permute-start.14 = (bf16[48,384]{1,0:T(8,128)(2,1)S(1)}, bf16[48,384]{1,0:T(8,128)(2,1)S(1)}, u32[]{:S(2)}, u32[]{:S(2)}) collective-permute-start(bf16[48,384]{1,0:T(8,128)(2,1)S(1)} %get-tuple-element.52), channel_id=1, source_target_pairs={{0,192},{192,0},{64,128},{128,64},{1,193},{193,1},{65,129},{129,65... | collective-permute-start | bytes 110600 | tf_op jit(solution)/shard_map/ppermute | solution.py:423
  67.7 4.2 %collective-permute-done.14.got = bf16[48,384]{1,0:T(8,128)(2,1)S(1)} collective-permute-done((bf16[48,384]{1,0:T(8,128)(2,1)S(1)}, bf16[48,384]{1,0:T(8,128)(2,1)S(1)}, u32[]{:S(2)}, u32[]{:S(2)}) %collective-permute-start.14) | collective-permute-done | bytes 36896 | tf_op jit(solution)/shard_map/ppermute | solution.py:423
  71.9 0.7 shard_map.120
  72.6 0.5 all-to-all-done.1.got_ref
  73.1 1.9 %shard_map.121 = f32[512,128]{1,0:T(8,128)} custom-call(bf16[16,176,128]{2,1,0:T(8,128)(2,1)S(1)} %all-to-all-done.1.got_ref), custom_call_target="tpu_custom_call" | custom-call | flops 2000000000 | bytes 2000000 | tf_op jit(solution)/shard_map/pallas_call | solution.py:333
  (27 shorter events, 0.8 us)
Async XLA Ops:
  0.6 3.1 %collective-permute-start.2 = (bf16[128,2176]{1,0:T(8,128)(2,1)}, bf16[128,2176]{1,0:T(8,128)(2,1)S(1)}, u32[]{:S(2)}, u32[]{:S(2)}) collective-permute-start(bf16[128,2176]{1,0:T(8,128)(2,1)} %cot_hbm.1), channel_id=1, source_target_pairs={{0,1},{1,0},{2,3},{3,2},{4,5},{5,4},{6,7},{7,6},{8,9},{9,8},{10,11... | collective-permute-start | bytes 1671176 | tf_op jit(solution)/shard_map/ppermute | solution.py:359
  0.7 3.0 %collective-permute-start = (bf16[128,2048]{1,0:T(8,128)(2,1)}, bf16[128,2048]{1,0:T(8,128)(2,1)S(1)}, u32[]{:S(2)}, u32[]{:S(2)}) collective-permute-start(bf16[128,2048]{1,0:T(8,128)(2,1)} %pooled_hbm.1), channel_id=1, source_target_pairs={{0,1},{1,0},{2,3},{3,2},{4,5},{5,4},{6,7},{7,6},{8,9},{9,8},{10,11... | collective-permute-start | bytes 1572872 | tf_op jit(solution)/shard_map/ppermute | solution.py:359
  1.2 2.5 %collective-permute-start.1 = (bf16[128,128]{1,0:T(8,128)(2,1)}, bf16[128,128]{1,0:T(8,128)(2,1)S(1)}, u32[]{:S(2)}, u32[]{:S(2)}) collective-permute-start(bf16[128,128]{1,0:T(8,128)(2,1)} %dense_hbm.1), channel_id=1, source_target_pairs={{0,1},{1,0},{2,3},{3,2},{4,5},{5,4},{6,7},{7,6},{8,9},{9,8},{10,11... | collective-permute-start | bytes 98312 | tf_op jit(solution)/shard_map/ppermute | solution.py:359
  3.7 0.6 copy-start.6
  3.7 0.8 %copy-start.5 = (bf16[128,2048]{1,0:T(8,128)(2,1)}, bf16[128,2048]{1,0:T(8,128)(2,1)S(1)}, u32[]{:S(2)}) copy-start(bf16[128,2048]{1,0:T(8,128)(2,1)S(1)} %collective-permute-done.pooled2_hbm) | copy-start | bytes 1572868
  3.7 1.0 %copy-start.4 = (bf16[128,2176]{1,0:T(8,128)(2,1)}, bf16[128,2176]{1,0:T(8,128)(2,1)S(1)}, u32[]{:S(2)}) copy-start(bf16[128,2176]{1,0:T(8,128)(2,1)S(1)} %collective-permute-done.2.cot2_hbm) | copy-start | bytes 1671172
  11.8 12.0 %collective-permute-start.6 = (bf16[544,384]{1,0:T(8,128)(2,1)}, bf16[544,384]{1,0:T(8,128)(2,1)S(1)}, u32[]{:S(2)}, u32[]{:S(2)}) collective-permute-start(bf16[544,384]{1,0:T(8,128)(2,1)} %get-tuple-element.35), channel_id=1, source_target_pairs={{0,8},{8,0},{1,9},{9,1},{2,10},{10,2},{3,11},{11,3},{4,12},{12,4},... | collective-permute-start | bytes 1253384 | tf_op jit(solution)/shard_map/ppermute | solution.py:381
  12.0 16.2 %collective-permute-start.3 = (bf16[288,384]{1,0:T(8,128)(2,1)}, bf16[288,384]{1,0:T(8,128)(2,1)S(1)}, u32[]{:S(2)}, u32[]{:S(2)}) collective-permute-start(bf16[288,384]{1,0:T(8,128)(2,1)} %get-tuple-element.31), channel_id=1, source_target_pairs={{0,2},{2,4},{4,6},{6,0},{1,3},{3,5},{5,7},{7,1},{8,10},{10,12},{12... | collective-permute-start | bytes 663560 | tf_op jit(solution)/shard_map/ppermute | solution.py:351
  13.6 16.9 %collective-permute-start.4 = (bf16[288,384]{1,0:T(8,128)(2,1)}, bf16[288,384]{1,0:T(8,128)(2,1)S(1)}, u32[]{:S(2)}, u32[]{:S(2)}) collective-permute-start(bf16[288,384]{1,0:T(8,128)(2,1)} %get-tuple-element.32), channel_id=1, source_target_pairs={{0,4},{2,6},{4,0},{6,2},{1,5},{3,7},{5,1},{7,3},{8,12},{10,14},{12... | collective-permute-start | bytes 663560 | tf_op jit(solution)/shard_map/ppermute | solution.py:351
  16.3 14.3 %collective-permute-start.5 = (bf16[288,384]{1,0:T(8,128)(2,1)}, bf16[288,384]{1,0:T(8,128)(2,1)S(1)}, u32[]{:S(2)}, u32[]{:S(2)}) collective-permute-start(bf16[288,384]{1,0:T(8,128)(2,1)} %get-tuple-element.33), channel_id=1, source_target_pairs={{0,6},{2,0},{4,2},{6,4},{1,7},{3,1},{5,3},{7,5},{8,14},{10,8},{12,... | collective-permute-start | bytes 663560 | tf_op jit(solution)/shard_map/ppermute | solution.py:351
  17.0 17.9 %all-to-all-start = ((bf16[16,128,128]{2,1,0:T(8,128)(2,1)}), bf16[16,128,128]{2,1,0:T(8,128)(2,1)S(1)}, u32[]{:S(2)}, u32[]{:S(2)}) async-start(bf16[16,128,128]{2,1,0:T(8,128)(2,1)} %get-tuple-element.43), calls=%async_computation | async-start | bytes 1048576 | tf_op jit(solution)/shard_map/all_to_all | solution.py:379
  23.8 1.0 %copy-start.2 = (bf16[544,384]{1,0:T(8,128)(2,1)S(1)}, bf16[544,384]{1,0:T(8,128)(2,1)}, u32[]{:S(2)}) copy-start(bf16[544,384]{1,0:T(8,128)(2,1)} %get-tuple-element.34.own) | copy-start | bytes 1253380
  24.8 5.7 %copy-start.3 = (bf16[288,384]{1,0:T(8,128)(2,1)S(1)}, bf16[288,384]{1,0:T(8,128)(2,1)}, u32[]{:S(2)}) copy-start(bf16[288,384]{1,0:T(8,128)(2,1)} %get-tuple-element.30.m0) | copy-start | bytes 663556
  25.5 13.0 %collective-permute-start.8 = (bf16[144,384]{1,0:T(8,128)(2,1)S(1)}, bf16[144,384]{1,0:T(8,128)(2,1)S(1)}, u32[]{:S(2)}, u32[]{:S(2)}) collective-permute-start(bf16[144,384]{1,0:T(8,128)(2,1)S(1)} %get-tuple-element.39), channel_id=1, source_target_pairs={{0,2},{2,4},{4,6},{6,0},{1,3},{3,5},{5,7},{7,1},{8,10},{10,12},{12... | collective-permute-start | bytes 331784 | tf_op jit(solution)/shard_map/ppermute | solution.py:351
  27.2 11.4 %collective-permute-start.9 = (bf16[144,384]{1,0:T(8,128)(2,1)S(1)}, bf16[144,384]{1,0:T(8,128)(2,1)S(1)}, u32[]{:S(2)}, u32[]{:S(2)}) collective-permute-start(bf16[144,384]{1,0:T(8,128)(2,1)S(1)} %get-tuple-element.40), channel_id=1, source_target_pairs={{0,4},{2,6},{4,0},{6,2},{1,5},{3,7},{5,1},{7,3},{8,12},{10,14},{12... | collective-permute-start | bytes 331784 | tf_op jit(solution)/shard_map/ppermute | solution.py:351
  28.2 10.3 %collective-permute-start.10 = (bf16[144,384]{1,0:T(8,128)(2,1)S(1)}, bf16[144,384]{1,0:T(8,128)(2,1)S(1)}, u32[]{:S(2)}, u32[]{:S(2)}) collective-permute-start(bf16[144,384]{1,0:T(8,128)(2,1)S(1)} %get-tuple-element.41), channel_id=1, source_target_pairs={{0,6},{2,0},{4,2},{6,4},{1,7},{3,1},{5,3},{7,5},{8,14},{10,8},{12,... | collective-permute-start | bytes 331784 | tf_op jit(solution)/shard_map/ppermute | solution.py:351
  30.6 2.7 %copy-start = (s32[2048,1,2]{0,2,1:T(2,128)S(1)}, s32[2048,1,2]{0,2,1:T(2,128)}, u32[]{:S(2)}) copy-start(s32[2048,1,2]{0,2,1:T(2,128)} %param.14) | copy-start | bytes 49156
  30.6 2.7 %copy-start.1 = (s32[1,1,2048]{2,1,0:T(1,128)S(1)}, s32[1,1,2048]{2,1,0:T(1,128)}, u32[]{:S(2)}) copy-start(s32[1,1,2048]{2,1,0:T(1,128)} %param.15) | copy-start | bytes 24580
  31.0 7.6 %collective-permute-start.7 = (bf16[160,384]{1,0:T(8,128)(2,1)S(1)}, bf16[160,384]{1,0:T(8,128)(2,1)S(1)}, u32[]{:S(2)}, u32[]{:S(2)}) collective-permute-start(bf16[160,384]{1,0:T(8,128)(2,1)S(1)} %get-tuple-element.38), channel_id=1, source_target_pairs={{0,8},{8,0},{1,9},{9,1},{2,10},{10,2},{3,11},{11,3},{4,12},{12,4},... | collective-permute-start | bytes 368648 | tf_op jit(solution)/shard_map/ppermute | solution.py:411
  39.1 11.7 %collective-permute-start.11 = (bf16[208,384]{1,0:T(8,128)(2,1)S(1)}, bf16[208,384]{1,0:T(8,128)(2,1)S(1)}, u32[]{:S(2)}, u32[]{:S(2)}) collective-permute-start(bf16[208,384]{1,0:T(8,128)(2,1)S(1)} %get-tuple-element.46), channel_id=1, source_target_pairs={{0,64},{64,0},{128,192},{192,128},{1,65},{65,1},{129,193},{193,129... | collective-permute-start | bytes 479240 | tf_op jit(solution)/shard_map/ppermute | solution.py:423
  42.5 30.6 %all-to-all-start.1 = ((bf16[16,176,128]{2,1,0:T(8,128)(2,1)}), bf16[16,176,128]{2,1,0:T(8,128)(2,1)S(1)}, u32[]{:S(2)}, u32[]{:S(2)}) async-start(bf16[16,176,128]{2,1,0:T(8,128)(2,1)} %shard_map.115._), calls=%async_computation.1 | async-start | bytes 1441792 | tf_op jit(solution)/shard_map/all_to_all | solution.py:426
  51.0 6.1 %collective-permute-start.12 = (bf16[112,384]{1,0:T(8,128)(2,1)S(1)}, bf16[112,384]{1,0:T(8,128)(2,1)S(1)}, u32[]{:S(2)}, u32[]{:S(2)}) collective-permute-start(bf16[112,384]{1,0:T(8,128)(2,1)S(1)} %get-tuple-element.48), channel_id=1, source_target_pairs={{0,16},{16,0},{32,48},{48,32},{1,17},{17,1},{33,49},{49,33},{2,18}... | collective-permute-start | bytes 258056 | tf_op jit(solution)/shard_map/ppermute | solution.py:423
  57.3 6.9 %collective-permute-start.13 = (bf16[64,384]{1,0:T(8,128)(2,1)S(1)}, bf16[64,384]{1,0:T(8,128)(2,1)S(1)}, u32[]{:S(2)}, u32[]{:S(2)}) collective-permute-start(bf16[64,384]{1,0:T(8,128)(2,1)S(1)} %get-tuple-element.50), channel_id=1, source_target_pairs={{0,48},{48,0},{16,32},{32,16},{1,49},{49,1},{17,33},{33,17},{2,50}... | collective-permute-start | bytes 147464 | tf_op jit(solution)/shard_map/ppermute | solution.py:423
  64.2 7.7 %collective-permute-start.14 = (bf16[48,384]{1,0:T(8,128)(2,1)S(1)}, bf16[48,384]{1,0:T(8,128)(2,1)S(1)}, u32[]{:S(2)}, u32[]{:S(2)}) collective-permute-start(bf16[48,384]{1,0:T(8,128)(2,1)S(1)} %get-tuple-element.52), channel_id=1, source_target_pairs={{0,192},{192,0},{64,128},{128,64},{1,193},{193,1},{65,129},{129,65... | collective-permute-start | bytes 110600 | tf_op jit(solution)/shard_map/ppermute | solution.py:423

commit v6 on v5

--- a/solution.py
+++ b/solution.py
@@ -88,13 +88,10 @@
     for load in loads[7:]:
         load.wait()
     gl = nt(mix_ref[...], u_ref[...]).astype(BF)
-    for j in range(D0 // EMB):
-        cols = slice(j * EMB, (j + 1) * EMB)
-        mix = mix_ref[:, cols]
-        feat = dense_ref[...] if j == 0 else pooled_ref[:, (j - 1) * EMB : j * EMB]
-        gu[cols, :] = tn(mix, lat)
-        gv[cols, :] = tn(feat, gl)
-        bias_row[:, cols] = jnp.sum(mix.astype(F32), axis=0, keepdims=True)
+    bias_row[...] = jnp.sum(mix_ref[...].astype(F32), axis=0, keepdims=True)
+    gu[...] = tn(mix_ref[...], lat)
+    gv[:EMB, :] = tn(dense_ref[...], gl)
+    gv[EMB:, :] = tn(pooled_ref[...], gl)
     high = bias_row[...].astype(BF)
     low = (bias_row[...] - high.astype(F32)).astype(BF)
     tail = jnp.zeros((1, 6 * LAT - D0), BF)
@@ -127,13 +124,16 @@
             buffer[i * 272 : (i + 1) * 272, :] = pair.astype(BF)
         leave(buffer, out)
     latent, grad_latent = lat[0:128, :], gl[0:128, :]
-    for t in range(N_TAB):
-        cols = slice(EMB + t * EMB, EMB + (t + 1) * EMB)
-        mixing = nn(latent, u_ref[:, cols]) + bias_ref[t + 1 : t + 2, :]
+    for t in range(0, N_TAB, 2):
+        cols = slice(EMB + t * EMB, EMB + (t + 2) * EMB)
+        bias = jnp.concatenate([bias_ref[t + 1 : t + 2, :], bias_ref[t + 2 : t + 3, :]], axis=1)
+        mixing = nn(latent, u_ref[:, cols]) + bias
         backward = nt(grad_latent, v_ref[cols, :])
-        out_ref[t] = (cot_ref[0:128, cols].astype(F32) * (mixing + 1.0) + backward).astype(BF)
-        if t % 4 == 3:
-            some = slice(t - 3, t + 1)
+        grads = (cot_ref[0:128, cols].astype(F32) * (mixing + 1.0) + backward).astype(BF)
+        out_ref[t] = grads[:, :EMB]
+        out_ref[t + 1] = grads[:, EMB:]
+        if t % 4 == 2:
+            some = slice(t - 2, t + 2)
             copy = pltpu.make_async_copy(out_ref.at[some], out_hbm.at[some], out_sems.at[t // 4])
             copy.start()
             copies.append(copy)
@@ -247,16 +247,15 @@
         lax.broadcasted_iota(jnp.int32, (128, 128), 0) <= lax.broadcasted_iota(jnp.int32, (128, 128), 1)
     ).astype(F32).astype(BF)
     which = lax.broadcasted_iota(jnp.int32, (N_REP, 128), 0)
+    blocks = [keeper[:, b * 128 : (b + 1) * 128] for b in range(UNIQ // 128)]
+    members = [(which == own).astype(F32) for own in blocks]
+    running = nn(jnp.concatenate(members, axis=0).astype(BF), upper)
     carry = jnp.zeros((N_REP, 1), F32)
-    members, ranks, keepers = [], [], []
-    for b in range(UNIQ // 128):
-        own = keeper[:, b * 128 : (b + 1) * 128]
-        member = (which == own).astype(F32)
-        running = nn(member.astype(BF), upper) + carry
-        carry = running[:, 127:128]
-        members.append(member)
-        keepers.append(own.astype(F32))
-        ranks.append(jnp.sum(member * (running - 1.0), axis=0, keepdims=True))
+    ranks, keepers = [], [own.astype(F32) for own in blocks]
+    for b, member in enumerate(members):
+        inside = running[b * N_REP : (b + 1) * N_REP, :]
+        ranks.append(jnp.sum(member * (inside + (carry - 1.0)), axis=0, keepdims=True))
+        carry = carry + inside[:, 127:128]
     member = jnp.concatenate(members, axis=1)
     rank = jnp.concatenate(ranks, axis=1)
     row_high = lax.shift_right_logical(row, 8).astype(F32)
@@ -292,9 +291,9 @@
     places = lax.broadcasted_iota(jnp.int32, (CAP, SAMP), 0).astype(F32).astype(BF)
     one, zero = jnp.ones((CAP, SAMP), BF), jnp.zeros((CAP, SAMP), BF)
     stores = []
-    for j in range(4):
-        for i in range(4):
-            k = j * 4 + i
+    for j in range(2):
+        for i in range(8):
+            k = j * 8 + i
             hits = []
             for p in range(2):
                 at, kept = found_ref[2 * p : 2 * p + 1, :], found_ref[2 * p + 1 : 2 * p + 2, :]
@@ -302,11 +301,11 @@
                 hits.append(jnp.where(places == own, one, zero))
             hot[j % 2, i * CAP : (i + 1) * CAP, :] = hits[0] + hits[1]
         sums = nn(hot[j % 2], got_ref[...]).astype(BF)
-        for i in range(4):
-            k = j * 4 + i
+        for i in range(8):
+            k = j * 8 + i
             out_ref[k, 0:CAP, :] = sums[i * CAP : (i + 1) * CAP, :]
             out_ref[k, CAP:PAYLOAD, :] = pos_ref[k]
-        some = slice(j * 4, j * 4 + 4)
+        some = slice(j * 8, j * 8 + 8)
         store = pltpu.make_async_copy(out_ref.at[some], out_hbm.at[some], sems.at[j])
         store.start()
         stores.append(store)
@@ -405,7 +404,7 @@
         rows_kernel,
         [(HBM, (N_REP, PAYLOAD, EMB), BF)],
         near(found, received, pos) + [(ANY, u_keep)],
-        [pltpu.VMEM((2, 4 * CAP, SAMP), BF), pltpu.VMEM((N_REP, PAYLOAD, EMB), BF), dma((4,))],
+        [pltpu.VMEM((2, 8 * CAP, SAMP), BF), pltpu.VMEM((N_REP, PAYLOAD, EMB), BF), dma((2,))],
         us=7,
     )
     u_got = lax.ppermute(u_send, "zl", swap)

time: 76.1 us -> 75.8 us (level)
  Pallas kernels: 16.9 us -> 15.6 us
  starting transfers between devices: 38.5 us -> 39.4 us
  waiting for transfers between devices: 16.8 us -> 17.6 us
    pallas_call x11, Pallas kernels: 16.9 us -> 15.6 us  [call(): pl.pallas_call(kernel, out_shape=tuple((jax.ShapeDtypeStruct(s, d) for _,...]
    ppermute x4, starting transfers between devices: 11 us -> 11.8 us  [halve(): return (kept, lax.ppermute(sent, axis, pairs))]
  transfers between devices with their start and end apart: 17 -> 17, of which waited for: 7 -> 6; matrix products, arithmetic and copies ran while one was open for 0% -> 0% of each run, Pallas kernels for 10% -> 9%
where the time goes in v6:
time: 75.8 us; the launch traced here: 75.4 us
  starting transfers between devices  39.4 us (52%)
  waiting for transfers between devices  17.6 us (23%)
  Pallas kernels  15.6 us (21%)
  local copies, waits for them, and re-layouts  2 us (3%)
  between operations  0.8 us (1%)
    pallas_call x11, Pallas kernels, call(): pl.pallas_call(kernel, out_shape=tuple((jax.ShapeDtypeStruct(s, d) for _,...  15.6 us
    ppermute x4, waiting for transfers between devices, halve(): return (kept, lax.ppermute(sent, axis, pairs))  13.2 us
    ppermute x4, starting transfers between devices, halve(): return (kept, lax.ppermute(sent, axis, pairs))  11.8 us
    ppermute x6, starting transfers between devices, shifted(): lax.ppermute(messages[s - 1], axis, [(i, (i + s) % 4) for i in range(4)])  9.93 us
    all_to_all x1, starting transfers between devices, shards(): gathered = lax.all_to_all(payload, REP, 0, 0, tiled=True)  8.33 us
    all_to_all x1, starting transfers between devices, shards(): lax.all_to_all(outgoing, TABLE, 0, 0, tiled=True).reshape(SAMP, EMB)  6.14 us
    ppermute x3, waiting for transfers between devices, shards(): other = [lax.ppermute(a, 'c', swap) for a in (dense, pooled, cot)]  2.36 us
    ppermute x1, starting transfers between devices, shards(): u_got = lax.ppermute(u_send, 'zl', swap)  2.27 us
  transfers between devices with their start and end apart: 17, of which 6 were waited for; matrix products, arithmetic and copies ran while one was open for 0% of the time, Pallas kernels for 9%

profile of v6, /device:TPU:40, one launch (start us, length us, event | category | flops | bytes accessed | tf_op | source)
XLA Modules:
  0.0 75.4 jit_solution(16376925430257377230)
XLA Ops:
  0.7 0.5 collective-permute-start
  1.3 2.4 %collective-permute-done.1.dense2_hbm = bf16[128,128]{1,0:T(8,128)(2,1)S(1)} collective-permute-done((bf16[128,128]{1,0:T(8,128)(2,1)}, bf16[128,128]{1,0:T(8,128)(2,1)S(1)}, u32[]{:S(2)}, u32[]{:S(2)}) %collective-permute-start.1) | collective-permute-done | bytes 32800 | tf_op jit(solution)/shard_map/ppermute | solution.py:358
  3.7 0.6 copy-done.6
  4.3 0.2 copy-done.5
  4.7 6.6 %shard_map.111 = (bf16[288,384]{1,0:T(8,128)(2,1)}, bf16[288,384]{1,0:T(8,128)(2,1)}, bf16[288,384]{1,0:T(8,128)(2,1)}, bf16[288,384]{1,0:T(8,128)(2,1)}, bf16[5...) custom-call(s32[1]{0:T(128)} %bitcast.place_ref._, bf16[128,2048]{1,0:T(8,128)(2,1)} %pooled_hbm.1, ...), custom_call_target="tpu_custom_call" | custom-call | flops 8000000000 | bytes 8000000 | tf_op jit(solution)/shard_map/pallas_call | solution.py:332
  11.3 0.2 collective-permute-start.6
  11.5 1.6 %collective-permute-start.3 = (bf16[288,384]{1,0:T(8,128)(2,1)}, bf16[288,384]{1,0:T(8,128)(2,1)S(1)}, u32[]{:S(2)}, u32[]{:S(2)}) collective-permute-start(bf16[288,384]{1,0:T(8,128)(2,1)} %get-tuple-element.31), channel_id=1, source_target_pairs={{0,2},{2,4},{4,6},{6,0},{1,3},{3,5},{5,7},{7,1},{8,10},{10,12},{12... | collective-permute-start | bytes 663560 | tf_op jit(solution)/shard_map/ppermute | solution.py:350
  13.1 2.7 %collective-permute-start.4 = (bf16[288,384]{1,0:T(8,128)(2,1)}, bf16[288,384]{1,0:T(8,128)(2,1)S(1)}, u32[]{:S(2)}, u32[]{:S(2)}) collective-permute-start(bf16[288,384]{1,0:T(8,128)(2,1)} %get-tuple-element.32), channel_id=1, source_target_pairs={{0,4},{2,6},{4,0},{6,2},{1,5},{3,7},{5,1},{7,3},{8,12},{10,14},{12... | collective-permute-start | bytes 663560 | tf_op jit(solution)/shard_map/ppermute | solution.py:350
  15.8 0.7 collective-permute-start.5
  16.4 6.1 %all-to-all-start = ((bf16[16,128,128]{2,1,0:T(8,128)(2,1)}), bf16[16,128,128]{2,1,0:T(8,128)(2,1)S(1)}, u32[]{:S(2)}, u32[]{:S(2)}) async-start(bf16[16,128,128]{2,1,0:T(8,128)(2,1)} %get-tuple-element.43), calls=%async_computation | async-start | bytes 1048576 | tf_op jit(solution)/shard_map/all_to_all | solution.py:378
  22.6 0.8 %collective-permute-done.6.got = bf16[544,384]{1,0:T(8,128)(2,1)S(1)} collective-permute-done((bf16[544,384]{1,0:T(8,128)(2,1)}, bf16[544,384]{1,0:T(8,128)(2,1)S(1)}, u32[]{:S(2)}, u32[]{:S(2)}) %collective-permute-start.6) | collective-permute-done | bytes 417824 | tf_op jit(solution)/shard_map/ppermute | solution.py:380
  23.3 1.0 %copy-done.2 = bf16[544,384]{1,0:T(8,128)(2,1)S(1)} copy-done((bf16[544,384]{1,0:T(8,128)(2,1)S(1)}, bf16[544,384]{1,0:T(8,128)(2,1)}, u32[]{:S(2)}) %copy-start.2) | copy-done | bytes 417816
  24.3 0.7 shard_map.112
  25.0 1.6 %collective-permute-start.8 = (bf16[144,384]{1,0:T(8,128)(2,1)S(1)}, bf16[144,384]{1,0:T(8,128)(2,1)S(1)}, u32[]{:S(2)}, u32[]{:S(2)}) collective-permute-start(bf16[144,384]{1,0:T(8,128)(2,1)S(1)} %get-tuple-element.39), channel_id=1, source_target_pairs={{0,2},{2,4},{4,6},{6,0},{1,3},{3,5},{5,7},{7,1},{8,10},{10,12},{12... | collective-permute-start | bytes 331784 | tf_op jit(solution)/shard_map/ppermute | solution.py:350
  26.7 1.0 %collective-permute-start.9 = (bf16[144,384]{1,0:T(8,128)(2,1)S(1)}, bf16[144,384]{1,0:T(8,128)(2,1)S(1)}, u32[]{:S(2)}, u32[]{:S(2)}) collective-permute-start(bf16[144,384]{1,0:T(8,128)(2,1)S(1)} %get-tuple-element.40), channel_id=1, source_target_pairs={{0,4},{2,6},{4,0},{6,2},{1,5},{3,7},{5,1},{7,3},{8,12},{10,14},{12... | collective-permute-start | bytes 331784 | tf_op jit(solution)/shard_map/ppermute | solution.py:350
  27.7 2.3 %collective-permute-start.10 = (bf16[144,384]{1,0:T(8,128)(2,1)S(1)}, bf16[144,384]{1,0:T(8,128)(2,1)S(1)}, u32[]{:S(2)}, u32[]{:S(2)}) collective-permute-start(bf16[144,384]{1,0:T(8,128)(2,1)S(1)} %get-tuple-element.41), channel_id=1, source_target_pairs={{0,6},{2,0},{4,2},{6,4},{1,7},{3,1},{5,3},{7,5},{8,14},{10,8},{12,... | collective-permute-start | bytes 331784 | tf_op jit(solution)/shard_map/ppermute | solution.py:350
  30.1 0.4 shard_map.113
  30.5 2.3 %collective-permute-start.7 = (bf16[160,384]{1,0:T(8,128)(2,1)S(1)}, bf16[160,384]{1,0:T(8,128)(2,1)S(1)}, u32[]{:S(2)}, u32[]{:S(2)}) collective-permute-start(bf16[160,384]{1,0:T(8,128)(2,1)S(1)} %get-tuple-element.38), channel_id=1, source_target_pairs={{0,8},{8,0},{1,9},{9,1},{2,10},{10,2},{3,11},{11,3},{4,12},{12,4},... | collective-permute-start | bytes 368648 | tf_op jit(solution)/shard_map/ppermute | solution.py:410
  32.8 0.7 shard_map.114
  33.5 3.8 %shard_map.115._ = bf16[16,176,128]{2,1,0:T(8,128)(2,1)} custom-call(f32[8,2048]{1,0:T(8,128)S(1)} %get-tuple-element.42.found_ref, bf16[2048,128]{1,0:T(8,128)(2,1)S(1)} %bitcast.10, bf16[16,16,128]{2,1,0:T(8,128)(2,1)S(1)} %get-tuple-element.44.pos_ref, f32[160,384]{1,0:T(8,128)S(1)} %get-tuple-element.37._.u_keep), custom_call_target="tpu_custom_call" | custom-call | flops 7000000000 | bytes 7000000 | tf_op jit(solution)/shard_map/pallas_call | solution.py:332
  37.3 0.5 shard_map.116
  37.8 3.4 %collective-permute-start.11 = (bf16[208,384]{1,0:T(8,128)(2,1)S(1)}, bf16[208,384]{1,0:T(8,128)(2,1)S(1)}, u32[]{:S(2)}, u32[]{:S(2)}) collective-permute-start(bf16[208,384]{1,0:T(8,128)(2,1)S(1)} %get-tuple-element.46), channel_id=1, source_target_pairs={{0,64},{64,0},{128,192},{192,128},{1,65},{65,1},{129,193},{193,129... | collective-permute-start | bytes 479240 | tf_op jit(solution)/shard_map/ppermute | solution.py:422
  41.2 8.3 %all-to-all-start.1 = ((bf16[16,176,128]{2,1,0:T(8,128)(2,1)}), bf16[16,176,128]{2,1,0:T(8,128)(2,1)S(1)}, u32[]{:S(2)}, u32[]{:S(2)}) async-start(bf16[16,176,128]{2,1,0:T(8,128)(2,1)} %shard_map.115._), calls=%async_computation.1 | async-start | bytes 1441792 | tf_op jit(solution)/shard_map/all_to_all | solution.py:425
  49.7 2.0 %collective-permute-start.12 = (bf16[112,384]{1,0:T(8,128)(2,1)S(1)}, bf16[112,384]{1,0:T(8,128)(2,1)S(1)}, u32[]{:S(2)}, u32[]{:S(2)}) collective-permute-start(bf16[112,384]{1,0:T(8,128)(2,1)S(1)} %get-tuple-element.48), channel_id=1, source_target_pairs={{0,16},{16,0},{32,48},{48,32},{1,17},{17,1},{33,49},{49,33},{2,18}... | collective-permute-start | bytes 258056 | tf_op jit(solution)/shard_map/ppermute | solution.py:422
  51.8 4.5 %collective-permute-done.12.got = bf16[112,384]{1,0:T(8,128)(2,1)S(1)} collective-permute-done((bf16[112,384]{1,0:T(8,128)(2,1)S(1)}, bf16[112,384]{1,0:T(8,128)(2,1)S(1)}, u32[]{:S(2)}, u32[]{:S(2)}) %collective-permute-start.12) | collective-permute-done | bytes 86048 | tf_op jit(solution)/shard_map/ppermute | solution.py:422
  56.4 2.6 %collective-permute-start.13 = (bf16[64,384]{1,0:T(8,128)(2,1)S(1)}, bf16[64,384]{1,0:T(8,128)(2,1)S(1)}, u32[]{:S(2)}, u32[]{:S(2)}) collective-permute-start(bf16[64,384]{1,0:T(8,128)(2,1)S(1)} %get-tuple-element.50), channel_id=1, source_target_pairs={{0,48},{48,0},{16,32},{32,16},{1,49},{49,1},{17,33},{33,17},{2,50}... | collective-permute-start | bytes 147464 | tf_op jit(solution)/shard_map/ppermute | solution.py:422
  58.9 3.5 %collective-permute-done.13.got = bf16[64,384]{1,0:T(8,128)(2,1)S(1)} collective-permute-done((bf16[64,384]{1,0:T(8,128)(2,1)S(1)}, bf16[64,384]{1,0:T(8,128)(2,1)S(1)}, u32[]{:S(2)}, u32[]{:S(2)}) %collective-permute-start.13) | collective-permute-done | bytes 49184 | tf_op jit(solution)/shard_map/ppermute | solution.py:422
  62.5 3.9 %collective-permute-start.14 = (bf16[48,384]{1,0:T(8,128)(2,1)S(1)}, bf16[48,384]{1,0:T(8,128)(2,1)S(1)}, u32[]{:S(2)}, u32[]{:S(2)}) collective-permute-start(bf16[48,384]{1,0:T(8,128)(2,1)S(1)} %get-tuple-element.52), channel_id=1, source_target_pairs={{0,192},{192,0},{64,128},{128,64},{1,193},{193,1},{65,129},{129,65... | collective-permute-start | bytes 110600 | tf_op jit(solution)/shard_map/ppermute | solution.py:422
  66.4 5.2 %collective-permute-done.14.got = bf16[48,384]{1,0:T(8,128)(2,1)S(1)} collective-permute-done((bf16[48,384]{1,0:T(8,128)(2,1)S(1)}, bf16[48,384]{1,0:T(8,128)(2,1)S(1)}, u32[]{:S(2)}, u32[]{:S(2)}) %collective-permute-start.14) | collective-permute-done | bytes 36896 | tf_op jit(solution)/shard_map/ppermute | solution.py:422
  71.6 0.7 shard_map.120
  72.2 1.2 %all-to-all-done.1.got_ref = bf16[16,176,128]{2,1,0:T(8,128)(2,1)S(1)} async-done(((bf16[16,176,128]{2,1,0:T(8,128)(2,1)}), bf16[16,176,128]{2,1,0:T(8,128)(2,1)S(1)}, u32[]{:S(2)}, u32[]{:S(2)}) %all-to-all-start.1) | async-done | bytes 720928 | tf_op jit(solution)/shard_map/all_to_all | solution.py:425
  73.5 1.9 %shard_map.121 = f32[512,128]{1,0:T(8,128)} custom-call(bf16[16,176,128]{2,1,0:T(8,128)(2,1)S(1)} %all-to-all-done.1.got_ref), custom_call_target="tpu_custom_call" | custom-call | flops 2000000000 | bytes 2000000 | tf_op jit(solution)/shard_map/pallas_call | solution.py:332
  (27 shorter events, 0.8 us)
Async XLA Ops:
  0.6 3.1 %collective-permute-start.2 = (bf16[128,2176]{1,0:T(8,128)(2,1)}, bf16[128,2176]{1,0:T(8,128)(2,1)S(1)}, u32[]{:S(2)}, u32[]{:S(2)}) collective-permute-start(bf16[128,2176]{1,0:T(8,128)(2,1)} %cot_hbm.1), channel_id=1, source_target_pairs={{0,1},{1,0},{2,3},{3,2},{4,5},{5,4},{6,7},{7,6},{8,9},{9,8},{10,11... | collective-permute-start | bytes 1671176 | tf_op jit(solution)/shard_map/ppermute | solution.py:358
  0.7 3.0 %collective-permute-start = (bf16[128,2048]{1,0:T(8,128)(2,1)}, bf16[128,2048]{1,0:T(8,128)(2,1)S(1)}, u32[]{:S(2)}, u32[]{:S(2)}) collective-permute-start(bf16[128,2048]{1,0:T(8,128)(2,1)} %pooled_hbm.1), channel_id=1, source_target_pairs={{0,1},{1,0},{2,3},{3,2},{4,5},{5,4},{6,7},{7,6},{8,9},{9,8},{10,11... | collective-permute-start | bytes 1572872 | tf_op jit(solution)/shard_map/ppermute | solution.py:358
  1.2 2.5 %collective-permute-start.1 = (bf16[128,128]{1,0:T(8,128)(2,1)}, bf16[128,128]{1,0:T(8,128)(2,1)S(1)}, u32[]{:S(2)}, u32[]{:S(2)}) collective-permute-start(bf16[128,128]{1,0:T(8,128)(2,1)} %dense_hbm.1), channel_id=1, source_target_pairs={{0,1},{1,0},{2,3},{3,2},{4,5},{5,4},{6,7},{7,6},{8,9},{9,8},{10,11... | collective-permute-start | bytes 98312 | tf_op jit(solution)/shard_map/ppermute | solution.py:358
  3.7 0.6 copy-start.6
  3.7 0.8 %copy-start.5 = (bf16[128,2048]{1,0:T(8,128)(2,1)}, bf16[128,2048]{1,0:T(8,128)(2,1)S(1)}, u32[]{:S(2)}) copy-start(bf16[128,2048]{1,0:T(8,128)(2,1)S(1)} %collective-permute-done.pooled2_hbm) | copy-start | bytes 1572868
  3.7 1.0 %copy-start.4 = (bf16[128,2176]{1,0:T(8,128)(2,1)}, bf16[128,2176]{1,0:T(8,128)(2,1)S(1)}, u32[]{:S(2)}) copy-start(bf16[128,2176]{1,0:T(8,128)(2,1)S(1)} %collective-permute-done.2.cot2_hbm) | copy-start | bytes 1671172
  11.3 12.0 %collective-permute-start.6 = (bf16[544,384]{1,0:T(8,128)(2,1)}, bf16[544,384]{1,0:T(8,128)(2,1)S(1)}, u32[]{:S(2)}, u32[]{:S(2)}) collective-permute-start(bf16[544,384]{1,0:T(8,128)(2,1)} %get-tuple-element.35), channel_id=1, source_target_pairs={{0,8},{8,0},{1,9},{9,1},{2,10},{10,2},{3,11},{11,3},{4,12},{12,4},... | collective-permute-start | bytes 1253384 | tf_op jit(solution)/shard_map/ppermute | solution.py:380
  11.5 16.2 %collective-permute-start.3 = (bf16[288,384]{1,0:T(8,128)(2,1)}, bf16[288,384]{1,0:T(8,128)(2,1)S(1)}, u32[]{:S(2)}, u32[]{:S(2)}) collective-permute-start(bf16[288,384]{1,0:T(8,128)(2,1)} %get-tuple-element.31), channel_id=1, source_target_pairs={{0,2},{2,4},{4,6},{6,0},{1,3},{3,5},{5,7},{7,1},{8,10},{10,12},{12... | collective-permute-start | bytes 663560 | tf_op jit(solution)/shard_map/ppermute | solution.py:350
  13.1 16.9 %collective-permute-start.4 = (bf16[288,384]{1,0:T(8,128)(2,1)}, bf16[288,384]{1,0:T(8,128)(2,1)S(1)}, u32[]{:S(2)}, u32[]{:S(2)}) collective-permute-start(bf16[288,384]{1,0:T(8,128)(2,1)} %get-tuple-element.32), channel_id=1, source_target_pairs={{0,4},{2,6},{4,0},{6,2},{1,5},{3,7},{5,1},{7,3},{8,12},{10,14},{12... | collective-permute-start | bytes 663560 | tf_op jit(solution)/shard_map/ppermute | solution.py:350
  15.8 14.3 %collective-permute-start.5 = (bf16[288,384]{1,0:T(8,128)(2,1)}, bf16[288,384]{1,0:T(8,128)(2,1)S(1)}, u32[]{:S(2)}, u32[]{:S(2)}) collective-permute-start(bf16[288,384]{1,0:T(8,128)(2,1)} %get-tuple-element.33), channel_id=1, source_target_pairs={{0,6},{2,0},{4,2},{6,4},{1,7},{3,1},{5,3},{7,5},{8,14},{10,8},{12,... | collective-permute-start | bytes 663560 | tf_op jit(solution)/shard_map/ppermute | solution.py:350
  16.4 17.0 %all-to-all-start = ((bf16[16,128,128]{2,1,0:T(8,128)(2,1)}), bf16[16,128,128]{2,1,0:T(8,128)(2,1)S(1)}, u32[]{:S(2)}, u32[]{:S(2)}) async-start(bf16[16,128,128]{2,1,0:T(8,128)(2,1)} %get-tuple-element.43), calls=%async_computation | async-start | bytes 1048576 | tf_op jit(solution)/shard_map/all_to_all | solution.py:378
  23.3 1.0 %copy-start.2 = (bf16[544,384]{1,0:T(8,128)(2,1)S(1)}, bf16[544,384]{1,0:T(8,128)(2,1)}, u32[]{:S(2)}) copy-start(bf16[544,384]{1,0:T(8,128)(2,1)} %get-tuple-element.34.own) | copy-start | bytes 1253380
  24.3 5.7 %copy-start.3 = (bf16[288,384]{1,0:T(8,128)(2,1)S(1)}, bf16[288,384]{1,0:T(8,128)(2,1)}, u32[]{:S(2)}) copy-start(bf16[288,384]{1,0:T(8,128)(2,1)} %get-tuple-element.30.m0) | copy-start | bytes 663556
  25.0 12.2 %collective-permute-start.8 = (bf16[144,384]{1,0:T(8,128)(2,1)S(1)}, bf16[144,384]{1,0:T(8,128)(2,1)S(1)}, u32[]{:S(2)}, u32[]{:S(2)}) collective-permute-start(bf16[144,384]{1,0:T(8,128)(2,1)S(1)} %get-tuple-element.39), channel_id=1, source_target_pairs={{0,2},{2,4},{4,6},{6,0},{1,3},{3,5},{5,7},{7,1},{8,10},{10,12},{12... | collective-permute-start | bytes 331784 | tf_op jit(solution)/shard_map/ppermute | solution.py:350
  26.7 10.6 %collective-permute-start.9 = (bf16[144,384]{1,0:T(8,128)(2,1)S(1)}, bf16[144,384]{1,0:T(8,128)(2,1)S(1)}, u32[]{:S(2)}, u32[]{:S(2)}) collective-permute-start(bf16[144,384]{1,0:T(8,128)(2,1)S(1)} %get-tuple-element.40), channel_id=1, source_target_pairs={{0,4},{2,6},{4,0},{6,2},{1,5},{3,7},{5,1},{7,3},{8,12},{10,14},{12... | collective-permute-start | bytes 331784 | tf_op jit(solution)/shard_map/ppermute | solution.py:350
  27.7 9.6 %collective-permute-start.10 = (bf16[144,384]{1,0:T(8,128)(2,1)S(1)}, bf16[144,384]{1,0:T(8,128)(2,1)S(1)}, u32[]{:S(2)}, u32[]{:S(2)}) collective-permute-start(bf16[144,384]{1,0:T(8,128)(2,1)S(1)} %get-tuple-element.41), channel_id=1, source_target_pairs={{0,6},{2,0},{4,2},{6,4},{1,7},{3,1},{5,3},{7,5},{8,14},{10,8},{12,... | collective-permute-start | bytes 331784 | tf_op jit(solution)/shard_map/ppermute | solution.py:350
  30.1 2.7 %copy-start = (s32[2048,1,2]{0,2,1:T(2,128)S(1)}, s32[2048,1,2]{0,2,1:T(2,128)}, u32[]{:S(2)}) copy-start(s32[2048,1,2]{0,2,1:T(2,128)} %param.14) | copy-start | bytes 49156
  30.1 2.7 %copy-start.1 = (s32[1,1,2048]{2,1,0:T(1,128)S(1)}, s32[1,1,2048]{2,1,0:T(1,128)}, u32[]{:S(2)}) copy-start(s32[1,1,2048]{2,1,0:T(1,128)} %param.15) | copy-start | bytes 24580
  30.5 6.8 %collective-permute-start.7 = (bf16[160,384]{1,0:T(8,128)(2,1)S(1)}, bf16[160,384]{1,0:T(8,128)(2,1)S(1)}, u32[]{:S(2)}, u32[]{:S(2)}) collective-permute-start(bf16[160,384]{1,0:T(8,128)(2,1)S(1)} %get-tuple-element.38), channel_id=1, source_target_pairs={{0,8},{8,0},{1,9},{9,1},{2,10},{10,2},{3,11},{11,3},{4,12},{12,4},... | collective-permute-start | bytes 368648 | tf_op jit(solution)/shard_map/ppermute | solution.py:410
  37.8 11.7 %collective-permute-start.11 = (bf16[208,384]{1,0:T(8,128)(2,1)S(1)}, bf16[208,384]{1,0:T(8,128)(2,1)S(1)}, u32[]{:S(2)}, u32[]{:S(2)}) collective-permute-start(bf16[208,384]{1,0:T(8,128)(2,1)S(1)} %get-tuple-element.46), channel_id=1, source_target_pairs={{0,64},{64,0},{128,192},{192,128},{1,65},{65,1},{129,193},{193,129... | collective-permute-start | bytes 479240 | tf_op jit(solution)/shard_map/ppermute | solution.py:422
  41.2 32.2 %all-to-all-start.1 = ((bf16[16,176,128]{2,1,0:T(8,128)(2,1)}), bf16[16,176,128]{2,1,0:T(8,128)(2,1)S(1)}, u32[]{:S(2)}, u32[]{:S(2)}) async-start(bf16[16,176,128]{2,1,0:T(8,128)(2,1)} %shard_map.115._), calls=%async_computation.1 | async-start | bytes 1441792 | tf_op jit(solution)/shard_map/all_to_all | solution.py:425
  49.7 6.5 %collective-permute-start.12 = (bf16[112,384]{1,0:T(8,128)(2,1)S(1)}, bf16[112,384]{1,0:T(8,128)(2,1)S(1)}, u32[]{:S(2)}, u32[]{:S(2)}) collective-permute-start(bf16[112,384]{1,0:T(8,128)(2,1)S(1)} %get-tuple-element.48), channel_id=1, source_target_pairs={{0,16},{16,0},{32,48},{48,32},{1,17},{17,1},{33,49},{49,33},{2,18}... | collective-permute-start | bytes 258056 | tf_op jit(solution)/shard_map/ppermute | solution.py:422
  56.4 6.1 %collective-permute-start.13 = (bf16[64,384]{1,0:T(8,128)(2,1)S(1)}, bf16[64,384]{1,0:T(8,128)(2,1)S(1)}, u32[]{:S(2)}, u32[]{:S(2)}) collective-permute-start(bf16[64,384]{1,0:T(8,128)(2,1)S(1)} %get-tuple-element.50), channel_id=1, source_target_pairs={{0,48},{48,0},{16,32},{32,16},{1,49},{49,1},{17,33},{33,17},{2,50}... | collective-permute-start | bytes 147464 | tf_op jit(solution)/shard_map/ppermute | solution.py:422
  62.5 9.0 %collective-permute-start.14 = (bf16[48,384]{1,0:T(8,128)(2,1)S(1)}, bf16[48,384]{1,0:T(8,128)(2,1)S(1)}, u32[]{:S(2)}, u32[]{:S(2)}) collective-permute-start(bf16[48,384]{1,0:T(8,128)(2,1)S(1)} %get-tuple-element.52), channel_id=1, source_target_pairs={{0,192},{192,0},{64,128},{128,64},{1,193},{193,1},{65,129},{129,65... | collective-permute-start | bytes 110600 | tf_op jit(solution)/shard_map/ppermute | solution.py:422

commit v7 on v6

--- a/solution.py
+++ b/solution.py
@@ -314,18 +314,21 @@
 
 
 def keep_kernel(got_ref, out_ref):
-    names = lax.broadcasted_iota(jnp.int32, (256, CAP), 0).astype(F32).astype(BF)
-    one, zero = jnp.ones((256, CAP), BF), jnp.zeros((256, CAP), BF)
-    accs = [jnp.zeros((256, EMB), F32) for _ in range(2)]
-    for g in range(N_REP):
-        pos = got_ref[g, CAP:PAYLOAD, :].astype(F32)
-        at = [jnp.concatenate([pos[i : i + 1, :], pos[i + 1 : i + 2, 0 : CAP - 128]], axis=1) for i in (0, 2)]
-        for half in range(2):
-            own = jnp.where(at[0] == float(half), at[1], -1.0).astype(BF)
-            hot = jnp.where(names == own, one, zero)
-            accs[half] = accs[half] + nn(hot, got_ref[g, 0:CAP, :])
+    wide = N_REP * PAYLOAD
+    nowhere = jnp.full((1, PAYLOAD - CAP), -1.0, F32)
+    digits = []
+    for i in (0, 2):
+        pieces = []
+        for g in range(N_REP):
+            pos = got_ref[g, CAP:PAYLOAD, :].astype(F32)
+            pieces += [pos[i : i + 1, :], pos[i + 1 : i + 2, 0 : CAP - 128], nowhere]
+        digits.append(jnp.concatenate(pieces, axis=1))
+    got = got_ref[...].reshape(wide, EMB)
+    names = lax.broadcasted_iota(jnp.int32, (256, wide), 0).astype(F32).astype(BF)
+    one, zero = jnp.ones((256, wide), BF), jnp.zeros((256, wide), BF)
     for half in range(2):
-        out_ref[half * 256 : (half + 1) * 256, :] = accs[half]
+        own = jnp.where(digits[0] == float(half), digits[1], -1.0).astype(BF)
+        out_ref[half * 256 : (half + 1) * 256, :] = nn(jnp.where(names == own, one, zero), got)
 
 
 def call(kernel, outs, ins, scratch=(), mib=24, spare=None, us=2):

time: 75.8 us -> 75.5 us (level)
  no operation moved by 1% of the time
where the time goes in v7:
time: 75.5 us; the launch traced here: 75.1 us
  starting transfers between devices  39.4 us (52%)
  waiting for transfers between devices  17.6 us (23%)
  Pallas kernels  15.4 us (20%)
  local copies, waits for them, and re-layouts  2 us (3%)
  between operations  0.8 us (1%)
    pallas_call x11, Pallas kernels, call(): pl.pallas_call(kernel, out_shape=tuple((jax.ShapeDtypeStruct(s, d) for _,...  15.4 us
    ppermute x4, waiting for transfers between devices, halve(): return (kept, lax.ppermute(sent, axis, pairs))  13.2 us
    ppermute x4, starting transfers between devices, halve(): return (kept, lax.ppermute(sent, axis, pairs))  11.8 us
    ppermute x6, starting transfers between devices, shifted(): lax.ppermute(messages[s - 1], axis, [(i, (i + s) % 4) for i in range(4)])  9.93 us
    all_to_all x1, starting transfers between devices, shards(): gathered = lax.all_to_all(payload, REP, 0, 0, tiled=True)  8.33 us
    all_to_all x1, starting transfers between devices, shards(): lax.all_to_all(outgoing, TABLE, 0, 0, tiled=True).reshape(SAMP, EMB)  6.14 us
    ppermute x3, waiting for transfers between devices, shards(): other = [lax.ppermute(a, 'c', swap) for a in (dense, pooled, cot)]  2.36 us
    ppermute x1, starting transfers between devices, shards(): u_got = lax.ppermute(u_send, 'zl', swap)  2.27 us
  transfers between devices with their start and end apart: 17, of which 6 were waited for; matrix products, arithmetic and copies ran while one was open for 0% of the time, Pallas kernels for 9%

profile of v7, /device:TPU:40, one launch (start us, length us, event | category | flops | bytes accessed | tf_op | source)
XLA Modules:
  0.0 75.1 jit_solution(10963819241487450253)
XLA Ops:
  0.7 0.5 collective-permute-start
  1.3 2.4 %collective-permute-done.1.dense2_hbm = bf16[128,128]{1,0:T(8,128)(2,1)S(1)} collective-permute-done((bf16[128,128]{1,0:T(8,128)(2,1)}, bf16[128,128]{1,0:T(8,128)(2,1)S(1)}, u32[]{:S(2)}, u32[]{:S(2)}) %collective-permute-start.1) | collective-permute-done | bytes 32800 | tf_op jit(solution)/shard_map/ppermute | solution.py:361
  3.7 0.6 copy-done.6
  4.3 0.2 copy-done.5
  4.7 6.6 %shard_map.111 = (bf16[288,384]{1,0:T(8,128)(2,1)}, bf16[288,384]{1,0:T(8,128)(2,1)}, bf16[288,384]{1,0:T(8,128)(2,1)}, bf16[288,384]{1,0:T(8,128)(2,1)}, bf16[5...) custom-call(s32[1]{0:T(128)} %bitcast.place_ref._, bf16[128,2048]{1,0:T(8,128)(2,1)} %pooled_hbm.1, ...), custom_call_target="tpu_custom_call" | custom-call | flops 8000000000 | bytes 8000000 | tf_op jit(solution)/shard_map/pallas_call | solution.py:335
  11.3 0.2 collective-permute-start.6
  11.5 1.6 %collective-permute-start.3 = (bf16[288,384]{1,0:T(8,128)(2,1)}, bf16[288,384]{1,0:T(8,128)(2,1)S(1)}, u32[]{:S(2)}, u32[]{:S(2)}) collective-permute-start(bf16[288,384]{1,0:T(8,128)(2,1)} %get-tuple-element.31), channel_id=1, source_target_pairs={{0,2},{2,4},{4,6},{6,0},{1,3},{3,5},{5,7},{7,1},{8,10},{10,12},{12... | collective-permute-start | bytes 663560 | tf_op jit(solution)/shard_map/ppermute | solution.py:353
  13.1 2.7 %collective-permute-start.4 = (bf16[288,384]{1,0:T(8,128)(2,1)}, bf16[288,384]{1,0:T(8,128)(2,1)S(1)}, u32[]{:S(2)}, u32[]{:S(2)}) collective-permute-start(bf16[288,384]{1,0:T(8,128)(2,1)} %get-tuple-element.32), channel_id=1, source_target_pairs={{0,4},{2,6},{4,0},{6,2},{1,5},{3,7},{5,1},{7,3},{8,12},{10,14},{12... | collective-permute-start | bytes 663560 | tf_op jit(solution)/shard_map/ppermute | solution.py:353
  15.8 0.7 collective-permute-start.5
  16.4 6.1 %all-to-all-start = ((bf16[16,128,128]{2,1,0:T(8,128)(2,1)}), bf16[16,128,128]{2,1,0:T(8,128)(2,1)S(1)}, u32[]{:S(2)}, u32[]{:S(2)}) async-start(bf16[16,128,128]{2,1,0:T(8,128)(2,1)} %get-tuple-element.43), calls=%async_computation | async-start | bytes 1048576 | tf_op jit(solution)/shard_map/all_to_all | solution.py:381
  22.6 0.8 %collective-permute-done.6.got = bf16[544,384]{1,0:T(8,128)(2,1)S(1)} collective-permute-done((bf16[544,384]{1,0:T(8,128)(2,1)}, bf16[544,384]{1,0:T(8,128)(2,1)S(1)}, u32[]{:S(2)}, u32[]{:S(2)}) %collective-permute-start.6) | collective-permute-done | bytes 417824 | tf_op jit(solution)/shard_map/ppermute | solution.py:383
  23.3 1.0 %copy-done.2 = bf16[544,384]{1,0:T(8,128)(2,1)S(1)} copy-done((bf16[544,384]{1,0:T(8,128)(2,1)S(1)}, bf16[544,384]{1,0:T(8,128)(2,1)}, u32[]{:S(2)}) %copy-start.2) | copy-done | bytes 417816
  24.3 0.7 shard_map.112
  25.0 1.6 %collective-permute-start.8 = (bf16[144,384]{1,0:T(8,128)(2,1)S(1)}, bf16[144,384]{1,0:T(8,128)(2,1)S(1)}, u32[]{:S(2)}, u32[]{:S(2)}) collective-permute-start(bf16[144,384]{1,0:T(8,128)(2,1)S(1)} %get-tuple-element.39), channel_id=1, source_target_pairs={{0,2},{2,4},{4,6},{6,0},{1,3},{3,5},{5,7},{7,1},{8,10},{10,12},{12... | collective-permute-start | bytes 331784 | tf_op jit(solution)/shard_map/ppermute | solution.py:353
  26.7 1.0 %collective-permute-start.9 = (bf16[144,384]{1,0:T(8,128)(2,1)S(1)}, bf16[144,384]{1,0:T(8,128)(2,1)S(1)}, u32[]{:S(2)}, u32[]{:S(2)}) collective-permute-start(bf16[144,384]{1,0:T(8,128)(2,1)S(1)} %get-tuple-element.40), channel_id=1, source_target_pairs={{0,4},{2,6},{4,0},{6,2},{1,5},{3,7},{5,1},{7,3},{8,12},{10,14},{12... | collective-permute-start | bytes 331784 | tf_op jit(solution)/shard_map/ppermute | solution.py:353
  27.7 2.3 %collective-permute-start.10 = (bf16[144,384]{1,0:T(8,128)(2,1)S(1)}, bf16[144,384]{1,0:T(8,128)(2,1)S(1)}, u32[]{:S(2)}, u32[]{:S(2)}) collective-permute-start(bf16[144,384]{1,0:T(8,128)(2,1)S(1)} %get-tuple-element.41), channel_id=1, source_target_pairs={{0,6},{2,0},{4,2},{6,4},{1,7},{3,1},{5,3},{7,5},{8,14},{10,8},{12,... | collective-permute-start | bytes 331784 | tf_op jit(solution)/shard_map/ppermute | solution.py:353
  30.1 0.4 shard_map.113
  30.5 2.3 %collective-permute-start.7 = (bf16[160,384]{1,0:T(8,128)(2,1)S(1)}, bf16[160,384]{1,0:T(8,128)(2,1)S(1)}, u32[]{:S(2)}, u32[]{:S(2)}) collective-permute-start(bf16[160,384]{1,0:T(8,128)(2,1)S(1)} %get-tuple-element.38), channel_id=1, source_target_pairs={{0,8},{8,0},{1,9},{9,1},{2,10},{10,2},{3,11},{11,3},{4,12},{12,4},... | collective-permute-start | bytes 368648 | tf_op jit(solution)/shard_map/ppermute | solution.py:413
  32.8 0.7 shard_map.114
  33.5 3.8 %shard_map.115._ = bf16[16,176,128]{2,1,0:T(8,128)(2,1)} custom-call(f32[8,2048]{1,0:T(8,128)S(1)} %get-tuple-element.42.found_ref, bf16[2048,128]{1,0:T(8,128)(2,1)S(1)} %bitcast.10, bf16[16,16,128]{2,1,0:T(8,128)(2,1)S(1)} %get-tuple-element.44.pos_ref, f32[160,384]{1,0:T(8,128)S(1)} %get-tuple-element.37._.u_keep), custom_call_target="tpu_custom_call" | custom-call | flops 7000000000 | bytes 7000000 | tf_op jit(solution)/shard_map/pallas_call | solution.py:335
  37.3 0.5 shard_map.116
  37.8 3.4 %collective-permute-start.11 = (bf16[208,384]{1,0:T(8,128)(2,1)S(1)}, bf16[208,384]{1,0:T(8,128)(2,1)S(1)}, u32[]{:S(2)}, u32[]{:S(2)}) collective-permute-start(bf16[208,384]{1,0:T(8,128)(2,1)S(1)} %get-tuple-element.46), channel_id=1, source_target_pairs={{0,64},{64,0},{128,192},{192,128},{1,65},{65,1},{129,193},{193,129... | collective-permute-start | bytes 479240 | tf_op jit(solution)/shard_map/ppermute | solution.py:425
  41.2 8.3 %all-to-all-start.1 = ((bf16[16,176,128]{2,1,0:T(8,128)(2,1)}), bf16[16,176,128]{2,1,0:T(8,128)(2,1)S(1)}, u32[]{:S(2)}, u32[]{:S(2)}) async-start(bf16[16,176,128]{2,1,0:T(8,128)(2,1)} %shard_map.115._), calls=%async_computation.1 | async-start | bytes 1441792 | tf_op jit(solution)/shard_map/all_to_all | solution.py:428
  49.7 2.0 %collective-permute-start.12 = (bf16[112,384]{1,0:T(8,128)(2,1)S(1)}, bf16[112,384]{1,0:T(8,128)(2,1)S(1)}, u32[]{:S(2)}, u32[]{:S(2)}) collective-permute-start(bf16[112,384]{1,0:T(8,128)(2,1)S(1)} %get-tuple-element.48), channel_id=1, source_target_pairs={{0,16},{16,0},{32,48},{48,32},{1,17},{17,1},{33,49},{49,33},{2,18}... | collective-permute-start | bytes 258056 | tf_op jit(solution)/shard_map/ppermute | solution.py:425
  51.8 4.5 %collective-permute-done.12.got = bf16[112,384]{1,0:T(8,128)(2,1)S(1)} collective-permute-done((bf16[112,384]{1,0:T(8,128)(2,1)S(1)}, bf16[112,384]{1,0:T(8,128)(2,1)S(1)}, u32[]{:S(2)}, u32[]{:S(2)}) %collective-permute-start.12) | collective-permute-done | bytes 86048 | tf_op jit(solution)/shard_map/ppermute | solution.py:425
  56.4 2.6 %collective-permute-start.13 = (bf16[64,384]{1,0:T(8,128)(2,1)S(1)}, bf16[64,384]{1,0:T(8,128)(2,1)S(1)}, u32[]{:S(2)}, u32[]{:S(2)}) collective-permute-start(bf16[64,384]{1,0:T(8,128)(2,1)S(1)} %get-tuple-element.50), channel_id=1, source_target_pairs={{0,48},{48,0},{16,32},{32,16},{1,49},{49,1},{17,33},{33,17},{2,50}... | collective-permute-start | bytes 147464 | tf_op jit(solution)/shard_map/ppermute | solution.py:425
  58.9 3.5 %collective-permute-done.13.got = bf16[64,384]{1,0:T(8,128)(2,1)S(1)} collective-permute-done((bf16[64,384]{1,0:T(8,128)(2,1)S(1)}, bf16[64,384]{1,0:T(8,128)(2,1)S(1)}, u32[]{:S(2)}, u32[]{:S(2)}) %collective-permute-start.13) | collective-permute-done | bytes 49184 | tf_op jit(solution)/shard_map/ppermute | solution.py:425
  62.5 3.9 %collective-permute-start.14 = (bf16[48,384]{1,0:T(8,128)(2,1)S(1)}, bf16[48,384]{1,0:T(8,128)(2,1)S(1)}, u32[]{:S(2)}, u32[]{:S(2)}) collective-permute-start(bf16[48,384]{1,0:T(8,128)(2,1)S(1)} %get-tuple-element.52), channel_id=1, source_target_pairs={{0,192},{192,0},{64,128},{128,64},{1,193},{193,1},{65,129},{129,65... | collective-permute-start | bytes 110600 | tf_op jit(solution)/shard_map/ppermute | solution.py:425
  66.4 5.2 %collective-permute-done.14.got = bf16[48,384]{1,0:T(8,128)(2,1)S(1)} collective-permute-done((bf16[48,384]{1,0:T(8,128)(2,1)S(1)}, bf16[48,384]{1,0:T(8,128)(2,1)S(1)}, u32[]{:S(2)}, u32[]{:S(2)}) %collective-permute-start.14) | collective-permute-done | bytes 36896 | tf_op jit(solution)/shard_map/ppermute | solution.py:425
  71.6 0.7 shard_map.120
  72.2 1.2 %all-to-all-done.1.got_ref = bf16[16,176,128]{2,1,0:T(8,128)(2,1)S(1)} async-done(((bf16[16,176,128]{2,1,0:T(8,128)(2,1)}), bf16[16,176,128]{2,1,0:T(8,128)(2,1)S(1)}, u32[]{:S(2)}, u32[]{:S(2)}) %all-to-all-start.1) | async-done | bytes 720928 | tf_op jit(solution)/shard_map/all_to_all | solution.py:428
  73.5 1.7 %shard_map.121 = f32[512,128]{1,0:T(8,128)} custom-call(bf16[16,176,128]{2,1,0:T(8,128)(2,1)S(1)} %all-to-all-done.1.got_ref), custom_call_target="tpu_custom_call" | custom-call | flops 2000000000 | bytes 2000000 | tf_op jit(solution)/shard_map/pallas_call | solution.py:335
  (27 shorter events, 0.8 us)
Async XLA Ops:
  0.6 3.1 %collective-permute-start.2 = (bf16[128,2176]{1,0:T(8,128)(2,1)}, bf16[128,2176]{1,0:T(8,128)(2,1)S(1)}, u32[]{:S(2)}, u32[]{:S(2)}) collective-permute-start(bf16[128,2176]{1,0:T(8,128)(2,1)} %cot_hbm.1), channel_id=1, source_target_pairs={{0,1},{1,0},{2,3},{3,2},{4,5},{5,4},{6,7},{7,6},{8,9},{9,8},{10,11... | collective-permute-start | bytes 1671176 | tf_op jit(solution)/shard_map/ppermute | solution.py:361
  0.7 3.0 %collective-permute-start = (bf16[128,2048]{1,0:T(8,128)(2,1)}, bf16[128,2048]{1,0:T(8,128)(2,1)S(1)}, u32[]{:S(2)}, u32[]{:S(2)}) collective-permute-start(bf16[128,2048]{1,0:T(8,128)(2,1)} %pooled_hbm.1), channel_id=1, source_target_pairs={{0,1},{1,0},{2,3},{3,2},{4,5},{5,4},{6,7},{7,6},{8,9},{9,8},{10,11... | collective-permute-start | bytes 1572872 | tf_op jit(solution)/shard_map/ppermute | solution.py:361
  1.2 2.5 %collective-permute-start.1 = (bf16[128,128]{1,0:T(8,128)(2,1)}, bf16[128,128]{1,0:T(8,128)(2,1)S(1)}, u32[]{:S(2)}, u32[]{:S(2)}) collective-permute-start(bf16[128,128]{1,0:T(8,128)(2,1)} %dense_hbm.1), channel_id=1, source_target_pairs={{0,1},{1,0},{2,3},{3,2},{4,5},{5,4},{6,7},{7,6},{8,9},{9,8},{10,11... | collective-permute-start | bytes 98312 | tf_op jit(solution)/shard_map/ppermute | solution.py:361
  3.7 0.6 copy-start.6
  3.7 0.8 %copy-start.5 = (bf16[128,2048]{1,0:T(8,128)(2,1)}, bf16[128,2048]{1,0:T(8,128)(2,1)S(1)}, u32[]{:S(2)}) copy-start(bf16[128,2048]{1,0:T(8,128)(2,1)S(1)} %collective-permute-done.pooled2_hbm) | copy-start | bytes 1572868
  3.7 1.0 %copy-start.4 = (bf16[128,2176]{1,0:T(8,128)(2,1)}, bf16[128,2176]{1,0:T(8,128)(2,1)S(1)}, u32[]{:S(2)}) copy-start(bf16[128,2176]{1,0:T(8,128)(2,1)S(1)} %collective-permute-done.2.cot2_hbm) | copy-start | bytes 1671172
  11.3 12.0 %collective-permute-start.6 = (bf16[544,384]{1,0:T(8,128)(2,1)}, bf16[544,384]{1,0:T(8,128)(2,1)S(1)}, u32[]{:S(2)}, u32[]{:S(2)}) collective-permute-start(bf16[544,384]{1,0:T(8,128)(2,1)} %get-tuple-element.35), channel_id=1, source_target_pairs={{0,8},{8,0},{1,9},{9,1},{2,10},{10,2},{3,11},{11,3},{4,12},{12,4},... | collective-permute-start | bytes 1253384 | tf_op jit(solution)/shard_map/ppermute | solution.py:383
  11.5 16.2 %collective-permute-start.3 = (bf16[288,384]{1,0:T(8,128)(2,1)}, bf16[288,384]{1,0:T(8,128)(2,1)S(1)}, u32[]{:S(2)}, u32[]{:S(2)}) collective-permute-start(bf16[288,384]{1,0:T(8,128)(2,1)} %get-tuple-element.31), channel_id=1, source_target_pairs={{0,2},{2,4},{4,6},{6,0},{1,3},{3,5},{5,7},{7,1},{8,10},{10,12},{12... | collective-permute-start | bytes 663560 | tf_op jit(solution)/shard_map/ppermute | solution.py:353
  13.1 16.9 %collective-permute-start.4 = (bf16[288,384]{1,0:T(8,128)(2,1)}, bf16[288,384]{1,0:T(8,128)(2,1)S(1)}, u32[]{:S(2)}, u32[]{:S(2)}) collective-permute-start(bf16[288,384]{1,0:T(8,128)(2,1)} %get-tuple-element.32), channel_id=1, source_target_pairs={{0,4},{2,6},{4,0},{6,2},{1,5},{3,7},{5,1},{7,3},{8,12},{10,14},{12... | collective-permute-start | bytes 663560 | tf_op jit(solution)/shard_map/ppermute | solution.py:353
  15.8 14.3 %collective-permute-start.5 = (bf16[288,384]{1,0:T(8,128)(2,1)}, bf16[288,384]{1,0:T(8,128)(2,1)S(1)}, u32[]{:S(2)}, u32[]{:S(2)}) collective-permute-start(bf16[288,384]{1,0:T(8,128)(2,1)} %get-tuple-element.33), channel_id=1, source_target_pairs={{0,6},{2,0},{4,2},{6,4},{1,7},{3,1},{5,3},{7,5},{8,14},{10,8},{12,... | collective-permute-start | bytes 663560 | tf_op jit(solution)/shard_map/ppermute | solution.py:353
  16.4 17.0 %all-to-all-start = ((bf16[16,128,128]{2,1,0:T(8,128)(2,1)}), bf16[16,128,128]{2,1,0:T(8,128)(2,1)S(1)}, u32[]{:S(2)}, u32[]{:S(2)}) async-start(bf16[16,128,128]{2,1,0:T(8,128)(2,1)} %get-tuple-element.43), calls=%async_computation | async-start | bytes 1048576 | tf_op jit(solution)/shard_map/all_to_all | solution.py:381
  23.3 1.0 %copy-start.2 = (bf16[544,384]{1,0:T(8,128)(2,1)S(1)}, bf16[544,384]{1,0:T(8,128)(2,1)}, u32[]{:S(2)}) copy-start(bf16[544,384]{1,0:T(8,128)(2,1)} %get-tuple-element.34.own) | copy-start | bytes 1253380
  24.3 5.7 %copy-start.3 = (bf16[288,384]{1,0:T(8,128)(2,1)S(1)}, bf16[288,384]{1,0:T(8,128)(2,1)}, u32[]{:S(2)}) copy-start(bf16[288,384]{1,0:T(8,128)(2,1)} %get-tuple-element.30.m0) | copy-start | bytes 663556
  25.0 12.2 %collective-permute-start.8 = (bf16[144,384]{1,0:T(8,128)(2,1)S(1)}, bf16[144,384]{1,0:T(8,128)(2,1)S(1)}, u32[]{:S(2)}, u32[]{:S(2)}) collective-permute-start(bf16[144,384]{1,0:T(8,128)(2,1)S(1)} %get-tuple-element.39), channel_id=1, source_target_pairs={{0,2},{2,4},{4,6},{6,0},{1,3},{3,5},{5,7},{7,1},{8,10},{10,12},{12... | collective-permute-start | bytes 331784 | tf_op jit(solution)/shard_map/ppermute | solution.py:353
  26.7 10.6 %collective-permute-start.9 = (bf16[144,384]{1,0:T(8,128)(2,1)S(1)}, bf16[144,384]{1,0:T(8,128)(2,1)S(1)}, u32[]{:S(2)}, u32[]{:S(2)}) collective-permute-start(bf16[144,384]{1,0:T(8,128)(2,1)S(1)} %get-tuple-element.40), channel_id=1, source_target_pairs={{0,4},{2,6},{4,0},{6,2},{1,5},{3,7},{5,1},{7,3},{8,12},{10,14},{12... | collective-permute-start | bytes 331784 | tf_op jit(solution)/shard_map/ppermute | solution.py:353
  27.7 9.6 %collective-permute-start.10 = (bf16[144,384]{1,0:T(8,128)(2,1)S(1)}, bf16[144,384]{1,0:T(8,128)(2,1)S(1)}, u32[]{:S(2)}, u32[]{:S(2)}) collective-permute-start(bf16[144,384]{1,0:T(8,128)(2,1)S(1)} %get-tuple-element.41), channel_id=1, source_target_pairs={{0,6},{2,0},{4,2},{6,4},{1,7},{3,1},{5,3},{7,5},{8,14},{10,8},{12,... | collective-permute-start | bytes 331784 | tf_op jit(solution)/shard_map/ppermute | solution.py:353
  30.1 2.7 %copy-start = (s32[2048,1,2]{0,2,1:T(2,128)S(1)}, s32[2048,1,2]{0,2,1:T(2,128)}, u32[]{:S(2)}) copy-start(s32[2048,1,2]{0,2,1:T(2,128)} %param.14) | copy-start | bytes 49156
  30.1 2.7 %copy-start.1 = (s32[1,1,2048]{2,1,0:T(1,128)S(1)}, s32[1,1,2048]{2,1,0:T(1,128)}, u32[]{:S(2)}) copy-start(s32[1,1,2048]{2,1,0:T(1,128)} %param.15) | copy-start | bytes 24580
  30.5 6.8 %collective-permute-start.7 = (bf16[160,384]{1,0:T(8,128)(2,1)S(1)}, bf16[160,384]{1,0:T(8,128)(2,1)S(1)}, u32[]{:S(2)}, u32[]{:S(2)}) collective-permute-start(bf16[160,384]{1,0:T(8,128)(2,1)S(1)} %get-tuple-element.38), channel_id=1, source_target_pairs={{0,8},{8,0},{1,9},{9,1},{2,10},{10,2},{3,11},{11,3},{4,12},{12,4},... | collective-permute-start | bytes 368648 | tf_op jit(solution)/shard_map/ppermute | solution.py:413
  37.8 11.7 %collective-permute-start.11 = (bf16[208,384]{1,0:T(8,128)(2,1)S(1)}, bf16[208,384]{1,0:T(8,128)(2,1)S(1)}, u32[]{:S(2)}, u32[]{:S(2)}) collective-permute-start(bf16[208,384]{1,0:T(8,128)(2,1)S(1)} %get-tuple-element.46), channel_id=1, source_target_pairs={{0,64},{64,0},{128,192},{192,128},{1,65},{65,1},{129,193},{193,129... | collective-permute-start | bytes 479240 | tf_op jit(solution)/shard_map/ppermute | solution.py:425
  41.2 32.2 %all-to-all-start.1 = ((bf16[16,176,128]{2,1,0:T(8,128)(2,1)}), bf16[16,176,128]{2,1,0:T(8,128)(2,1)S(1)}, u32[]{:S(2)}, u32[]{:S(2)}) async-start(bf16[16,176,128]{2,1,0:T(8,128)(2,1)} %shard_map.115._), calls=%async_computation.1 | async-start | bytes 1441792 | tf_op jit(solution)/shard_map/all_to_all | solution.py:428
  49.7 6.5 %collective-permute-start.12 = (bf16[112,384]{1,0:T(8,128)(2,1)S(1)}, bf16[112,384]{1,0:T(8,128)(2,1)S(1)}, u32[]{:S(2)}, u32[]{:S(2)}) collective-permute-start(bf16[112,384]{1,0:T(8,128)(2,1)S(1)} %get-tuple-element.48), channel_id=1, source_target_pairs={{0,16},{16,0},{32,48},{48,32},{1,17},{17,1},{33,49},{49,33},{2,18}... | collective-permute-start | bytes 258056 | tf_op jit(solution)/shard_map/ppermute | solution.py:425
  56.4 6.1 %collective-permute-start.13 = (bf16[64,384]{1,0:T(8,128)(2,1)S(1)}, bf16[64,384]{1,0:T(8,128)(2,1)S(1)}, u32[]{:S(2)}, u32[]{:S(2)}) collective-permute-start(bf16[64,384]{1,0:T(8,128)(2,1)S(1)} %get-tuple-element.50), channel_id=1, source_target_pairs={{0,48},{48,0},{16,32},{32,16},{1,49},{49,1},{17,33},{33,17},{2,50}... | collective-permute-start | bytes 147464 | tf_op jit(solution)/shard_map/ppermute | solution.py:425
  62.5 9.0 %collective-permute-start.14 = (bf16[48,384]{1,0:T(8,128)(2,1)S(1)}, bf16[48,384]{1,0:T(8,128)(2,1)S(1)}, u32[]{:S(2)}, u32[]{:S(2)}) collective-permute-start(bf16[48,384]{1,0:T(8,128)(2,1)S(1)} %get-tuple-element.52), channel_id=1, source_target_pairs={{0,192},{192,0},{64,128},{128,64},{1,193},{193,1},{65,129},{129,65... | collective-permute-start | bytes 110600 | tf_op jit(solution)/shard_map/ppermute | solution.py:425

commit v8 on v7

--- a/solution.py
+++ b/solution.py
@@ -20,7 +20,7 @@
 KEEP = 512
 CAP = 160
 SLOTS = N_REP * CAP
-PAYLOAD = CAP + 16
+PAYLOAD = CAP + 8
 UNIQ = 2048
 SAMP = 2048
 SCALE = float(32768) ** -0.5
@@ -300,12 +300,14 @@
                 own = jnp.where(kept == float(k), at, -1.0).astype(BF)
                 hits.append(jnp.where(places == own, one, zero))
             hot[j % 2, i * CAP : (i + 1) * CAP, :] = hits[0] + hits[1]
-        sums = nn(hot[j % 2], got_ref[...]).astype(BF)
-        for i in range(8):
-            k = j * 8 + i
-            out_ref[k, 0:CAP, :] = sums[i * CAP : (i + 1) * CAP, :]
-            out_ref[k, CAP:PAYLOAD, :] = pos_ref[k]
-        some = slice(j * 8, j * 8 + 8)
+        sums = nn(hot[j % 2], got_ref[...])
+        for i in range(0, 8, 2):
+            pair = []
+            for k in (i, i + 1):
+                pair += [sums[k * CAP : (k + 1) * CAP, :], pos_ref[j * 8 + k].astype(F32)[0:8, :]]
+            start = (j * 8 + i) * PAYLOAD
+            out_ref[start : start + 2 * PAYLOAD, :] = jnp.concatenate(pair, axis=0).astype(BF)
+        some = slice(j * 8 * PAYLOAD, (j + 1) * 8 * PAYLOAD)
         store = pltpu.make_async_copy(out_ref.at[some], out_hbm.at[some], sems.at[j])
         store.start()
         stores.append(store)
@@ -320,10 +322,11 @@
     for i in (0, 2):
         pieces = []
         for g in range(N_REP):
-            pos = got_ref[g, CAP:PAYLOAD, :].astype(F32)
+            start = g * PAYLOAD + CAP - 8 * (g % 2)
+            pos = got_ref[start : start + 16, :].astype(F32)[8 * (g % 2) : 8 * (g % 2) + 8, :]
             pieces += [pos[i : i + 1, :], pos[i + 1 : i + 2, 0 : CAP - 128], nowhere]
         digits.append(jnp.concatenate(pieces, axis=1))
-    got = got_ref[...].reshape(wide, EMB)
+    got = got_ref[...]
     names = lax.broadcasted_iota(jnp.int32, (256, wide), 0).astype(F32).astype(BF)
     one, zero = jnp.ones((256, wide), BF), jnp.zeros((256, wide), BF)
     for half in range(2):
@@ -405,9 +408,9 @@
     )
     (payload,) = call(
         rows_kernel,
-        [(HBM, (N_REP, PAYLOAD, EMB), BF)],
+        [(HBM, (N_REP * PAYLOAD, EMB), BF)],
         near(found, received, pos) + [(ANY, u_keep)],
-        [pltpu.VMEM((2, 8 * CAP, SAMP), BF), pltpu.VMEM((N_REP, PAYLOAD, EMB), BF), dma((2,))],
+        [pltpu.VMEM((2, 8 * CAP, SAMP), BF), pltpu.VMEM((N_REP * PAYLOAD, EMB), BF), dma((2,))],
         us=7,
     )
     u_got = lax.ppermute(u_send, "zl", swap)

time: 75.5 us -> 74.6 us (0.988)
  waiting for transfers between devices: 17.6 us -> 16.4 us
    ppermute x4, waiting for transfers between devices: 13.2 us -> 12.1 us  [halve(): return (kept, lax.ppermute(sent, axis, pairs))]
where the time goes in v8:
time: 74.6 us; the launch traced here: 74.2 us
  starting transfers between devices  39.7 us (53%)
  waiting for transfers between devices  16.4 us (22%)
  Pallas kernels  15.3 us (21%)
  local copies, waits for them, and re-layouts  2 us (3%)
  between operations  0.8 us (1%)
    pallas_call x11, Pallas kernels, call(): pl.pallas_call(kernel, out_shape=tuple((jax.ShapeDtypeStruct(s, d) for _,...  15.3 us
    ppermute x4, starting transfers between devices, halve(): return (kept, lax.ppermute(sent, axis, pairs))  12.2 us
    ppermute x4, waiting for transfers between devices, halve(): return (kept, lax.ppermute(sent, axis, pairs))  12.1 us
    ppermute x6, starting transfers between devices, shifted(): lax.ppermute(messages[s - 1], axis, [(i, (i + s) % 4) for i in range(4)])  9.93 us
    all_to_all x1, starting transfers between devices, shards(): gathered = lax.all_to_all(payload, REP, 0, 0, tiled=True)  8.33 us
    all_to_all x1, starting transfers between devices, shards(): lax.all_to_all(outgoing, TABLE, 0, 0, tiled=True).reshape(SAMP, EMB)  6.14 us
    ppermute x3, waiting for transfers between devices, shards(): other = [lax.ppermute(a, 'c', swap) for a in (dense, pooled, cot)]  2.36 us
    ppermute x1, starting transfers between devices, shards(): u_got = lax.ppermute(u_send, 'zl', swap)  2.27 us
  transfers between devices with their start and end apart: 17, of which 6 were waited for; matrix products, arithmetic and copies ran while one was open for 0% of the time, Pallas kernels for 9%

profile of v8, /device:TPU:40, one launch (start us, length us, event | category | flops | bytes accessed | tf_op | source)
XLA Modules:
  0.0 74.2 jit_solution(14809596807483654202)
XLA Ops:
  0.7 0.5 collective-permute-start
  1.3 2.4 %collective-permute-done.1.dense2_hbm = bf16[128,128]{1,0:T(8,128)(2,1)S(1)} collective-permute-done((bf16[128,128]{1,0:T(8,128)(2,1)}, bf16[128,128]{1,0:T(8,128)(2,1)S(1)}, u32[]{:S(2)}, u32[]{:S(2)}) %collective-permute-start.1) | collective-permute-done | bytes 32800 | tf_op jit(solution)/shard_map/ppermute | solution.py:364
  3.7 0.6 copy-done.6
  4.3 0.2 copy-done.5
  4.7 6.6 %shard_map.111 = (bf16[288,384]{1,0:T(8,128)(2,1)}, bf16[288,384]{1,0:T(8,128)(2,1)}, bf16[288,384]{1,0:T(8,128)(2,1)}, bf16[288,384]{1,0:T(8,128)(2,1)}, bf16[5...) custom-call(s32[1]{0:T(128)} %bitcast.place_ref._, bf16[128,2048]{1,0:T(8,128)(2,1)} %pooled_hbm.1, ...), custom_call_target="tpu_custom_call" | custom-call | flops 8000000000 | bytes 8000000 | tf_op jit(solution)/shard_map/pallas_call | solution.py:338
  11.3 0.2 collective-permute-start.6
  11.5 1.6 %collective-permute-start.3 = (bf16[288,384]{1,0:T(8,128)(2,1)}, bf16[288,384]{1,0:T(8,128)(2,1)S(1)}, u32[]{:S(2)}, u32[]{:S(2)}) collective-permute-start(bf16[288,384]{1,0:T(8,128)(2,1)} %get-tuple-element.31), channel_id=1, source_target_pairs={{0,2},{2,4},{4,6},{6,0},{1,3},{3,5},{5,7},{7,1},{8,10},{10,12},{12... | collective-permute-start | bytes 663560 | tf_op jit(solution)/shard_map/ppermute | solution.py:356
  13.1 2.7 %collective-permute-start.4 = (bf16[288,384]{1,0:T(8,128)(2,1)}, bf16[288,384]{1,0:T(8,128)(2,1)S(1)}, u32[]{:S(2)}, u32[]{:S(2)}) collective-permute-start(bf16[288,384]{1,0:T(8,128)(2,1)} %get-tuple-element.32), channel_id=1, source_target_pairs={{0,4},{2,6},{4,0},{6,2},{1,5},{3,7},{5,1},{7,3},{8,12},{10,14},{12... | collective-permute-start | bytes 663560 | tf_op jit(solution)/shard_map/ppermute | solution.py:356
  15.8 0.7 collective-permute-start.5
  16.4 6.1 %all-to-all-start = ((bf16[16,128,128]{2,1,0:T(8,128)(2,1)}), bf16[16,128,128]{2,1,0:T(8,128)(2,1)S(1)}, u32[]{:S(2)}, u32[]{:S(2)}) async-start(bf16[16,128,128]{2,1,0:T(8,128)(2,1)} %get-tuple-element.43), calls=%async_computation | async-start | bytes 1048576 | tf_op jit(solution)/shard_map/all_to_all | solution.py:384
  22.6 0.8 %collective-permute-done.6.got = bf16[544,384]{1,0:T(8,128)(2,1)S(1)} collective-permute-done((bf16[544,384]{1,0:T(8,128)(2,1)}, bf16[544,384]{1,0:T(8,128)(2,1)S(1)}, u32[]{:S(2)}, u32[]{:S(2)}) %collective-permute-start.6) | collective-permute-done | bytes 417824 | tf_op jit(solution)/shard_map/ppermute | solution.py:386
  23.3 1.0 %copy-done.2 = bf16[544,384]{1,0:T(8,128)(2,1)S(1)} copy-done((bf16[544,384]{1,0:T(8,128)(2,1)S(1)}, bf16[544,384]{1,0:T(8,128)(2,1)}, u32[]{:S(2)}) %copy-start.2) | copy-done | bytes 417816
  24.3 0.7 shard_map.112
  25.0 1.6 %collective-permute-start.8 = (bf16[144,384]{1,0:T(8,128)(2,1)S(1)}, bf16[144,384]{1,0:T(8,128)(2,1)S(1)}, u32[]{:S(2)}, u32[]{:S(2)}) collective-permute-start(bf16[144,384]{1,0:T(8,128)(2,1)S(1)} %get-tuple-element.39), channel_id=1, source_target_pairs={{0,2},{2,4},{4,6},{6,0},{1,3},{3,5},{5,7},{7,1},{8,10},{10,12},{12... | collective-permute-start | bytes 331784 | tf_op jit(solution)/shard_map/ppermute | solution.py:356
  26.7 1.0 %collective-permute-start.9 = (bf16[144,384]{1,0:T(8,128)(2,1)S(1)}, bf16[144,384]{1,0:T(8,128)(2,1)S(1)}, u32[]{:S(2)}, u32[]{:S(2)}) collective-permute-start(bf16[144,384]{1,0:T(8,128)(2,1)S(1)} %get-tuple-element.40), channel_id=1, source_target_pairs={{0,4},{2,6},{4,0},{6,2},{1,5},{3,7},{5,1},{7,3},{8,12},{10,14},{12... | collective-permute-start | bytes 331784 | tf_op jit(solution)/shard_map/ppermute | solution.py:356
  27.7 2.3 %collective-permute-start.10 = (bf16[144,384]{1,0:T(8,128)(2,1)S(1)}, bf16[144,384]{1,0:T(8,128)(2,1)S(1)}, u32[]{:S(2)}, u32[]{:S(2)}) collective-permute-start(bf16[144,384]{1,0:T(8,128)(2,1)S(1)} %get-tuple-element.41), channel_id=1, source_target_pairs={{0,6},{2,0},{4,2},{6,4},{1,7},{3,1},{5,3},{7,5},{8,14},{10,8},{12,... | collective-permute-start | bytes 331784 | tf_op jit(solution)/shard_map/ppermute | solution.py:356
  30.1 0.4 shard_map.113
  30.5 2.3 %collective-permute-start.7 = (bf16[160,384]{1,0:T(8,128)(2,1)S(1)}, bf16[160,384]{1,0:T(8,128)(2,1)S(1)}, u32[]{:S(2)}, u32[]{:S(2)}) collective-permute-start(bf16[160,384]{1,0:T(8,128)(2,1)S(1)} %get-tuple-element.38), channel_id=1, source_target_pairs={{0,8},{8,0},{1,9},{9,1},{2,10},{10,2},{3,11},{11,3},{4,12},{12,4},... | collective-permute-start | bytes 368648 | tf_op jit(solution)/shard_map/ppermute | solution.py:416
  32.8 0.7 shard_map.114
  33.5 3.8 %shard_map.115._ = bf16[2688,128]{1,0:T(8,128)(2,1)} custom-call(f32[8,2048]{1,0:T(8,128)S(1)} %get-tuple-element.42.found_ref, bf16[2048,128]{1,0:T(8,128)(2,1)S(1)} %bitcast.13, bf16[16,16,128]{2,1,0:T(8,128)(2,1)S(1)} %get-tuple-element.44.pos_ref, f32[160,384]{1,0:T(8,128)S(1)} %get-tuple-element.37._.u_keep), custom_call_target="tpu_custom_call" | custom-call | flops 7000000000 | bytes 7000000 | tf_op jit(solution)/shard_map/pallas_call | solution.py:338
  37.3 0.5 shard_map.116
  37.8 3.4 %collective-permute-start.11 = (bf16[208,384]{1,0:T(8,128)(2,1)S(1)}, bf16[208,384]{1,0:T(8,128)(2,1)S(1)}, u32[]{:S(2)}, u32[]{:S(2)}) collective-permute-start(bf16[208,384]{1,0:T(8,128)(2,1)S(1)} %get-tuple-element.46), channel_id=1, source_target_pairs={{0,64},{64,0},{128,192},{192,128},{1,65},{65,1},{129,193},{193,129... | collective-permute-start | bytes 479240 | tf_op jit(solution)/shard_map/ppermute | solution.py:428
  41.2 8.3 %all-to-all-start.1 = ((bf16[16,168,128]{2,1,0:T(8,128)(2,1)}), bf16[16,168,128]{2,1,0:T(8,128)(2,1)S(1)}, u32[]{:S(2)}, u32[]{:S(2)}) async-start(bf16[16,168,128]{2,1,0:T(8,128)(2,1)} %bitcast.8), calls=%async_computation.1 | async-start | bytes 1376256 | tf_op jit(solution)/shard_map/all_to_all | solution.py:431
  49.7 2.0 %collective-permute-start.12 = (bf16[112,384]{1,0:T(8,128)(2,1)S(1)}, bf16[112,384]{1,0:T(8,128)(2,1)S(1)}, u32[]{:S(2)}, u32[]{:S(2)}) collective-permute-start(bf16[112,384]{1,0:T(8,128)(2,1)S(1)} %get-tuple-element.48), channel_id=1, source_target_pairs={{0,16},{16,0},{32,48},{48,32},{1,17},{17,1},{33,49},{49,33},{2,18}... | collective-permute-start | bytes 258056 | tf_op jit(solution)/shard_map/ppermute | solution.py:428
  51.7 4.4 %collective-permute-done.12.got = bf16[112,384]{1,0:T(8,128)(2,1)S(1)} collective-permute-done((bf16[112,384]{1,0:T(8,128)(2,1)S(1)}, bf16[112,384]{1,0:T(8,128)(2,1)S(1)}, u32[]{:S(2)}, u32[]{:S(2)}) %collective-permute-start.12) | collective-permute-done | bytes 86048 | tf_op jit(solution)/shard_map/ppermute | solution.py:428
  56.3 2.5 %collective-permute-start.13 = (bf16[64,384]{1,0:T(8,128)(2,1)S(1)}, bf16[64,384]{1,0:T(8,128)(2,1)S(1)}, u32[]{:S(2)}, u32[]{:S(2)}) collective-permute-start(bf16[64,384]{1,0:T(8,128)(2,1)S(1)} %get-tuple-element.50), channel_id=1, source_target_pairs={{0,48},{48,0},{16,32},{32,16},{1,49},{49,1},{17,33},{33,17},{2,50}... | collective-permute-start | bytes 147464 | tf_op jit(solution)/shard_map/ppermute | solution.py:428
  58.8 3.3 %collective-permute-done.13.got = bf16[64,384]{1,0:T(8,128)(2,1)S(1)} collective-permute-done((bf16[64,384]{1,0:T(8,128)(2,1)S(1)}, bf16[64,384]{1,0:T(8,128)(2,1)S(1)}, u32[]{:S(2)}, u32[]{:S(2)}) %collective-permute-start.13) | collective-permute-done | bytes 49184 | tf_op jit(solution)/shard_map/ppermute | solution.py:428
  62.2 4.3 %collective-permute-start.14 = (bf16[48,384]{1,0:T(8,128)(2,1)S(1)}, bf16[48,384]{1,0:T(8,128)(2,1)S(1)}, u32[]{:S(2)}, u32[]{:S(2)}) collective-permute-start(bf16[48,384]{1,0:T(8,128)(2,1)S(1)} %get-tuple-element.52), channel_id=1, source_target_pairs={{0,192},{192,0},{64,128},{128,64},{1,193},{193,1},{65,129},{129,65... | collective-permute-start | bytes 110600 | tf_op jit(solution)/shard_map/ppermute | solution.py:428
  66.5 4.4 %collective-permute-done.14.got = bf16[48,384]{1,0:T(8,128)(2,1)S(1)} collective-permute-done((bf16[48,384]{1,0:T(8,128)(2,1)S(1)}, bf16[48,384]{1,0:T(8,128)(2,1)S(1)}, u32[]{:S(2)}, u32[]{:S(2)}) %collective-permute-start.14) | collective-permute-done | bytes 36896 | tf_op jit(solution)/shard_map/ppermute | solution.py:428
  70.8 0.7 shard_map.120
  71.5 1.1 %all-to-all-done.1 = bf16[16,168,128]{2,1,0:T(8,128)(2,1)S(1)} async-done(((bf16[16,168,128]{2,1,0:T(8,128)(2,1)}), bf16[16,168,128]{2,1,0:T(8,128)(2,1)S(1)}, u32[]{:S(2)}, u32[]{:S(2)}) %all-to-all-start.1) | async-done | bytes 688160 | tf_op jit(solution)/shard_map/all_to_all | solution.py:431
  72.6 1.6 %shard_map.121 = f32[512,128]{1,0:T(8,128)} custom-call(bf16[2688,128]{1,0:T(8,128)(2,1)S(1)} %bitcast.12), custom_call_target="tpu_custom_call" | custom-call | flops 2000000000 | bytes 2000000 | tf_op jit(solution)/shard_map/pallas_call | solution.py:338
  (27 shorter events, 0.8 us)
Async XLA Ops:
  0.6 3.1 %collective-permute-start.2 = (bf16[128,2176]{1,0:T(8,128)(2,1)}, bf16[128,2176]{1,0:T(8,128)(2,1)S(1)}, u32[]{:S(2)}, u32[]{:S(2)}) collective-permute-start(bf16[128,2176]{1,0:T(8,128)(2,1)} %cot_hbm.1), channel_id=1, source_target_pairs={{0,1},{1,0},{2,3},{3,2},{4,5},{5,4},{6,7},{7,6},{8,9},{9,8},{10,11... | collective-permute-start | bytes 1671176 | tf_op jit(solution)/shard_map/ppermute | solution.py:364
  0.7 3.0 %collective-permute-start = (bf16[128,2048]{1,0:T(8,128)(2,1)}, bf16[128,2048]{1,0:T(8,128)(2,1)S(1)}, u32[]{:S(2)}, u32[]{:S(2)}) collective-permute-start(bf16[128,2048]{1,0:T(8,128)(2,1)} %pooled_hbm.1), channel_id=1, source_target_pairs={{0,1},{1,0},{2,3},{3,2},{4,5},{5,4},{6,7},{7,6},{8,9},{9,8},{10,11... | collective-permute-start | bytes 1572872 | tf_op jit(solution)/shard_map/ppermute | solution.py:364
  1.2 2.5 %collective-permute-start.1 = (bf16[128,128]{1,0:T(8,128)(2,1)}, bf16[128,128]{1,0:T(8,128)(2,1)S(1)}, u32[]{:S(2)}, u32[]{:S(2)}) collective-permute-start(bf16[128,128]{1,0:T(8,128)(2,1)} %dense_hbm.1), channel_id=1, source_target_pairs={{0,1},{1,0},{2,3},{3,2},{4,5},{5,4},{6,7},{7,6},{8,9},{9,8},{10,11... | collective-permute-start | bytes 98312 | tf_op jit(solution)/shard_map/ppermute | solution.py:364
  3.7 0.6 copy-start.6
  3.7 0.8 %copy-start.5 = (bf16[128,2048]{1,0:T(8,128)(2,1)}, bf16[128,2048]{1,0:T(8,128)(2,1)S(1)}, u32[]{:S(2)}) copy-start(bf16[128,2048]{1,0:T(8,128)(2,1)S(1)} %collective-permute-done.pooled2_hbm) | copy-start | bytes 1572868
  3.7 1.0 %copy-start.4 = (bf16[128,2176]{1,0:T(8,128)(2,1)}, bf16[128,2176]{1,0:T(8,128)(2,1)S(1)}, u32[]{:S(2)}) copy-start(bf16[128,2176]{1,0:T(8,128)(2,1)S(1)} %collective-permute-done.2.cot2_hbm) | copy-start | bytes 1671172
  11.3 12.0 %collective-permute-start.6 = (bf16[544,384]{1,0:T(8,128)(2,1)}, bf16[544,384]{1,0:T(8,128)(2,1)S(1)}, u32[]{:S(2)}, u32[]{:S(2)}) collective-permute-start(bf16[544,384]{1,0:T(8,128)(2,1)} %get-tuple-element.35), channel_id=1, source_target_pairs={{0,8},{8,0},{1,9},{9,1},{2,10},{10,2},{3,11},{11,3},{4,12},{12,4},... | collective-permute-start | bytes 1253384 | tf_op jit(solution)/shard_map/ppermute | solution.py:386
  11.5 16.2 %collective-permute-start.3 = (bf16[288,384]{1,0:T(8,128)(2,1)}, bf16[288,384]{1,0:T(8,128)(2,1)S(1)}, u32[]{:S(2)}, u32[]{:S(2)}) collective-permute-start(bf16[288,384]{1,0:T(8,128)(2,1)} %get-tuple-element.31), channel_id=1, source_target_pairs={{0,2},{2,4},{4,6},{6,0},{1,3},{3,5},{5,7},{7,1},{8,10},{10,12},{12... | collective-permute-start | bytes 663560 | tf_op jit(solution)/shard_map/ppermute | solution.py:356
  13.1 16.9 %collective-permute-start.4 = (bf16[288,384]{1,0:T(8,128)(2,1)}, bf16[288,384]{1,0:T(8,128)(2,1)S(1)}, u32[]{:S(2)}, u32[]{:S(2)}) collective-permute-start(bf16[288,384]{1,0:T(8,128)(2,1)} %get-tuple-element.32), channel_id=1, source_target_pairs={{0,4},{2,6},{4,0},{6,2},{1,5},{3,7},{5,1},{7,3},{8,12},{10,14},{12... | collective-permute-start | bytes 663560 | tf_op jit(solution)/shard_map/ppermute | solution.py:356
  15.8 14.3 %collective-permute-start.5 = (bf16[288,384]{1,0:T(8,128)(2,1)}, bf16[288,384]{1,0:T(8,128)(2,1)S(1)}, u32[]{:S(2)}, u32[]{:S(2)}) collective-permute-start(bf16[288,384]{1,0:T(8,128)(2,1)} %get-tuple-element.33), channel_id=1, source_target_pairs={{0,6},{2,0},{4,2},{6,4},{1,7},{3,1},{5,3},{7,5},{8,14},{10,8},{12,... | collective-permute-start | bytes 663560 | tf_op jit(solution)/shard_map/ppermute | solution.py:356
  16.4 17.0 %all-to-all-start = ((bf16[16,128,128]{2,1,0:T(8,128)(2,1)}), bf16[16,128,128]{2,1,0:T(8,128)(2,1)S(1)}, u32[]{:S(2)}, u32[]{:S(2)}) async-start(bf16[16,128,128]{2,1,0:T(8,128)(2,1)} %get-tuple-element.43), calls=%async_computation | async-start | bytes 1048576 | tf_op jit(solution)/shard_map/all_to_all | solution.py:384
  23.3 1.0 %copy-start.2 = (bf16[544,384]{1,0:T(8,128)(2,1)S(1)}, bf16[544,384]{1,0:T(8,128)(2,1)}, u32[]{:S(2)}) copy-start(bf16[544,384]{1,0:T(8,128)(2,1)} %get-tuple-element.34.own) | copy-start | bytes 1253380
  24.3 5.7 %copy-start.3 = (bf16[288,384]{1,0:T(8,128)(2,1)S(1)}, bf16[288,384]{1,0:T(8,128)(2,1)}, u32[]{:S(2)}) copy-start(bf16[288,384]{1,0:T(8,128)(2,1)} %get-tuple-element.30.m0) | copy-start | bytes 663556
  25.0 12.2 %collective-permute-start.8 = (bf16[144,384]{1,0:T(8,128)(2,1)S(1)}, bf16[144,384]{1,0:T(8,128)(2,1)S(1)}, u32[]{:S(2)}, u32[]{:S(2)}) collective-permute-start(bf16[144,384]{1,0:T(8,128)(2,1)S(1)} %get-tuple-element.39), channel_id=1, source_target_pairs={{0,2},{2,4},{4,6},{6,0},{1,3},{3,5},{5,7},{7,1},{8,10},{10,12},{12... | collective-permute-start | bytes 331784 | tf_op jit(solution)/shard_map/ppermute | solution.py:356
  26.7 10.6 %collective-permute-start.9 = (bf16[144,384]{1,0:T(8,128)(2,1)S(1)}, bf16[144,384]{1,0:T(8,128)(2,1)S(1)}, u32[]{:S(2)}, u32[]{:S(2)}) collective-permute-start(bf16[144,384]{1,0:T(8,128)(2,1)S(1)} %get-tuple-element.40), channel_id=1, source_target_pairs={{0,4},{2,6},{4,0},{6,2},{1,5},{3,7},{5,1},{7,3},{8,12},{10,14},{12... | collective-permute-start | bytes 331784 | tf_op jit(solution)/shard_map/ppermute | solution.py:356
  27.7 9.6 %collective-permute-start.10 = (bf16[144,384]{1,0:T(8,128)(2,1)S(1)}, bf16[144,384]{1,0:T(8,128)(2,1)S(1)}, u32[]{:S(2)}, u32[]{:S(2)}) collective-permute-start(bf16[144,384]{1,0:T(8,128)(2,1)S(1)} %get-tuple-element.41), channel_id=1, source_target_pairs={{0,6},{2,0},{4,2},{6,4},{1,7},{3,1},{5,3},{7,5},{8,14},{10,8},{12,... | collective-permute-start | bytes 331784 | tf_op jit(solution)/shard_map/ppermute | solution.py:356
  30.1 2.7 %copy-start = (s32[2048,1,2]{0,2,1:T(2,128)S(1)}, s32[2048,1,2]{0,2,1:T(2,128)}, u32[]{:S(2)}) copy-start(s32[2048,1,2]{0,2,1:T(2,128)} %param.14) | copy-start | bytes 49156
  30.1 2.7 %copy-start.1 = (s32[1,1,2048]{2,1,0:T(1,128)S(1)}, s32[1,1,2048]{2,1,0:T(1,128)}, u32[]{:S(2)}) copy-start(s32[1,1,2048]{2,1,0:T(1,128)} %param.15) | copy-start | bytes 24580
  30.5 6.8 %collective-permute-start.7 = (bf16[160,384]{1,0:T(8,128)(2,1)S(1)}, bf16[160,384]{1,0:T(8,128)(2,1)S(1)}, u32[]{:S(2)}, u32[]{:S(2)}) collective-permute-start(bf16[160,384]{1,0:T(8,128)(2,1)S(1)} %get-tuple-element.38), channel_id=1, source_target_pairs={{0,8},{8,0},{1,9},{9,1},{2,10},{10,2},{3,11},{11,3},{4,12},{12,4},... | collective-permute-start | bytes 368648 | tf_op jit(solution)/shard_map/ppermute | solution.py:416
  37.8 11.7 %collective-permute-start.11 = (bf16[208,384]{1,0:T(8,128)(2,1)S(1)}, bf16[208,384]{1,0:T(8,128)(2,1)S(1)}, u32[]{:S(2)}, u32[]{:S(2)}) collective-permute-start(bf16[208,384]{1,0:T(8,128)(2,1)S(1)} %get-tuple-element.46), channel_id=1, source_target_pairs={{0,64},{64,0},{128,192},{192,128},{1,65},{65,1},{129,193},{193,129... | collective-permute-start | bytes 479240 | tf_op jit(solution)/shard_map/ppermute | solution.py:428
  41.2 31.4 %all-to-all-start.1 = ((bf16[16,168,128]{2,1,0:T(8,128)(2,1)}), bf16[16,168,128]{2,1,0:T(8,128)(2,1)S(1)}, u32[]{:S(2)}, u32[]{:S(2)}) async-start(bf16[16,168,128]{2,1,0:T(8,128)(2,1)} %bitcast.8), calls=%async_computation.1 | async-start | bytes 1376256 | tf_op jit(solution)/shard_map/all_to_all | solution.py:431
  49.7 6.4 %collective-permute-start.12 = (bf16[112,384]{1,0:T(8,128)(2,1)S(1)}, bf16[112,384]{1,0:T(8,128)(2,1)S(1)}, u32[]{:S(2)}, u32[]{:S(2)}) collective-permute-start(bf16[112,384]{1,0:T(8,128)(2,1)S(1)} %get-tuple-element.48), channel_id=1, source_target_pairs={{0,16},{16,0},{32,48},{48,32},{1,17},{17,1},{33,49},{49,33},{2,18}... | collective-permute-start | bytes 258056 | tf_op jit(solution)/shard_map/ppermute | solution.py:428
  56.3 5.8 %collective-permute-start.13 = (bf16[64,384]{1,0:T(8,128)(2,1)S(1)}, bf16[64,384]{1,0:T(8,128)(2,1)S(1)}, u32[]{:S(2)}, u32[]{:S(2)}) collective-permute-start(bf16[64,384]{1,0:T(8,128)(2,1)S(1)} %get-tuple-element.50), channel_id=1, source_target_pairs={{0,48},{48,0},{16,32},{32,16},{1,49},{49,1},{17,33},{33,17},{2,50}... | collective-permute-start | bytes 147464 | tf_op jit(solution)/shard_map/ppermute | solution.py:428
  62.2 8.7 %collective-permute-start.14 = (bf16[48,384]{1,0:T(8,128)(2,1)S(1)}, bf16[48,384]{1,0:T(8,128)(2,1)S(1)}, u32[]{:S(2)}, u32[]{:S(2)}) collective-permute-start(bf16[48,384]{1,0:T(8,128)(2,1)S(1)} %get-tuple-element.52), channel_id=1, source_target_pairs={{0,192},{192,0},{64,128},{128,64},{1,193},{193,1},{65,129},{129,65... | collective-permute-start | bytes 110600 | tf_op jit(solution)/shard_map/ppermute | solution.py:428
